TPU v7x, 256 devices: a whole 4x4x8 slice. The times are simulated.
256 devices in a mesh: dp: 2 (over core), row: 8 (over z), col: 16 (over y, x).
Axes of the slice: x: 4, y: 4, z: 8, core: 2. Of those that a mesh axis runs over, the one named last changes fastest.
Arguments:
- tokens: bfloat16 [1024, 8192], P(('dp', 'row'), 'col'), may hold values from -6 to 6
- cotangent: bfloat16 [1024, 8192], P(('dp', 'row'), 'col'), may hold values from -1.5 to 1.5
- gate_weight: bfloat16 [8192, 14336], P('col', 'row'), may hold values from -0.0625 to 0.0625
- up_weight: bfloat16 [8192, 14336], P('col', 'row'), may hold values from -0.0625 to 0.0625
- down_weight: bfloat16 [14336, 8192], P('row', 'col'), may hold values from -0.046875 to 0.046875
Outputs:
- input_grad: bfloat16 [1024, 8192], P(('dp', 'row'), 'col')
- gate_wgrad: bfloat16 [8192, 14336], P('col', 'row')
- up_wgrad: bfloat16 [8192, 14336], P('col', 'row')
- down_wgrad: bfloat16 [14336, 8192], P('row', 'col')
All inputs are finite; a program needn't handle non-finite values.
Results may differ from a plain program's by a relative error of at most 0.033.
Values may be sent and summed in bfloat16 or wider, within the bound.
No kernel may reach another device: no remote copies, remote signals or barrier semaphores. Data moves between devices by JAX's collectives and lax.ppermute only.
A program may use at most 128 MiB of HBM per device.

v0:
```python
import jax
import jax.numpy as jnp
from jax import lax
from jax.sharding import PartitionSpec as P


def for_sending(x):

    def short(part):
        return part.astype(jnp.bfloat16) if part.dtype == jnp.float32 else part

    return jax.tree.map(short, x)


def rounded(values):
    return lax.optimization_barrier(values.astype(jnp.bfloat16)).astype(jnp.float32)


def weight_terms(in_rows, up_rows, packed, hidden_cols):
    contract = (((0,), (0,)), ((), ()))
    gate_term = lax.dot_general(
        in_rows,
        packed[:, hidden_cols : 2 * hidden_cols],
        contract,
        preferred_element_type=jnp.float32,
    )
    up_term = lax.dot_general(
        in_rows, packed[:, 2 * hidden_cols :], contract, preferred_element_type=jnp.float32
    )
    down_term = lax.dot_general(
        packed[:, :hidden_cols], up_rows, contract, preferred_element_type=jnp.float32
    )
    return (rounded(gate_term), rounded(up_term), rounded(down_term))


def body(tokens, cotangent, gate_weight, up_weight, down_weight):
    hidden_cols = gate_weight.shape[1]
    inputs, upstream = (
        lax.all_gather(tokens, "row", axis=0, tiled=True),
        lax.all_gather(cotangent, "row", axis=0, tiled=True),
    )
    contract_last = (((1,), (1,)), ((), ()))
    gate_part = jnp.dot(inputs, gate_weight, preferred_element_type=jnp.float32)
    up_part = jnp.dot(inputs, up_weight, preferred_element_type=jnp.float32)
    back_part = lax.dot_general(
        upstream, down_weight, contract_last, preferred_element_type=jnp.float32
    )
    summed = lax.psum_scatter(
        jnp.concatenate([gate_part, up_part, back_part], axis=1).astype(jnp.bfloat16),
        "col",
        scatter_dimension=0,
        tiled=True,
    ).astype(jnp.float32)
    gate_sum = summed[:, :hidden_cols]
    up_sum = summed[:, hidden_cols : 2 * hidden_cols]
    back_sum = summed[:, 2 * hidden_cols :]
    sigmoid_gate = jax.nn.sigmoid(gate_sum)
    hidden = (gate_sum * sigmoid_gate * up_sum).astype(jnp.bfloat16)
    gate_grad = (back_sum * up_sum * sigmoid_gate * (1.0 + gate_sum * (1.0 - sigmoid_gate))).astype(
        jnp.bfloat16
    )
    up_grad = (back_sum * gate_sum * sigmoid_gate).astype(jnp.bfloat16)
    packed = jnp.concatenate([hidden, gate_grad, up_grad], axis=1)
    allrows = lax.all_gather(packed, "col", axis=0, tiled=True)
    total = lax.dot_general(
        allrows[:, hidden_cols : 2 * hidden_cols],
        gate_weight,
        contract_last,
        preferred_element_type=jnp.float32,
    )
    input_grad = lax.psum_scatter(
        (
            total
            + lax.dot_general(
                allrows[:, 2 * hidden_cols :],
                up_weight,
                contract_last,
                preferred_element_type=jnp.float32,
            )
        ).astype(jnp.bfloat16),
        "row",
        scatter_dimension=0,
        tiled=True,
    )
    totals = jax.tree.map(
        lambda part: part.astype(jnp.float32),
        lax.psum(for_sending(weight_terms(inputs, upstream, allrows, hidden_cols)), "dp"),
    )
    return (
        input_grad,
        totals[0].astype(jnp.bfloat16),
        totals[1].astype(jnp.bfloat16),
        totals[2].astype(jnp.bfloat16),
    )


def solution(mesh):
    placed = (
        P(("dp", "row"), "col"),
        P(("dp", "row"), "col"),
        P("col", "row"),
        P("col", "row"),
        P("row", "col"),
    )
    return jax.shard_map(
        body,
        mesh=mesh,
        in_specs=placed,
        out_specs=(P(("dp", "row"), "col"), P("col", "row"), P("col", "row"), P("row", "col")),
        check_vma=False,
    )
```

profile of v0, /device:TPU:2, one launch (start us, length us, event | category | flops | bytes accessed | tf_op | source)
XLA Modules:
  0.0 320.6 jit_solution(13616498360148616602)
XLA Ops:
  7.2 0.0 copy-start
  7.2 0.0 reduce-scatter.3.cloned.1.call-start
  7.2 29.5 %all_gather.9 = bf16[512,512]{1,0:T(8,128)(2,1)S(1)} all-gather(bf16[64,512]{1,0:T(8,128)(2,1)} %param.5), channel_id=1, replica_groups=mesh['dp'=2,'row'=8,'col'=16] {'row'}, dimensions={0}, use_global_device_ids=true | all-gather | bytes 589824 | tf_op jit(solution)/shard_map/all_gather | solution.py:39
  36.7 25.9 %all_gather.10 = bf16[512,512]{1,0:T(8,128)(2,1)S(1)} all-gather(bf16[64,512]{1,0:T(8,128)(2,1)} %param.6), channel_id=1, replica_groups=mesh['dp'=2,'row'=8,'col'=16] {'row'}, dimensions={0}, use_global_device_ids=true | all-gather | bytes 589824 | tf_op jit(solution)/shard_map/all_gather | solution.py:40
  62.6 0.0 copy-done
  62.6 0.0 copy-start.3
  62.6 1.1 convolution_convert_fusion.4
  63.7 0.4 copy-done.3
  64.1 0.0 copy-start.2
  64.1 1.1 convolution_convert_fusion.5
  65.2 0.4 copy-done.2
  65.6 1.2 convolution_convert_fusion.3
  66.7 3.6 %pad_maximum_fusion = bf16[512,5376]{1,0:T(8,128)(2,1)} fusion(bf16[512,1792]{1,0:T(8,128)(2,1)S(1)} %convolution_convert_fusion.3, bf16[512,1792]{1,0:T(8,128)(2,1)S(1)} %convolution_convert_fusion.4, bf16[512,1792]{1,0:T(8,128)(2,1)S(1)} %convolution_convert_fusion.5), kind=kLoop, calls=%fused_computation | loop fusion | flops 16515072 | bytes 11010048 | tf_op jit(solution)/shard_map/concatenate | solution.py:49
  70.3 0.0 reduce-scatter.3.cloned.1.call-update
  70.3 0.0 all-gather.2.cloned.1.call-start
  70.4 83.5 %reduce-scatter.3.cloned.1.call-done = bf16[32,5376]{1,0:T(8,128)(2,1)} async-done(((bf16[512,5376]{1,0:T(8,128)(2,1)}), bf16[32,5376]{1,0:T(8,128)(2,1)}) %reduce-scatter.3.cloned.1.call-update) | async-done | bytes 344080 | tf_op jit(solution)/shard_map/reduce_scatter | solution.py:48
  153.9 1.0 convert_element_type.43
  154.9 0.1 multiply_convert_fusion.2
  155.0 0.8 pad_maximum_fusion.1
  155.8 0.0 all-gather.2.cloned.1.call-update
  155.8 0.0 all-reduce.3.cloned.1.call-start
  155.9 63.4 %all-gather.2.cloned.1.call-done = bf16[512,5376]{1,0:T(8,128)(2,1)} async-done(((bf16[32,5376]{1,0:T(8,128)(2,1)}), bf16[512,5376]{1,0:T(8,128)(2,1)}) %all-gather.2.cloned.1.call-update) | async-done | bytes 5505040 | tf_op jit(solution)/shard_map/all_gather | solution.py:64
  219.2 0.0 copy-start.1
  219.2 4.0 %convolution_convert_fusion = bf16[1792,512]{1,0:T(8,128)(2,1)} fusion(bf16[512,512]{1,0:T(8,128)(2,1)S(1)} %all_gather.10, bf16[512,5376]{1,0:T(8,128)(2,1)} %all-gather.2.cloned.1.call-done), kind=kOutput, calls=%fused_computation.1 | convolution fusion | flops 940441600 | bytes 4194304 | tf_op jit(solution)/shard_map/dot_general | solution.py:30
  223.3 0.0 copy-done.1
  223.3 2.4 fusion.1
  225.7 2.4 fusion
  228.0 0.0 all-reduce.3.cloned.1.call-update
  228.1 0.0 reduce-scatter.5.cloned.1.call-start
  228.1 0.0 copy-start.4
  228.1 2.8 fusion.4
  230.9 0.0 copy-done.4
  230.9 3.4 %fusion.12 = bf16[512,512]{1,0:T(8,128)(2,1)} fusion(f32[512,512]{1,0:T(8,128)S(1)} %fusion.4, bf16[512,1792]{1,0:T(8,128)(2,1)S(1)} %copy-done.4, bf16[512,5376]{1,0:T(8,128)(2,1)} %all-gather.2.cloned.1.call-done), kind=kOutput, calls=%fused_computation.17 | convolution fusion | flops 940048384 | bytes 5242880 | tf_op jit(solution)/shard_map/dot_general | solution.py:65
  234.3 0.0 reduce-scatter.5.cloned.1.call-update
  234.4 35.2 %all-reduce.3.cloned.1.call-done = (bf16[512,1792]{0,1:T(8,128)(2,1)}, bf16[512,1792]{0,1:T(8,128)(2,1)}, bf16[1792,512]{1,0:T(8,128)(2,1)}) async-done(((bf16[512,1792]{0,1:T(8,128)(2,1)}, bf16[512,1792]{0,1:T(8,128)(2,1)}, bf16[1792,512]{1,0:T(8,128)(2,1)}), (bf16[512,1792]{0,1:T(8,128)(2,1)}, bf16[512,1792]{0,1:T(8,128)(2,1)}, bf16[1792,512]{1,0:T(8,128)(2,1)})) %all-reduce.3.cloned.1.call-update) | async-done | bytes 5505040 | tf_op jit(solution)/shard_map/psum | solution.py:87
  269.5 3.8 %copy.9 = bf16[512,1792]{1,0:T(8,128)(2,1)} copy(bf16[512,1792]{0,1:T(8,128)(2,1)} %get-tuple-element.8) | data formatting | bytes 3670016
  273.3 3.8 %copy.10 = bf16[512,1792]{1,0:T(8,128)(2,1)} copy(bf16[512,1792]{0,1:T(8,128)(2,1)} %get-tuple-element.9) | data formatting | bytes 3670016
  277.1 34.1 %reduce-scatter.5.cloned.1.call-done = bf16[64,512]{1,0:T(8,128)(2,1)} async-done(((bf16[512,512]{1,0:T(8,128)(2,1)}), bf16[64,512]{1,0:T(8,128)(2,1)}) %reduce-scatter.5.cloned.1.call-update) | async-done | bytes 65552 | tf_op jit(solution)/shard_map/reduce_scatter | solution.py:71
  311.2 2.8 copy.14
Async XLA Ops:
  7.2 55.4 %copy-start = (bf16[512,1792]{1,0:T(8,128)(2,1)S(1)}, bf16[512,1792]{1,0:T(8,128)(2,1)}, u32[]{:S(2)}) copy-start(bf16[512,1792]{1,0:T(8,128)(2,1)} %param.8) | copy-start | bytes 5505028
  7.2 146.7 %reduce-scatter.3.cloned.1.call-start = ((), (), s32[]{:S(2)}) async-start(), calls=%async_computation.2 | async-start | bytes 5849088 | tf_op jit(solution)/shard_map/reduce_scatter | solution.py:48
  62.6 1.5 copy-start.3
  64.1 1.5 copy-start.2
  70.3 148.9 %all-gather.2.cloned.1.call-start = ((), (), s32[]{:S(2)}) async-start(), calls=%async_computation.3 | async-start | bytes 5849088 | tf_op jit(solution)/shard_map/all_gather | solution.py:64
  155.8 113.7 %all-reduce.3.cloned.1.call-start = ((), (), s32[]{:S(2)}) async-start(), calls=%async_computation.5 | async-start | bytes 11010048 | tf_op jit(solution)/shard_map/psum | solution.py:87
  219.2 4.0 %copy-start.1 = (bf16[512,5376]{1,0:T(8,128)(2,1)S(1)}, bf16[512,5376]{1,0:T(8,128)(2,1)}, u32[]{:S(2)}) copy-start(bf16[512,5376]{1,0:T(8,128)(2,1)} %all-gather.2.cloned.1.call-done) | copy-start | bytes 16515076
  228.1 83.2 %reduce-scatter.5.cloned.1.call-start = ((), (), s32[]{:S(2)}) async-start(), calls=%async_computation.4 | async-start | bytes 589824 | tf_op jit(solution)/shard_map/reduce_scatter | solution.py:71
  228.1 2.8 copy-start.4
Sparse Core Ops, SparseCore 0:
  70.4 83.3 reduce-scatter.2
  156.9 62.3 all-gather.1
  228.2 41.3 all-reduce.2
  272.6 38.5 reduce-scatter.4
where the time goes:
time: 321 us
  waiting for transfers between devices  216 us (67%)
  blocking collectives  55.3 us (17%)
  matrix products  18.4 us (6%)
  between operations  13.8 us (4%)
  local copies, waits for them, and re-layouts  11.2 us (3%)
  other arithmetic  5.47 us (2%)
    reduce_scatter x1, waiting for transfers between devices, body(): lax.psum_scatter(jnp.concatenate([gate_part, up_part, back_part], axis=1)...  83.5 us
    all_gather x1, waiting for transfers between devices, body(): allrows = lax.all_gather(packed, 'col', axis=0, tiled=True)  63.4 us
    psum x1, waiting for transfers between devices, body(): lax.psum(for_sending(weight_terms(inputs, upstream, allrows, hidden_cols)...  35.2 us
    reduce_scatter x1, waiting for transfers between devices, body(): lax.psum_scatter((total + lax.dot_general(allrows[:, 2 * hidden_cols:], u...  34.1 us
    all_gather x1, blocking collectives, body(): lax.all_gather(tokens, 'row', axis=0, tiled=True)  29.5 us
    all_gather x1, blocking collectives, body(): lax.all_gather(cotangent, 'row', axis=0, tiled=True)  25.9 us
    unnamed x13, local copies, waits for them, and re-layouts  11.2 us
  transfers between devices with their start and end apart: 4, of which 4 were waited for; matrix products, arithmetic and copies ran while one was open for 4% of the time, Pallas kernels for 0%

commit v1 on v0

v1 whole, which is shorter than its diff:
```python
import jax
import jax.numpy as jnp
from jax import lax
from jax.experimental import pallas as pl
from jax.experimental.pallas import tpu as pltpu
from jax.sharding import PartitionSpec as P

RING = 4
BF16 = jnp.bfloat16
F32 = jnp.float32


def send_col(value, axis, step):
    pairs = []
    for dp in range(2):
        for y in range(RING):
            for x in range(RING):
                if axis ^ dp == 0:
                    to = y * RING + (x + step) % RING
                else:
                    to = ((y + step) % RING) * RING + x
                pairs.append((dp * 16 + y * RING + x, dp * 16 + to))
    return lax.ppermute(value, ("dp", "col"), pairs)


def send_row(value, step):
    pairs = []
    for dp in range(2):
        for row in range(8):
            to = (row + step if dp == 0 else row - step) % 8
            pairs.append((dp * 8 + row, dp * 8 + to))
    return lax.ppermute(value, ("dp", "row"), pairs)


def partner(dp, row):
    return (row + 1 if row % 2 == dp else row - 1) % 8


def swap_row(value):
    pairs = [(dp * 8 + row, dp * 8 + partner(dp, row)) for dp in range(2) for row in range(8)]
    return lax.ppermute(value, ("dp", "row"), pairs)


def swap_dp(value):
    return lax.ppermute(value, "dp", [(0, 1), (1, 0)])


def call(kernel, outs, args, scratch=(), flops=0, vmem=24, placed=True):
    whole = pl.BlockSpec(memory_space=pltpu.VMEM)
    small = pl.BlockSpec(memory_space=pltpu.SMEM)
    where = whole if placed else pl.BlockSpec(memory_space=pl.ANY)
    moved = sum(a.size * a.dtype.itemsize for a in args)
    return pl.pallas_call(
        kernel,
        out_shape=[jax.ShapeDtypeStruct(shape, kind) for shape, kind in outs],
        in_specs=[small if a.dtype == jnp.int32 else where for a in args],
        out_specs=[whole] * len(outs),
        scratch_shapes=list(scratch),
        compiler_params=pltpu.CompilerParams(vmem_limit_bytes=vmem * 1024 * 1024),
        cost_estimate=pl.CostEstimate(flops=flops, bytes_accessed=moved, transcendentals=0),
    )(*args)


def rows_of(start, count):
    return pl.ds(pl.multiple_of(start, 32), count)


def pack_kernel(tokens, cotangent, out):
    width = tokens.shape[1]
    out[:, :width] = tokens[...]
    out[:, width:] = cotangent[...]


def bundle_kernel(*refs):
    count = refs[0].shape[0]
    for i in range(4):
        refs[4][count * i : count * i + count] = refs[i][...]


def product_kernel(place, act, gate, up, down, *refs):
    first, outs = refs[:-8], refs[-8:]
    width = gate.shape[0]
    rows = [rows_of(lax.rem(place[0] + step, RING) * 64, 64) for step in (2, 1, 3, 0)]
    both = jnp.concatenate([act[r] for r in rows], axis=0)
    tok, cot = both[:, :width], both[:, width:]
    for k in range(3):
        if k < 2:
            term = jnp.dot(tok, (gate, up)[k][...], preferred_element_type=F32)
        else:
            term = lax.dot_general(
                cot, down[...], (((1,), (1,)), ((), ())), preferred_element_type=F32
            )
        term = term.astype(BF16)
        for q in range(8):
            out = outs[q]
            out[k, out.shape[1] - 32 :] = term[32 * q : 32 * q + 32]
    if first:
        for q in range(8):
            outs[q][:, :32] = first[q][...]


def add_kernel(*refs):
    count = len(refs) // 3
    for i in range(count):
        total = refs[i][...].astype(F32) + refs[count + i][...].astype(F32)
        refs[2 * count + i][...] = total.astype(BF16)


def own_kernel(place, *refs):
    got, outs, held = refs[:6], refs[6:10], refs[10]
    for part in range(2):
        mine, relay, near = got[3 * part : 3 * part + 3]
        total = mine[...].astype(F32) + relay[...].astype(F32) + near[...].astype(F32)
        total = total.astype(BF16)
        held[part] = total[:, :32]
        held[2 + part] = total[:, 32:]
    for step in range(RING):
        outs[step][...] = held[lax.rem(place[1] + step, RING)]


def unit_kernel(own, one, two, three, out):
    gate_sum, up_sum, back_sum = (
        own[k].astype(F32) + one[k].astype(F32) + two[k].astype(F32) + three[k].astype(F32)
        for k in range(3)
    )
    sig = jax.nn.sigmoid(gate_sum)
    silu = gate_sum * sig
    out[0] = (back_sum * up_sum * sig * (1.0 + gate_sum * (1.0 - sig))).astype(BF16)
    out[1] = (back_sum * silu).astype(BF16)
    out[2] = (silu * up_sum).astype(BF16)


def join_kernel(*refs):
    low, high, hid = refs[4:]
    for j in range(4):
        rows = slice(32 * (j % 2), 32 * (j % 2) + 32)
        (low if j < 2 else high)[:, rows] = refs[j][:2]
        hid[32 * j : 32 * j + 32] = refs[j][2]


def rows_at(place, step, j):
    block = lax.rem(place[0] + step, RING)
    sub = lax.rem(place[1] + RING - j, RING)
    return rows_of(256 * lax.div(sub, 2) + 64 * block + 32 * lax.rem(sub, 2), 32)


def assemble(place, pieces, gg, ug):
    for i, step in enumerate((0, 3, 1, 2)):
        for j in range(4):
            piece, lower = pieces[2 * i + j // 2], 32 * (j % 2)
            rows = rows_at(place, step, j)
            gg[rows] = piece[0, lower : lower + 32, :]
            ug[rows] = piece[1, lower : lower + 32, :]


def input_kernel(place, gate, up, *refs):
    pieces, keep, give, gg, ug = refs[:8], *refs[8:]
    assemble(place, pieces, gg, ug)
    contract = (((1,), (1,)), ((), ()))
    total = lax.dot_general(gg[...], gate[...], contract, preferred_element_type=F32)
    total += lax.dot_general(ug[...], up[...], contract, preferred_element_type=F32)
    total = total.astype(BF16)
    rows = keep.shape[0]
    keep[...] = total[:rows]
    give[...] = total[rows:]


def feature_kernel(place, low, high, *refs):
    pieces, gate_out, up_out, act, gg, ug = refs[:8], *refs[8:]
    assemble(place, pieces, gg, ug)
    width, rows = gate_out.shape[0], low.shape[0]
    act[:rows] = low[:, :width]
    act[rows:] = high[:, :width]
    contract = (((0,), (0,)), ((), ()))
    for grad, out in ((gg, gate_out), (ug, up_out)):
        out[...] = lax.dot_general(
            act[...], grad[...], contract, preferred_element_type=F32
        ).astype(BF16)


def hidden_kernel(place, low, high, *refs):
    pieces, down_out, act, hid = refs[:4], *refs[4:]
    for i, step in enumerate((0, 3, 1, 2)):
        for j in range(4):
            hid[rows_at(place, step, j)] = pieces[i][32 * j : 32 * j + 32]
    width, rows = down_out.shape[1], low.shape[0]
    act[:rows] = low[:, width:]
    act[rows:] = high[:, width:]
    contract = (((0,), (0,)), ((), ()))
    down_out[...] = lax.dot_general(
        hid[...], act[...], contract, preferred_element_type=F32
    ).astype(BF16)


def relay_kernel(keep, got, *outs):
    count = outs[0].shape[0]
    for i in range(4):
        rows = slice(count * i, count * i + count)
        outs[i][...] = (keep[rows].astype(F32) + got[rows].astype(F32)).astype(BF16)


def sum_kernel(*refs):
    total = refs[0][...].astype(F32)
    for ref in refs[1:-1]:
        total = total + ref[...].astype(F32)
    refs[-1][...] = total.astype(BF16)


def body(tokens, cotangent, gate, up, down):
    width, hidden = gate.shape
    count = tokens.shape[0]
    rows = 8 * count
    col, row, dp = lax.axis_index("col"), lax.axis_index("row"), lax.axis_index("dp")
    x, y = lax.rem(col, RING), lax.div(col, RING)
    here, other = jnp.where(dp == 0, x, y), jnp.where(dp == 0, y, x)
    place = jnp.stack([here, other]).astype(jnp.int32)

    mine = call(pack_kernel, [((count, 2 * width), BF16)], (tokens, cotangent))[0]
    evens = [mine] + [send_row(mine, -2 * i) for i in range(1, 4)]
    even = call(bundle_kernel, [((4 * count, 2 * width), BF16)], evens)[0]
    odd = swap_row(even)

    third, half = ((3, 32, hidden), BF16), ((3, 64, hidden), BF16)
    part = ()
    for act, kind in ((even, third), (odd, half)):
        part = call(
            product_kernel,
            [kind] * 8,
            (place, act, gate, up, down) + tuple(part),
            flops=2 * 256 * width * hidden * 3,
        )
    far_up, far_down, pass_up, near_up, near_down, pass_down, low, high = part
    far_up, far_down = send_col(far_up, 0, 1), send_col(far_down, 0, -1)
    near_up, near_down = send_col(near_up, 0, 1), send_col(near_down, 0, -1)
    relay = call(add_kernel, [half] * 2, (pass_up, pass_down, far_up, far_down))
    relay_up, relay_down = send_col(relay[0], 0, 1), send_col(relay[1], 0, -1)
    own = call(
        own_kernel,
        [third] * 4,
        (place, low, relay_up, near_down, high, relay_down, near_up),
        scratch=[pltpu.VMEM((4, 3, 32, hidden), BF16)],
    )
    got = [own[0]] + [send_col(own[step], 1, step) for step in range(1, RING)]
    unit = call(unit_kernel, [third], got)[0]
    got = [unit] + [send_col(unit, 1, step) for step in range(1, RING)]
    low, high, hid = call(
        join_kernel,
        [((2, 64, hidden), BF16)] * 2 + [((128, hidden), BF16)],
        got,
    )
    low_left, high_right = send_col(low, 0, 1), send_col(high, 0, -1)
    low, high, low_left, high_right = lax.optimization_barrier((low, high, low_left, high_right))
    low_far, high_far = send_col(low_left, 0, 1), send_col(high_right, 0, -1)
    high_left, low_right = send_col(high, 0, 1), send_col(low, 0, -1)
    hid, high_left, low_right = lax.optimization_barrier((hid, high_left, low_right))
    pieces = (low, high, low_left, high_left, low_right, high_right, low_far, high_far)
    hids = (hid, send_col(hid, 0, 1), send_col(hid, 0, -1), send_col(hid, 0, 2))

    whole = pltpu.VMEM((rows, hidden), BF16)
    lhs = pltpu.VMEM((rows, width), BF16)
    work = 2 * rows * width * hidden
    keep, give = call(
        input_kernel,
        [((4 * count, width), BF16)] * 2,
        (place, gate, up) + pieces,
        scratch=[whole, whole],
        flops=2 * work,
    )
    keep, give, pieces = lax.optimization_barrier((keep, give, pieces))
    swapped = swap_row(give)
    features = call(
        feature_kernel,
        [((width, hidden), BF16)] * 2,
        (place, even, odd) + pieces,
        scratch=[lhs, whole, whole],
        flops=2 * work,
    )
    swapped, *features = lax.optimization_barrier((swapped, *features))
    block = ((count, width), BF16)
    sums = call(relay_kernel, [block] * 4, (keep, swapped))
    sums, hids = lax.optimization_barrier((sums, hids))
    outs = [
        call(sum_kernel, [(term.shape, BF16)], (term, swap_dp(term)))[0] for term in features
    ]
    down_term = call(
        hidden_kernel,
        [((hidden, width), BF16)],
        (place, even, odd) + hids,
        scratch=[lhs, whole],
        flops=work,
    )[0]
    got = [sums[0]] + [send_row(sums[i], 2 * i) for i in range(1, 3)]
    last, *outs = lax.optimization_barrier((sums[3], *outs))
    got.append(send_row(last, 6))
    input_grad = call(sum_kernel, [block], got)[0]
    outs.append(
        call(sum_kernel, [(down_term.shape, BF16)], (down_term, swap_dp(down_term)))[0]
    )
    return (input_grad,) + tuple(outs)


def solution(mesh):
    placed = (
        P(("dp", "row"), "col"),
        P(("dp", "row"), "col"),
        P("col", "row"),
        P("col", "row"),
        P("row", "col"),
    )
    return jax.shard_map(
        body,
        mesh=mesh,
        in_specs=placed,
        out_specs=(P(("dp", "row"), "col"), P("col", "row"), P("col", "row"), P("row", "col")),
        check_vma=False,
    )
```

time: 321 us -> 146 us (0.45)
  waiting for transfers between devices: 216 us -> 63.8 us
  blocking collectives: 55.3 us -> 0 us
  starting transfers between devices: 0.16 us -> 53.4 us
  Pallas kernels: 0 us -> 20 us
  matrix products: 18.4 us -> 0 us
  between operations: 13.8 us -> 0.77 us
  other arithmetic: 5.47 us -> 0.07 us
  local copies, waits for them, and re-layouts: 11.2 us -> 6.19 us
    reduce_scatter x2 -> x0, waiting for transfers between devices: 118 us -> none  [the longest x1 83.5 us: body(): lax.psum_scatter(jnp.concatenate([gate_part, up_part, back_part], axis=1)...]
    ppermute x0 -> x32, waiting for transfers between devices: none -> 63.8 us  [the longest x21 50 us: send_col(): return lax.ppermute(value, ('dp', 'col'), pairs)]
    all_gather x1 -> x0, waiting for transfers between devices: 63.4 us -> none  [body(): allrows = lax.all_gather(packed, 'col', axis=0, tiled=True)]
    all_gather x2 -> x0, blocking collectives: 55.3 us -> none  [the longest x1 29.5 us: body(): lax.all_gather(tokens, 'row', axis=0, tiled=True)]
    ppermute x0 -> x32, starting transfers between devices: none -> 53.4 us  [the longest x21 28.6 us: send_col(): return lax.ppermute(value, ('dp', 'col'), pairs)]
    psum x1 -> x0, waiting for transfers between devices: 35.2 us -> none  [body(): lax.psum(for_sending(weight_terms(inputs, upstream, allrows, hidden_cols)...]
    pallas_call x0 -> x16, Pallas kernels: none -> 20 us  [call(): pl.pallas_call(kernel, out_shape=[jax.ShapeDtypeStruct(shape, kind) for s...]
    dot_general x8 -> x0, matrix products: 18.4 us -> none  [the longest x1 4.02 us: weight_terms(): lax.dot_general(packed[:, :hidden_cols], up_rows, contract, preferred_ele...]
  transfers between devices with their start and end apart: 4 -> 32, of which waited for: 4 -> 20; matrix products, arithmetic and copies ran while one was open for 4% -> 0% of each run, Pallas kernels for 0% -> 10%
where the time goes in v1:
time: 146 us; the launch traced here: 144 us
  waiting for transfers between devices  63.8 us (44%)
  starting transfers between devices  53.4 us (37%)
  Pallas kernels  20 us (14%)
  local copies, waits for them, and re-layouts  6.19 us (4%)
    ppermute x21, waiting for transfers between devices, send_col(): return lax.ppermute(value, ('dp', 'col'), pairs)  50 us
    ppermute x21, starting transfers between devices, send_col(): return lax.ppermute(value, ('dp', 'col'), pairs)  28.6 us
    pallas_call x16, Pallas kernels, call(): pl.pallas_call(kernel, out_shape=[jax.ShapeDtypeStruct(shape, kind) for s...  20 us
    ppermute x6, starting transfers between devices, send_row(): return lax.ppermute(value, ('dp', 'row'), pairs)  17 us
    ppermute x6, waiting for transfers between devices, send_row(): return lax.ppermute(value, ('dp', 'row'), pairs)  11.9 us
    ppermute x2, starting transfers between devices, swap_row(): return lax.ppermute(value, ('dp', 'row'), pairs)  7.32 us
    unnamed x16, local copies, waits for them, and re-layouts  6.19 us
  transfers between devices with their start and end apart: 32, of which 20 were waited for; matrix products, arithmetic and copies ran while one was open for 0% of the time, Pallas kernels for 10%

profile of v1, /device:TPU:2, one launch (start us, length us, event | category | flops | bytes accessed | tf_op | source)
XLA Modules:
  0.0 144.3 jit_solution(3746660722776516219)
XLA Ops:
  0.6 0.8 copy-done.6
  1.5 0.8 copy-done.7
  2.3 6.4 %collective-permute-start = (bf16[64,1024]{1,0:T(8,128)(2,1)S(1)}, bf16[64,1024]{1,0:T(8,128)(2,1)S(1)}, u32[]{:S(2)}, u32[]{:S(2)}) collective-permute-start(bf16[64,1024]{1,0:T(8,128)(2,1)S(1)} %shard_map.84.refs_0_), channel_id=1, source_target_pairs={{0,96},{16,112},{32,0},{48,16},{64,32},{80,48},{96,64},{112,80},{1... | collective-permute-start | bytes 393224 | tf_op jit(solution)/shard_map/ppermute | solution.py:32
  8.7 1.0 collective-permute-start.1
  9.7 2.8 %collective-permute-start.2 = (bf16[64,1024]{1,0:T(8,128)(2,1)S(1)}, bf16[64,1024]{1,0:T(8,128)(2,1)S(1)}, u32[]{:S(2)}, u32[]{:S(2)}) collective-permute-start(bf16[64,1024]{1,0:T(8,128)(2,1)S(1)} %shard_map.84.refs_0_), channel_id=1, source_target_pairs={{0,32},{16,48},{32,64},{48,80},{64,96},{80,112},{96,0},{112,16},{1... | collective-permute-start | bytes 393224 | tf_op jit(solution)/shard_map/ppermute | solution.py:32
  12.5 6.0 %collective-permute-done.refs_1_ = bf16[64,1024]{1,0:T(8,128)(2,1)S(1)} collective-permute-done((bf16[64,1024]{1,0:T(8,128)(2,1)S(1)}, bf16[64,1024]{1,0:T(8,128)(2,1)S(1)}, u32[]{:S(2)}, u32[]{:S(2)}) %collective-permute-start) | collective-permute-done | bytes 131104 | tf_op jit(solution)/shard_map/ppermute | solution.py:32
  18.5 1.2 collective-permute-done.1.refs_2_
  19.8 3.3 %collective-permute-start.3 = (bf16[256,1024]{1,0:T(8,128)(2,1)S(1)}, bf16[256,1024]{1,0:T(8,128)(2,1)S(1)}, u32[]{:S(2)}, u32[]{:S(2)}) collective-permute-start(bf16[256,1024]{1,0:T(8,128)(2,1)S(1)} %shard_map.85.act.low), channel_id=1, source_target_pairs={{0,16},{16,0},{32,48},{48,32},{64,80},{80,64},{96,112},{112,96},{1... | collective-permute-start | bytes 1572872 | tf_op jit(solution)/shard_map/ppermute | solution.py:41
  23.2 1.5 %copy-done = bf16[512,1792]{1,0:T(8,128)(2,1)S(1)} copy-done((bf16[512,1792]{1,0:T(8,128)(2,1)S(1)}, bf16[512,1792]{1,0:T(8,128)(2,1)}, u32[]{:S(2)}) %copy-start) | copy-done | bytes 1835032
  24.7 1.5 %copy-done.2 = bf16[512,1792]{1,0:T(8,128)(2,1)S(1)} copy-done((bf16[512,1792]{1,0:T(8,128)(2,1)S(1)}, bf16[512,1792]{1,0:T(8,128)(2,1)}, u32[]{:S(2)}) %copy-start.2) | copy-done | bytes 1835032
  26.2 1.5 %copy-done.4 = bf16[1792,512]{1,0:T(8,128)(2,1)S(1)} copy-done((bf16[1792,512]{1,0:T(8,128)(2,1)S(1)}, bf16[1792,512]{1,0:T(8,128)(2,1)}, u32[]{:S(2)}) %copy-start.4) | copy-done | bytes 1835032
  27.7 2.1 %shard_map.86 = (bf16[3,32,1792]{2,1,0:T(8,128)(2,1)S(1)}, bf16[3,32,1792]{2,1,0:T(8,128)(2,1)S(1)}, bf16[3,32,1792]{2,1,0:T(8,128)(2,1)S(1)}, bf16[3,32,1792]{2...) custom-call(s32[2]{0:T(128)S(1)} %pad_add_fusion.place, ...), custom_call_target="tpu_custom_call" | custom-call | flops 1409286144 | bytes 6029320 | tf_op jit(solution)/shard_map/pallas_call | solution.py:53
  29.8 0.4 collective-permute-done.3.act.high
  30.3 2.3 %shard_map.87 = (bf16[3,64,1792]{2,1,0:T(8,128)(2,1)S(1)}, bf16[3,64,1792]{2,1,0:T(8,128)(2,1)S(1)}, bf16[3,64,1792]{2,1,0:T(8,128)(2,1)S(1)}, bf16[3,64,1792]{2...) custom-call(s32[2]{0:T(128)S(1)} %pad_add_fusion.place, ...), custom_call_target="tpu_custom_call" | custom-call | flops 1409286144 | bytes 8781832 | tf_op jit(solution)/shard_map/pallas_call | solution.py:53
  32.5 1.6 %collective-permute-start.4 = (bf16[3,64,1792]{2,1,0:T(8,128)(2,1)S(1)}, bf16[3,64,1792]{2,1,0:T(8,128)(2,1)S(1)}, u32[]{:S(2)}, u32[]{:S(2)}) collective-permute-start(bf16[3,64,1792]{2,1,0:T(8,128)(2,1)S(1)} %get-tuple-element.79), channel_id=1, source_target_pairs={{0,1},{1,2},{2,3},{3,0},{4,5},{5,6},{6,7},{7,4},{8,9},{9,10},{10,1... | collective-permute-start | bytes 2064392 | tf_op jit(solution)/shard_map/ppermute | solution.py:23
  34.1 0.5 collective-permute-start.5
  34.6 2.1 %collective-permute-start.7 = (bf16[3,64,1792]{2,1,0:T(8,128)(2,1)S(1)}, bf16[3,64,1792]{2,1,0:T(8,128)(2,1)S(1)}, u32[]{:S(2)}, u32[]{:S(2)}) collective-permute-start(bf16[3,64,1792]{2,1,0:T(8,128)(2,1)S(1)} %get-tuple-element.82), channel_id=1, source_target_pairs={{0,3},{1,0},{2,1},{3,2},{4,7},{5,4},{6,5},{7,6},{8,11},{9,8},{10,9... | collective-permute-start | bytes 2064392 | tf_op jit(solution)/shard_map/ppermute | solution.py:23
  36.7 6.8 %collective-permute-done.4.refs_2_ = bf16[3,64,1792]{2,1,0:T(8,128)(2,1)S(1)} collective-permute-done((bf16[3,64,1792]{2,1,0:T(8,128)(2,1)S(1)}, bf16[3,64,1792]{2,1,0:T(8,128)(2,1)S(1)}, u32[]{:S(2)}, u32[]{:S(2)}) %collective-permute-start.4) | collective-permute-done | bytes 688160 | tf_op jit(solution)/shard_map/ppermute | solution.py:23
  43.6 1.5 %collective-permute-done.5.refs_3_ = bf16[3,64,1792]{2,1,0:T(8,128)(2,1)S(1)} collective-permute-done((bf16[3,64,1792]{2,1,0:T(8,128)(2,1)S(1)}, bf16[3,64,1792]{2,1,0:T(8,128)(2,1)S(1)}, u32[]{:S(2)}, u32[]{:S(2)}) %collective-permute-start.5) | collective-permute-done | bytes 688160 | tf_op jit(solution)/shard_map/ppermute | solution.py:23
  45.0 0.3 shard_map.88
  45.4 1.3 collective-permute-start.6
  46.6 0.8 collective-permute-start.8
  47.5 5.0 %collective-permute-done.7.refs_2_ = bf16[3,64,1792]{2,1,0:T(8,128)(2,1)S(1)} collective-permute-done((bf16[3,64,1792]{2,1,0:T(8,128)(2,1)S(1)}, bf16[3,64,1792]{2,1,0:T(8,128)(2,1)S(1)}, u32[]{:S(2)}, u32[]{:S(2)}) %collective-permute-start.7) | collective-permute-done | bytes 688160 | tf_op jit(solution)/shard_map/ppermute | solution.py:23
  52.4 5.9 %collective-permute-done.6.refs_1_ = bf16[3,64,1792]{2,1,0:T(8,128)(2,1)S(1)} collective-permute-done((bf16[3,64,1792]{2,1,0:T(8,128)(2,1)S(1)}, bf16[3,64,1792]{2,1,0:T(8,128)(2,1)S(1)}, u32[]{:S(2)}, u32[]{:S(2)}) %collective-permute-start.6) | collective-permute-done | bytes 688160 | tf_op jit(solution)/shard_map/ppermute | solution.py:23
  58.3 1.5 %collective-permute-done.8.refs_4_ = bf16[3,64,1792]{2,1,0:T(8,128)(2,1)S(1)} collective-permute-done((bf16[3,64,1792]{2,1,0:T(8,128)(2,1)S(1)}, bf16[3,64,1792]{2,1,0:T(8,128)(2,1)S(1)}, u32[]{:S(2)}, u32[]{:S(2)}) %collective-permute-start.8) | collective-permute-done | bytes 688160 | tf_op jit(solution)/shard_map/ppermute | solution.py:23
  59.8 1.7 %shard_map.89 = (bf16[3,32,1792]{2,1,0:T(8,128)(2,1)S(1)}, bf16[3,32,1792]{2,1,0:T(8,128)(2,1)S(1)}, bf16[3,32,1792]{2,1,0:T(8,128)(2,1)S(1)}, bf16[3,32,1792]{2,1,0:T(8,128)(2,1)S(1)}) custom-call(s32[2]{0:T(128)S(1)} %pad_add_fusion.place, bf16[3,64,1792]{2,1,0:T(8,128)(2,1)S(1)} %get-tuple-element.76.refs_0_, ...), custom_call_target="tpu_custom_call" | custom-call | bytes 4128776 | tf_op jit(solution)/shard_map/pallas_call | solution.py:53
  61.5 1.8 %collective-permute-start.10 = (bf16[3,32,1792]{2,1,0:T(8,128)(2,1)S(1)}, bf16[3,32,1792]{2,1,0:T(8,128)(2,1)S(1)}, u32[]{:S(2)}, u32[]{:S(2)}) collective-permute-start(bf16[3,32,1792]{2,1,0:T(8,128)(2,1)S(1)} %get-tuple-element.87), channel_id=1, source_target_pairs={{0,4},{1,5},{2,6},{3,7},{4,8},{5,9},{6,10},{7,11},{8,12},{9,13},{1... | collective-permute-start | bytes 1032200 | tf_op jit(solution)/shard_map/ppermute | solution.py:23
  63.3 2.9 %collective-permute-start.11 = (bf16[3,32,1792]{2,1,0:T(8,128)(2,1)S(1)}, bf16[3,32,1792]{2,1,0:T(8,128)(2,1)S(1)}, u32[]{:S(2)}, u32[]{:S(2)}) collective-permute-start(bf16[3,32,1792]{2,1,0:T(8,128)(2,1)S(1)} %get-tuple-element.88), channel_id=1, source_target_pairs={{0,8},{1,9},{2,10},{3,11},{4,12},{5,13},{6,14},{7,15},{8,0},{9,1},... | collective-permute-start | bytes 1032200 | tf_op jit(solution)/shard_map/ppermute | solution.py:23
  66.2 1.3 collective-permute-start.12
  67.5 2.6 %collective-permute-done.10.one = bf16[3,32,1792]{2,1,0:T(8,128)(2,1)S(1)} collective-permute-done((bf16[3,32,1792]{2,1,0:T(8,128)(2,1)S(1)}, bf16[3,32,1792]{2,1,0:T(8,128)(2,1)S(1)}, u32[]{:S(2)}, u32[]{:S(2)}) %collective-permute-start.10) | collective-permute-done | bytes 344096 | tf_op jit(solution)/shard_map/ppermute | solution.py:23
  70.2 4.9 %collective-permute-done.11.two = bf16[3,32,1792]{2,1,0:T(8,128)(2,1)S(1)} collective-permute-done((bf16[3,32,1792]{2,1,0:T(8,128)(2,1)S(1)}, bf16[3,32,1792]{2,1,0:T(8,128)(2,1)S(1)}, u32[]{:S(2)}, u32[]{:S(2)}) %collective-permute-start.11) | collective-permute-done | bytes 344096 | tf_op jit(solution)/shard_map/ppermute | solution.py:23
  75.4 1.7 %collective-permute-start.13 = (bf16[3,32,1792]{2,1,0:T(8,128)(2,1)S(1)}, bf16[3,32,1792]{2,1,0:T(8,128)(2,1)S(1)}, u32[]{:S(2)}, u32[]{:S(2)}) collective-permute-start(bf16[3,32,1792]{2,1,0:T(8,128)(2,1)S(1)} %shard_map.90.refs_0_), channel_id=1, source_target_pairs={{0,4},{1,5},{2,6},{3,7},{4,8},{5,9},{6,10},{7,11},{8,12},{9,13},{1... | collective-permute-start | bytes 1032200 | tf_op jit(solution)/shard_map/ppermute | solution.py:23
  77.1 2.1 %collective-permute-start.14 = (bf16[3,32,1792]{2,1,0:T(8,128)(2,1)S(1)}, bf16[3,32,1792]{2,1,0:T(8,128)(2,1)S(1)}, u32[]{:S(2)}, u32[]{:S(2)}) collective-permute-start(bf16[3,32,1792]{2,1,0:T(8,128)(2,1)S(1)} %shard_map.90.refs_0_), channel_id=1, source_target_pairs={{0,8},{1,9},{2,10},{3,11},{4,12},{5,13},{6,14},{7,15},{8,0},{9,1},... | collective-permute-start | bytes 1032200 | tf_op jit(solution)/shard_map/ppermute | solution.py:23
  79.2 1.7 %collective-permute-start.15 = (bf16[3,32,1792]{2,1,0:T(8,128)(2,1)S(1)}, bf16[3,32,1792]{2,1,0:T(8,128)(2,1)S(1)}, u32[]{:S(2)}, u32[]{:S(2)}) collective-permute-start(bf16[3,32,1792]{2,1,0:T(8,128)(2,1)S(1)} %shard_map.90.refs_0_), channel_id=1, source_target_pairs={{0,12},{1,13},{2,14},{3,15},{4,0},{5,1},{6,2},{7,3},{8,4},{9,5},{1... | collective-permute-start | bytes 1032200 | tf_op jit(solution)/shard_map/ppermute | solution.py:23
  80.9 3.0 %collective-permute-done.13.refs_1_ = bf16[3,32,1792]{2,1,0:T(8,128)(2,1)S(1)} collective-permute-done((bf16[3,32,1792]{2,1,0:T(8,128)(2,1)S(1)}, bf16[3,32,1792]{2,1,0:T(8,128)(2,1)S(1)}, u32[]{:S(2)}, u32[]{:S(2)}) %collective-permute-start.13) | collective-permute-done | bytes 344096 | tf_op jit(solution)/shard_map/ppermute | solution.py:23
  83.9 4.2 %collective-permute-done.14.refs_2_ = bf16[3,32,1792]{2,1,0:T(8,128)(2,1)S(1)} collective-permute-done((bf16[3,32,1792]{2,1,0:T(8,128)(2,1)S(1)}, bf16[3,32,1792]{2,1,0:T(8,128)(2,1)S(1)}, u32[]{:S(2)}, u32[]{:S(2)}) %collective-permute-start.14) | collective-permute-done | bytes 344096 | tf_op jit(solution)/shard_map/ppermute | solution.py:23
  88.1 0.4 collective-permute-done.15.refs_3_
  88.6 1.3 collective-permute-start.16
  89.9 0.8 collective-permute-start.17
  90.7 6.5 %collective-permute-done.16.refs_2_ = bf16[2,64,1792]{2,1,0:T(8,128)(2,1)S(1)} collective-permute-done((bf16[2,64,1792]{2,1,0:T(8,128)(2,1)S(1)}, bf16[2,64,1792]{2,1,0:T(8,128)(2,1)S(1)}, u32[]{:S(2)}, u32[]{:S(2)}) %collective-permute-start.16) | collective-permute-done | bytes 458784 | tf_op jit(solution)/shard_map/ppermute | solution.py:23
  97.1 1.2 collective-permute-done.17.refs_5_
  98.3 1.7 %collective-permute-start.18 = (bf16[2,64,1792]{2,1,0:T(8,128)(2,1)S(1)}, bf16[2,64,1792]{2,1,0:T(8,128)(2,1)S(1)}, u32[]{:S(2)}, u32[]{:S(2)}) collective-permute-start(bf16[2,64,1792]{2,1,0:T(8,128)(2,1)S(1)} %get-tuple-element.104.refs_1_), channel_id=1, source_target_pairs={{0,1},{1,2},{2,3},{3,0},{4,5},{5,6},{6,7},{7,4},{8,9},{9,10},{10,1... | collective-permute-start | bytes 1376264 | tf_op jit(solution)/shard_map/ppermute | solution.py:23
  100.0 0.3 collective-permute-start.19
  100.4 1.7 %collective-permute-start.20 = (bf16[2,64,1792]{2,1,0:T(8,128)(2,1)S(1)}, bf16[2,64,1792]{2,1,0:T(8,128)(2,1)S(1)}, u32[]{:S(2)}, u32[]{:S(2)}) collective-permute-start(bf16[2,64,1792]{2,1,0:T(8,128)(2,1)S(1)} %collective-permute-done.16.refs_2_), channel_id=1, source_target_pairs={{0,1},{1,2},{2,3},{3,0},{4,5},{5,6},{6,7},{7,4},{8,9},{9,10},{10,1... | collective-permute-start | bytes 1376264 | tf_op jit(solution)/shard_map/ppermute | solution.py:23
  102.1 0.4 collective-permute-start.21
  102.4 4.4 %collective-permute-done.18.refs_3_ = bf16[2,64,1792]{2,1,0:T(8,128)(2,1)S(1)} collective-permute-done((bf16[2,64,1792]{2,1,0:T(8,128)(2,1)S(1)}, bf16[2,64,1792]{2,1,0:T(8,128)(2,1)S(1)}, u32[]{:S(2)}, u32[]{:S(2)}) %collective-permute-start.18) | collective-permute-done | bytes 458784 | tf_op jit(solution)/shard_map/ppermute | solution.py:23
  106.8 1.7 %collective-permute-done.19.refs_4_ = bf16[2,64,1792]{2,1,0:T(8,128)(2,1)S(1)} collective-permute-done((bf16[2,64,1792]{2,1,0:T(8,128)(2,1)S(1)}, bf16[2,64,1792]{2,1,0:T(8,128)(2,1)S(1)}, u32[]{:S(2)}, u32[]{:S(2)}) %collective-permute-start.19) | collective-permute-done | bytes 458784 | tf_op jit(solution)/shard_map/ppermute | solution.py:23
  108.5 1.5 %collective-permute-start.23 = (bf16[128,1792]{1,0:T(8,128)(2,1)S(1)}, bf16[128,1792]{1,0:T(8,128)(2,1)S(1)}, u32[]{:S(2)}, u32[]{:S(2)}) collective-permute-start(bf16[128,1792]{1,0:T(8,128)(2,1)S(1)} %get-tuple-element.128.refs_0_), channel_id=1, source_target_pairs={{0,1},{1,2},{2,3},{3,0},{4,5},{5,6},{6,7},{7,4},{8,9},{9,10},{10,1... | collective-permute-start | bytes 1376264 | tf_op jit(solution)/shard_map/ppermute | solution.py:23
  110.0 0.5 collective-permute-start.24
  110.5 2.4 %collective-permute-start.25 = (bf16[128,1792]{1,0:T(8,128)(2,1)S(1)}, bf16[128,1792]{1,0:T(8,128)(2,1)S(1)}, u32[]{:S(2)}, u32[]{:S(2)}) collective-permute-start(bf16[128,1792]{1,0:T(8,128)(2,1)S(1)} %get-tuple-element.128.refs_0_), channel_id=1, source_target_pairs={{0,2},{1,3},{2,0},{3,1},{4,6},{5,7},{6,4},{7,5},{8,10},{9,11},{10,... | collective-permute-start | bytes 1376264 | tf_op jit(solution)/shard_map/ppermute | solution.py:23
  113.0 0.5 collective-permute-done.21.refs_7_
  113.4 2.8 %shard_map.92 = (bf16[256,512]{1,0:T(8,128)(2,1)S(1)}, bf16[256,512]{1,0:T(8,128)(2,1)S(1)}) custom-call(s32[2]{0:T(128)S(1)} %pad_add_fusion.place, bf16[512,1792]{1,0:T(8,128)(2,1)S(1)} %copy-done.1, bf16[512,1792]{1,0:T(8,128)(2,1)S(1)} %copy-done.3, bf16[2,64,1792]{2,1,0:T(8,128)(2,1)S(1)} %get-tuple-element.103.refs_0_, ...), custom_call_target="tpu_custom_call" | custom-call | flops 1879048192 | bytes 7340040 | tf_op jit(solution)/shard_map/pallas_call | solution.py:53
  116.2 4.0 %collective-permute-start.22 = (bf16[256,512]{1,0:T(8,128)(2,1)S(1)}, bf16[256,512]{1,0:T(8,128)(2,1)S(1)}, u32[]{:S(2)}, u32[]{:S(2)}) collective-permute-start(bf16[256,512]{1,0:T(8,128)(2,1)S(1)} %get-tuple-element.102), channel_id=1, source_target_pairs={{0,16},{16,0},{32,48},{48,32},{64,80},{80,64},{96,112},{112,96},{1... | collective-permute-start | bytes 786440 | tf_op jit(solution)/shard_map/ppermute | solution.py:41
  120.2 2.8 %shard_map.93 = (bf16[512,1792]{1,0:T(8,128)(2,1)S(1)}, bf16[512,1792]{1,0:T(8,128)(2,1)S(1)}) custom-call(s32[2]{0:T(128)S(1)} %pad_add_fusion.place, bf16[256,1024]{1,0:T(8,128)(2,1)S(1)} %shard_map.85.act.low, bf16[256,1024]{1,0:T(8,128)(2,1)S(1)} %collective-permute-done.3.act.high, bf16[2,64,1792]{2,1,0:T(8,128)(2,1)S(1)} %get-tuple-element.103.refs_0_, ...), custom_call_target="tpu_custom_call" | custom-call | flops 1879048192 | bytes 4718600 | tf_op jit(solution)/shard_map/pallas_call | solution.py:53
  123.1 1.5 %collective-permute-done.22.got = bf16[256,512]{1,0:T(8,128)(2,1)S(1)} collective-permute-done((bf16[256,512]{1,0:T(8,128)(2,1)S(1)}, bf16[256,512]{1,0:T(8,128)(2,1)S(1)}, u32[]{:S(2)}, u32[]{:S(2)}) %collective-permute-start.22) | collective-permute-done | bytes 262176 | tf_op jit(solution)/shard_map/ppermute | solution.py:41
  124.6 0.5 collective-permute-start.28
  125.2 1.8 %shard_map.98.refs_0_ = bf16[1792,512]{1,0:T(8,128)(2,1)S(1)} custom-call(s32[2]{0:T(128)S(1)} %pad_add_fusion.place, bf16[256,1024]{1,0:T(8,128)(2,1)S(1)} %shard_map.85.act.low, bf16[256,1024]{1,0:T(8,128)(2,1)S(1)} %collective-permute-done.3.act.high, bf16[128,1792]{1,0:T(8,128)(2,1)S(1)} %get-tuple-element.128.refs_0_, ...), custom_call_target="tpu_custom_call" | custom-call | flops 939524096 | bytes 2883592 | tf_op jit(solution)/shard_map/pallas_call | solution.py:53
  127.4 5.2 %collective-permute-start.27 = (bf16[64,512]{1,0:T(8,128)(2,1)S(1)}, bf16[64,512]{1,0:T(8,128)(2,1)S(1)}, u32[]{:S(2)}, u32[]{:S(2)}) collective-permute-start(bf16[64,512]{1,0:T(8,128)(2,1)S(1)} %get-tuple-element.121), channel_id=1, source_target_pairs={{0,64},{16,80},{32,96},{48,112},{64,0},{80,16},{96,32},{112,48},{1... | collective-permute-start | bytes 196616 | tf_op jit(solution)/shard_map/ppermute | solution.py:32
  132.6 1.7 %shard_map.96 = bf16[512,1792]{1,0:T(8,128)(2,1)} custom-call(bf16[512,1792]{1,0:T(8,128)(2,1)S(1)} %get-tuple-element.124.refs_0_, bf16[512,1792]{1,0:T(8,128)(2,1)S(1)} %collective-permute-done.29.refs_1_), custom_call_target="tpu_custom_call" | custom-call | bytes 3670016 | tf_op jit(solution)/shard_map/pallas_call | solution.py:53
  134.3 1.6 %shard_map.95 = bf16[512,1792]{1,0:T(8,128)(2,1)} custom-call(bf16[512,1792]{1,0:T(8,128)(2,1)S(1)} %get-tuple-element.123.refs_0_, bf16[512,1792]{1,0:T(8,128)(2,1)S(1)} %collective-permute-done.28.refs_1_), custom_call_target="tpu_custom_call" | custom-call | bytes 3670016 | tf_op jit(solution)/shard_map/pallas_call | solution.py:53
  135.9 1.3 collective-permute-start.30
  137.3 4.7 %collective-permute-done.30.refs_3_ = bf16[64,512]{1,0:T(8,128)(2,1)S(1)} collective-permute-done((bf16[64,512]{1,0:T(8,128)(2,1)S(1)}, bf16[64,512]{1,0:T(8,128)(2,1)S(1)}, u32[]{:S(2)}, u32[]{:S(2)}) %collective-permute-start.30) | collective-permute-done | bytes 65568 | tf_op jit(solution)/shard_map/ppermute | solution.py:32
  141.9 0.7 shard_map.97
  142.6 1.7 %shard_map.99 = bf16[1792,512]{1,0:T(8,128)(2,1)} custom-call(bf16[1792,512]{1,0:T(8,128)(2,1)S(1)} %shard_map.98.refs_0_, bf16[1792,512]{1,0:T(8,128)(2,1)S(1)} %collective-permute-done.31.refs_1_), custom_call_target="tpu_custom_call" | custom-call | bytes 3670016 | tf_op jit(solution)/shard_map/pallas_call | solution.py:53
  (33 shorter events, 1.0 us)
Async XLA Ops:
  0.6 0.8 copy-start.6
  1.5 0.8 copy-start.7
  2.3 16.2 %collective-permute-start = (bf16[64,1024]{1,0:T(8,128)(2,1)S(1)}, bf16[64,1024]{1,0:T(8,128)(2,1)S(1)}, u32[]{:S(2)}, u32[]{:S(2)}) collective-permute-start(bf16[64,1024]{1,0:T(8,128)(2,1)S(1)} %shard_map.84.refs_0_), channel_id=1, source_target_pairs={{0,96},{16,112},{32,0},{48,16},{64,32},{80,48},{96,64},{112,80},{1... | collective-permute-start | bytes 393224 | tf_op jit(solution)/shard_map/ppermute | solution.py:32
  8.7 11.1 %collective-permute-start.1 = (bf16[64,1024]{1,0:T(8,128)(2,1)S(1)}, bf16[64,1024]{1,0:T(8,128)(2,1)S(1)}, u32[]{:S(2)}, u32[]{:S(2)}) collective-permute-start(bf16[64,1024]{1,0:T(8,128)(2,1)S(1)} %shard_map.84.refs_0_), channel_id=1, source_target_pairs={{0,64},{16,80},{32,96},{48,112},{64,0},{80,16},{96,32},{112,48},{1... | collective-permute-start | bytes 393224 | tf_op jit(solution)/shard_map/ppermute | solution.py:32
  9.7 10.1 %collective-permute-start.2 = (bf16[64,1024]{1,0:T(8,128)(2,1)S(1)}, bf16[64,1024]{1,0:T(8,128)(2,1)S(1)}, u32[]{:S(2)}, u32[]{:S(2)}) collective-permute-start(bf16[64,1024]{1,0:T(8,128)(2,1)S(1)} %shard_map.84.refs_0_), channel_id=1, source_target_pairs={{0,32},{16,48},{32,64},{48,80},{64,96},{80,112},{96,0},{112,16},{1... | collective-permute-start | bytes 393224 | tf_op jit(solution)/shard_map/ppermute | solution.py:32
  19.8 10.5 %collective-permute-start.3 = (bf16[256,1024]{1,0:T(8,128)(2,1)S(1)}, bf16[256,1024]{1,0:T(8,128)(2,1)S(1)}, u32[]{:S(2)}, u32[]{:S(2)}) collective-permute-start(bf16[256,1024]{1,0:T(8,128)(2,1)S(1)} %shard_map.85.act.low), channel_id=1, source_target_pairs={{0,16},{16,0},{32,48},{48,32},{64,80},{80,64},{96,112},{112,96},{1... | collective-permute-start | bytes 1572872 | tf_op jit(solution)/shard_map/ppermute | solution.py:41
  23.2 1.5 %copy-start = (bf16[512,1792]{1,0:T(8,128)(2,1)S(1)}, bf16[512,1792]{1,0:T(8,128)(2,1)}, u32[]{:S(2)}) copy-start(bf16[512,1792]{1,0:T(8,128)(2,1)} %gate.5) | copy-start | bytes 5505028
  24.7 1.5 %copy-start.2 = (bf16[512,1792]{1,0:T(8,128)(2,1)S(1)}, bf16[512,1792]{1,0:T(8,128)(2,1)}, u32[]{:S(2)}) copy-start(bf16[512,1792]{1,0:T(8,128)(2,1)} %up.5) | copy-start | bytes 5505028
  26.2 1.5 %copy-start.4 = (bf16[1792,512]{1,0:T(8,128)(2,1)S(1)}, bf16[1792,512]{1,0:T(8,128)(2,1)}, u32[]{:S(2)}) copy-start(bf16[1792,512]{1,0:T(8,128)(2,1)} %down.3) | copy-start | bytes 5505028
  27.7 2.6 %copy-start.1 = (bf16[512,1792]{1,0:T(8,128)(2,1)S(1)}, bf16[512,1792]{1,0:T(8,128)(2,1)}, u32[]{:S(2)}) copy-start(bf16[512,1792]{1,0:T(8,128)(2,1)} %gate.5) | copy-start | bytes 5505028
  27.7 2.6 %copy-start.3 = (bf16[512,1792]{1,0:T(8,128)(2,1)S(1)}, bf16[512,1792]{1,0:T(8,128)(2,1)}, u32[]{:S(2)}) copy-start(bf16[512,1792]{1,0:T(8,128)(2,1)} %up.5) | copy-start | bytes 5505028
  27.7 2.6 %copy-start.5 = (bf16[1792,512]{1,0:T(8,128)(2,1)S(1)}, bf16[1792,512]{1,0:T(8,128)(2,1)}, u32[]{:S(2)}) copy-start(bf16[1792,512]{1,0:T(8,128)(2,1)} %down.3) | copy-start | bytes 5505028
  32.5 11.0 %collective-permute-start.4 = (bf16[3,64,1792]{2,1,0:T(8,128)(2,1)S(1)}, bf16[3,64,1792]{2,1,0:T(8,128)(2,1)S(1)}, u32[]{:S(2)}, u32[]{:S(2)}) collective-permute-start(bf16[3,64,1792]{2,1,0:T(8,128)(2,1)S(1)} %get-tuple-element.79), channel_id=1, source_target_pairs={{0,1},{1,2},{2,3},{3,0},{4,5},{5,6},{6,7},{7,4},{8,9},{9,10},{10,1... | collective-permute-start | bytes 2064392 | tf_op jit(solution)/shard_map/ppermute | solution.py:23
  34.1 10.9 %collective-permute-start.5 = (bf16[3,64,1792]{2,1,0:T(8,128)(2,1)S(1)}, bf16[3,64,1792]{2,1,0:T(8,128)(2,1)S(1)}, u32[]{:S(2)}, u32[]{:S(2)}) collective-permute-start(bf16[3,64,1792]{2,1,0:T(8,128)(2,1)S(1)} %get-tuple-element.80), channel_id=1, source_target_pairs={{0,3},{1,0},{2,1},{3,2},{4,7},{5,4},{6,5},{7,6},{8,11},{9,8},{10,9... | collective-permute-start | bytes 2064392 | tf_op jit(solution)/shard_map/ppermute | solution.py:23
  34.6 17.8 %collective-permute-start.7 = (bf16[3,64,1792]{2,1,0:T(8,128)(2,1)S(1)}, bf16[3,64,1792]{2,1,0:T(8,128)(2,1)S(1)}, u32[]{:S(2)}, u32[]{:S(2)}) collective-permute-start(bf16[3,64,1792]{2,1,0:T(8,128)(2,1)S(1)} %get-tuple-element.82), channel_id=1, source_target_pairs={{0,3},{1,0},{2,1},{3,2},{4,7},{5,4},{6,5},{7,6},{8,11},{9,8},{10,9... | collective-permute-start | bytes 2064392 | tf_op jit(solution)/shard_map/ppermute | solution.py:23
  36.7 15.7 %collective-permute-start.9 = (bf16[3,64,1792]{2,1,0:T(8,128)(2,1)S(1)}, bf16[3,64,1792]{2,1,0:T(8,128)(2,1)S(1)}, u32[]{:S(2)}, u32[]{:S(2)}) collective-permute-start(bf16[3,64,1792]{2,1,0:T(8,128)(2,1)S(1)} %get-tuple-element.85), channel_id=1, source_target_pairs={{0,1},{1,2},{2,3},{3,0},{4,5},{5,6},{6,7},{7,4},{8,9},{9,10},{10,1... | collective-permute-start | bytes 2064392 | tf_op jit(solution)/shard_map/ppermute | solution.py:23
  45.4 12.9 %collective-permute-start.6 = (bf16[3,64,1792]{2,1,0:T(8,128)(2,1)S(1)}, bf16[3,64,1792]{2,1,0:T(8,128)(2,1)S(1)}, u32[]{:S(2)}, u32[]{:S(2)}) collective-permute-start(bf16[3,64,1792]{2,1,0:T(8,128)(2,1)S(1)} %get-tuple-element.81), channel_id=1, source_target_pairs={{0,1},{1,2},{2,3},{3,0},{4,5},{5,6},{6,7},{7,4},{8,9},{9,10},{10,1... | collective-permute-start | bytes 2064392 | tf_op jit(solution)/shard_map/ppermute | solution.py:23
  46.6 13.2 %collective-permute-start.8 = (bf16[3,64,1792]{2,1,0:T(8,128)(2,1)S(1)}, bf16[3,64,1792]{2,1,0:T(8,128)(2,1)S(1)}, u32[]{:S(2)}, u32[]{:S(2)}) collective-permute-start(bf16[3,64,1792]{2,1,0:T(8,128)(2,1)S(1)} %get-tuple-element.84), channel_id=1, source_target_pairs={{0,3},{1,0},{2,1},{3,2},{4,7},{5,4},{6,5},{7,6},{8,11},{9,8},{10,9... | collective-permute-start | bytes 2064392 | tf_op jit(solution)/shard_map/ppermute | solution.py:23
  61.5 8.7 %collective-permute-start.10 = (bf16[3,32,1792]{2,1,0:T(8,128)(2,1)S(1)}, bf16[3,32,1792]{2,1,0:T(8,128)(2,1)S(1)}, u32[]{:S(2)}, u32[]{:S(2)}) collective-permute-start(bf16[3,32,1792]{2,1,0:T(8,128)(2,1)S(1)} %get-tuple-element.87), channel_id=1, source_target_pairs={{0,4},{1,5},{2,6},{3,7},{4,8},{5,9},{6,10},{7,11},{8,12},{9,13},{1... | collective-permute-start | bytes 1032200 | tf_op jit(solution)/shard_map/ppermute | solution.py:23
  63.3 11.8 %collective-permute-start.11 = (bf16[3,32,1792]{2,1,0:T(8,128)(2,1)S(1)}, bf16[3,32,1792]{2,1,0:T(8,128)(2,1)S(1)}, u32[]{:S(2)}, u32[]{:S(2)}) collective-permute-start(bf16[3,32,1792]{2,1,0:T(8,128)(2,1)S(1)} %get-tuple-element.88), channel_id=1, source_target_pairs={{0,8},{1,9},{2,10},{3,11},{4,12},{5,13},{6,14},{7,15},{8,0},{9,1},... | collective-permute-start | bytes 1032200 | tf_op jit(solution)/shard_map/ppermute | solution.py:23
  66.2 8.9 %collective-permute-start.12 = (bf16[3,32,1792]{2,1,0:T(8,128)(2,1)S(1)}, bf16[3,32,1792]{2,1,0:T(8,128)(2,1)S(1)}, u32[]{:S(2)}, u32[]{:S(2)}) collective-permute-start(bf16[3,32,1792]{2,1,0:T(8,128)(2,1)S(1)} %get-tuple-element.89), channel_id=1, source_target_pairs={{0,12},{1,13},{2,14},{3,15},{4,0},{5,1},{6,2},{7,3},{8,4},{9,5},{1... | collective-permute-start | bytes 1032200 | tf_op jit(solution)/shard_map/ppermute | solution.py:23
  75.4 8.5 %collective-permute-start.13 = (bf16[3,32,1792]{2,1,0:T(8,128)(2,1)S(1)}, bf16[3,32,1792]{2,1,0:T(8,128)(2,1)S(1)}, u32[]{:S(2)}, u32[]{:S(2)}) collective-permute-start(bf16[3,32,1792]{2,1,0:T(8,128)(2,1)S(1)} %shard_map.90.refs_0_), channel_id=1, source_target_pairs={{0,4},{1,5},{2,6},{3,7},{4,8},{5,9},{6,10},{7,11},{8,12},{9,13},{1... | collective-permute-start | bytes 1032200 | tf_op jit(solution)/shard_map/ppermute | solution.py:23
  77.1 11.0 %collective-permute-start.14 = (bf16[3,32,1792]{2,1,0:T(8,128)(2,1)S(1)}, bf16[3,32,1792]{2,1,0:T(8,128)(2,1)S(1)}, u32[]{:S(2)}, u32[]{:S(2)}) collective-permute-start(bf16[3,32,1792]{2,1,0:T(8,128)(2,1)S(1)} %shard_map.90.refs_0_), channel_id=1, source_target_pairs={{0,8},{1,9},{2,10},{3,11},{4,12},{5,13},{6,14},{7,15},{8,0},{9,1},... | collective-permute-start | bytes 1032200 | tf_op jit(solution)/shard_map/ppermute | solution.py:23
  79.2 9.3 %collective-permute-start.15 = (bf16[3,32,1792]{2,1,0:T(8,128)(2,1)S(1)}, bf16[3,32,1792]{2,1,0:T(8,128)(2,1)S(1)}, u32[]{:S(2)}, u32[]{:S(2)}) collective-permute-start(bf16[3,32,1792]{2,1,0:T(8,128)(2,1)S(1)} %shard_map.90.refs_0_), channel_id=1, source_target_pairs={{0,12},{1,13},{2,14},{3,15},{4,0},{5,1},{6,2},{7,3},{8,4},{9,5},{1... | collective-permute-start | bytes 1032200 | tf_op jit(solution)/shard_map/ppermute | solution.py:23
  88.6 8.6 %collective-permute-start.16 = (bf16[2,64,1792]{2,1,0:T(8,128)(2,1)S(1)}, bf16[2,64,1792]{2,1,0:T(8,128)(2,1)S(1)}, u32[]{:S(2)}, u32[]{:S(2)}) collective-permute-start(bf16[2,64,1792]{2,1,0:T(8,128)(2,1)S(1)} %get-tuple-element.103.refs_0_), channel_id=1, source_target_pairs={{0,1},{1,2},{2,3},{3,0},{4,5},{5,6},{6,7},{7,4},{8,9},{9,10},{10,1... | collective-permute-start | bytes 1376264 | tf_op jit(solution)/shard_map/ppermute | solution.py:23
  89.9 8.5 %collective-permute-start.17 = (bf16[2,64,1792]{2,1,0:T(8,128)(2,1)S(1)}, bf16[2,64,1792]{2,1,0:T(8,128)(2,1)S(1)}, u32[]{:S(2)}, u32[]{:S(2)}) collective-permute-start(bf16[2,64,1792]{2,1,0:T(8,128)(2,1)S(1)} %get-tuple-element.104.refs_1_), channel_id=1, source_target_pairs={{0,3},{1,0},{2,1},{3,2},{4,7},{5,4},{6,5},{7,6},{8,11},{9,8},{10,9... | collective-permute-start | bytes 1376264 | tf_op jit(solution)/shard_map/ppermute | solution.py:23
  98.3 8.5 %collective-permute-start.18 = (bf16[2,64,1792]{2,1,0:T(8,128)(2,1)S(1)}, bf16[2,64,1792]{2,1,0:T(8,128)(2,1)S(1)}, u32[]{:S(2)}, u32[]{:S(2)}) collective-permute-start(bf16[2,64,1792]{2,1,0:T(8,128)(2,1)S(1)} %get-tuple-element.104.refs_1_), channel_id=1, source_target_pairs={{0,1},{1,2},{2,3},{3,0},{4,5},{5,6},{6,7},{7,4},{8,9},{9,10},{10,1... | collective-permute-start | bytes 1376264 | tf_op jit(solution)/shard_map/ppermute | solution.py:23
  100.0 8.5 %collective-permute-start.19 = (bf16[2,64,1792]{2,1,0:T(8,128)(2,1)S(1)}, bf16[2,64,1792]{2,1,0:T(8,128)(2,1)S(1)}, u32[]{:S(2)}, u32[]{:S(2)}) collective-permute-start(bf16[2,64,1792]{2,1,0:T(8,128)(2,1)S(1)} %get-tuple-element.103.refs_0_), channel_id=1, source_target_pairs={{0,3},{1,0},{2,1},{3,2},{4,7},{5,4},{6,5},{7,6},{8,11},{9,8},{10,9... | collective-permute-start | bytes 1376264 | tf_op jit(solution)/shard_map/ppermute | solution.py:23
  100.4 12.6 %collective-permute-start.20 = (bf16[2,64,1792]{2,1,0:T(8,128)(2,1)S(1)}, bf16[2,64,1792]{2,1,0:T(8,128)(2,1)S(1)}, u32[]{:S(2)}, u32[]{:S(2)}) collective-permute-start(bf16[2,64,1792]{2,1,0:T(8,128)(2,1)S(1)} %collective-permute-done.16.refs_2_), channel_id=1, source_target_pairs={{0,1},{1,2},{2,3},{3,0},{4,5},{5,6},{6,7},{7,4},{8,9},{9,10},{10,1... | collective-permute-start | bytes 1376264 | tf_op jit(solution)/shard_map/ppermute | solution.py:23
  102.1 11.4 %collective-permute-start.21 = (bf16[2,64,1792]{2,1,0:T(8,128)(2,1)S(1)}, bf16[2,64,1792]{2,1,0:T(8,128)(2,1)S(1)}, u32[]{:S(2)}, u32[]{:S(2)}) collective-permute-start(bf16[2,64,1792]{2,1,0:T(8,128)(2,1)S(1)} %collective-permute-done.17.refs_5_), channel_id=1, source_target_pairs={{0,3},{1,0},{2,1},{3,2},{4,7},{5,4},{6,5},{7,6},{8,11},{9,8},{10,9... | collective-permute-start | bytes 1376264 | tf_op jit(solution)/shard_map/ppermute | solution.py:23
  108.5 16.6 %collective-permute-start.23 = (bf16[128,1792]{1,0:T(8,128)(2,1)S(1)}, bf16[128,1792]{1,0:T(8,128)(2,1)S(1)}, u32[]{:S(2)}, u32[]{:S(2)}) collective-permute-start(bf16[128,1792]{1,0:T(8,128)(2,1)S(1)} %get-tuple-element.128.refs_0_), channel_id=1, source_target_pairs={{0,1},{1,2},{2,3},{3,0},{4,5},{5,6},{6,7},{7,4},{8,9},{9,10},{10,1... | collective-permute-start | bytes 1376264 | tf_op jit(solution)/shard_map/ppermute | solution.py:23
  110.0 15.2 %collective-permute-start.24 = (bf16[128,1792]{1,0:T(8,128)(2,1)S(1)}, bf16[128,1792]{1,0:T(8,128)(2,1)S(1)}, u32[]{:S(2)}, u32[]{:S(2)}) collective-permute-start(bf16[128,1792]{1,0:T(8,128)(2,1)S(1)} %get-tuple-element.128.refs_0_), channel_id=1, source_target_pairs={{0,3},{1,0},{2,1},{3,2},{4,7},{5,4},{6,5},{7,6},{8,11},{9,8},{10,9... | collective-permute-start | bytes 1376264 | tf_op jit(solution)/shard_map/ppermute | solution.py:23
  110.5 14.6 %collective-permute-start.25 = (bf16[128,1792]{1,0:T(8,128)(2,1)S(1)}, bf16[128,1792]{1,0:T(8,128)(2,1)S(1)}, u32[]{:S(2)}, u32[]{:S(2)}) collective-permute-start(bf16[128,1792]{1,0:T(8,128)(2,1)S(1)} %get-tuple-element.128.refs_0_), channel_id=1, source_target_pairs={{0,2},{1,3},{2,0},{3,1},{4,6},{5,7},{6,4},{7,5},{8,10},{9,11},{10,... | collective-permute-start | bytes 1376264 | tf_op jit(solution)/shard_map/ppermute | solution.py:23
  116.2 8.4 %collective-permute-start.22 = (bf16[256,512]{1,0:T(8,128)(2,1)S(1)}, bf16[256,512]{1,0:T(8,128)(2,1)S(1)}, u32[]{:S(2)}, u32[]{:S(2)}) collective-permute-start(bf16[256,512]{1,0:T(8,128)(2,1)S(1)} %get-tuple-element.102), channel_id=1, source_target_pairs={{0,16},{16,0},{32,48},{48,32},{64,80},{80,64},{96,112},{112,96},{1... | collective-permute-start | bytes 786440 | tf_op jit(solution)/shard_map/ppermute | solution.py:41
  124.6 8.0 %collective-permute-start.29 = (bf16[512,1792]{1,0:T(8,128)(2,1)S(1)}, bf16[512,1792]{1,0:T(8,128)(2,1)S(1)}, u32[]{:S(2)}, u32[]{:S(2)}) collective-permute-start(bf16[512,1792]{1,0:T(8,128)(2,1)S(1)} %get-tuple-element.124.refs_0_), channel_id=1, source_target_pairs={{0,128},{128,0},{1,129},{129,1},{2,130},{130,2},{3,131},{131,3},{4... | collective-permute-start | bytes 5505032 | tf_op jit(solution)/shard_map/ppermute | solution.py:45
  124.6 9.7 %collective-permute-start.28 = (bf16[512,1792]{1,0:T(8,128)(2,1)S(1)}, bf16[512,1792]{1,0:T(8,128)(2,1)S(1)}, u32[]{:S(2)}, u32[]{:S(2)}) collective-permute-start(bf16[512,1792]{1,0:T(8,128)(2,1)S(1)} %get-tuple-element.123.refs_0_), channel_id=1, source_target_pairs={{0,128},{128,0},{1,129},{129,1},{2,130},{130,2},{3,131},{131,3},{4... | collective-permute-start | bytes 5505032 | tf_op jit(solution)/shard_map/ppermute | solution.py:45
  127.0 15.6 %collective-permute-start.31 = (bf16[1792,512]{1,0:T(8,128)(2,1)S(1)}, bf16[1792,512]{1,0:T(8,128)(2,1)S(1)}, u32[]{:S(2)}, u32[]{:S(2)}) collective-permute-start(bf16[1792,512]{1,0:T(8,128)(2,1)S(1)} %shard_map.98.refs_0_), channel_id=1, source_target_pairs={{0,128},{128,0},{1,129},{129,1},{2,130},{130,2},{3,131},{131,3},{4... | collective-permute-start | bytes 5505032 | tf_op jit(solution)/shard_map/ppermute | solution.py:45
  127.1 10.1 %collective-permute-start.26 = (bf16[64,512]{1,0:T(8,128)(2,1)S(1)}, bf16[64,512]{1,0:T(8,128)(2,1)S(1)}, u32[]{:S(2)}, u32[]{:S(2)}) collective-permute-start(bf16[64,512]{1,0:T(8,128)(2,1)S(1)} %get-tuple-element.120), channel_id=1, source_target_pairs={{0,32},{16,48},{32,64},{48,80},{64,96},{80,112},{96,0},{112,16},{1... | collective-permute-start | bytes 196616 | tf_op jit(solution)/shard_map/ppermute | solution.py:32
  127.4 9.9 %collective-permute-start.27 = (bf16[64,512]{1,0:T(8,128)(2,1)S(1)}, bf16[64,512]{1,0:T(8,128)(2,1)S(1)}, u32[]{:S(2)}, u32[]{:S(2)}) collective-permute-start(bf16[64,512]{1,0:T(8,128)(2,1)S(1)} %get-tuple-element.121), channel_id=1, source_target_pairs={{0,64},{16,80},{32,96},{48,112},{64,0},{80,16},{96,32},{112,48},{1... | collective-permute-start | bytes 196616 | tf_op jit(solution)/shard_map/ppermute | solution.py:32
  135.9 6.0 %collective-permute-start.30 = (bf16[64,512]{1,0:T(8,128)(2,1)S(1)}, bf16[64,512]{1,0:T(8,128)(2,1)S(1)}, u32[]{:S(2)}, u32[]{:S(2)}) collective-permute-start(bf16[64,512]{1,0:T(8,128)(2,1)S(1)} %get-tuple-element.125), channel_id=1, source_target_pairs={{0,96},{16,112},{32,0},{48,16},{64,32},{80,48},{96,64},{112,80},{1... | collective-permute-start | bytes 196616 | tf_op jit(solution)/shard_map/ppermute | solution.py:32

commit v2 on v1

--- a/solution.py
+++ b/solution.py
@@ -1,3 +1,5 @@
+import functools
+
 import jax
 import jax.numpy as jnp
 from jax import lax
@@ -6,6 +8,7 @@
 from jax.sharding import PartitionSpec as P
 
 RING = 4
+MERGE = 8
 BF16 = jnp.bfloat16
 F32 = jnp.float32
 
@@ -77,10 +80,11 @@
         refs[4][count * i : count * i + count] = refs[i][...]
 
 
-def product_kernel(place, act, gate, up, down, *refs):
-    first, outs = refs[:-8], refs[-8:]
+def product_kernel(steps, place, act, gate, up, down, *refs):
+    groups = 2 * len(steps)
+    first, outs = refs[:-groups], refs[-groups:]
     width = gate.shape[0]
-    rows = [rows_of(lax.rem(place[0] + step, RING) * 64, 64) for step in (2, 1, 3, 0)]
+    rows = [rows_of(lax.rem(place[0] + step, RING) * 64, 64) for step in steps]
     both = jnp.concatenate([act[r] for r in rows], axis=0)
     tok, cot = both[:, :width], both[:, width:]
     for k in range(3):
@@ -91,11 +95,11 @@
                 cot, down[...], (((1,), (1,)), ((), ())), preferred_element_type=F32
             )
         term = term.astype(BF16)
-        for q in range(8):
+        for q in range(groups):
             out = outs[q]
             out[k, out.shape[1] - 32 :] = term[32 * q : 32 * q + 32]
     if first:
-        for q in range(8):
+        for q in range(groups):
             outs[q][:, :32] = first[q][...]
 
 
@@ -153,21 +157,24 @@
             ug[rows] = piece[1, lower : lower + 32, :]
 
 
-def input_kernel(place, gate, up, *refs):
-    pieces, keep, give, gg, ug = refs[:8], *refs[8:]
+def give_kernel(place, gate, up, *refs):
+    pieces, out, gg, ug = refs[:8], *refs[8:]
     assemble(place, pieces, gg, ug)
+    out[...] = input_sum(gg[out.shape[0] :], ug[out.shape[0] :], gate, up).astype(BF16)
+
+
+def input_sum(gg, ug, gate, up):
     contract = (((1,), (1,)), ((), ()))
-    total = lax.dot_general(gg[...], gate[...], contract, preferred_element_type=F32)
-    total += lax.dot_general(ug[...], up[...], contract, preferred_element_type=F32)
-    total = total.astype(BF16)
-    rows = keep.shape[0]
-    keep[...] = total[:rows]
-    give[...] = total[rows:]
-
-
-def feature_kernel(place, low, high, *refs):
-    pieces, gate_out, up_out, act, gg, ug = refs[:8], *refs[8:]
-    assemble(place, pieces, gg, ug)
+    total = lax.dot_general(gg, gate[...], contract, preferred_element_type=F32)
+    return total + lax.dot_general(ug, up[...], contract, preferred_element_type=F32)
+
+
+def keep_kernel(gate, up, gg, ug, out):
+    rows = out.shape[0]
+    out[...] = input_sum(gg[:rows], ug[:rows], gate, up)
+
+
+def feature_kernel(low, high, gg, ug, gate_out, up_out, act):
     width, rows = gate_out.shape[0], low.shape[0]
     act[:rows] = low[:, :width]
     act[rows:] = high[:, :width]
@@ -192,11 +199,11 @@
     ).astype(BF16)
 
 
-def relay_kernel(keep, got, *outs):
+def split_kernel(keep, got, *outs):
     count = outs[0].shape[0]
     for i in range(4):
         rows = slice(count * i, count * i + count)
-        outs[i][...] = (keep[rows].astype(F32) + got[rows].astype(F32)).astype(BF16)
+        outs[i][...] = (keep[rows] + got[rows].astype(F32)).astype(BF16)
 
 
 def sum_kernel(*refs):
@@ -204,6 +211,29 @@
     for ref in refs[1:-1]:
         total = total + ref[...].astype(F32)
     refs[-1][...] = total.astype(BF16)
+
+
+def merge_kernel(mine, got, out, held, sems):
+    count = mine.shape[0] // MERGE
+    copies = []
+    for i in range(MERGE):
+        rows = pl.ds(count * i, count)
+        held[rows] = (mine[rows].astype(F32) + got[rows].astype(F32)).astype(BF16)
+        copies.append(pltpu.make_async_copy(held.at[rows], out.at[rows], sems.at[i]))
+        copies[-1].start()
+    for copy in copies:
+        copy.wait()
+
+
+def merge(term):
+    return pl.pallas_call(
+        merge_kernel,
+        out_shape=jax.ShapeDtypeStruct(term.shape, BF16),
+        in_specs=[pl.BlockSpec(memory_space=pltpu.VMEM)] * 2,
+        out_specs=pl.BlockSpec(memory_space=pl.ANY),
+        scratch_shapes=[pltpu.VMEM(term.shape, BF16), pltpu.SemaphoreType.DMA((MERGE,))],
+        compiler_params=pltpu.CompilerParams(vmem_limit_bytes=24 * 1024 * 1024),
+    )(term, swap_dp(term))
 
 
 def body(tokens, cotangent, gate, up, down):
@@ -221,14 +251,18 @@
     odd = swap_row(even)
 
     third, half = ((3, 32, hidden), BF16), ((3, 64, hidden), BF16)
-    part = ()
-    for act, kind in ((even, third), (odd, half)):
-        part = call(
-            product_kernel,
-            [kind] * 8,
-            (place, act, gate, up, down) + tuple(part),
-            flops=2 * 256 * width * hidden * 3,
+    weights = (gate, up, down)
+
+    def products(steps, kind, act, earlier):
+        return call(
+            functools.partial(product_kernel, steps),
+            [kind] * (2 * len(steps)),
+            (place, act) + weights + tuple(earlier),
+            flops=2 * 64 * len(steps) * width * hidden * 3,
         )
+
+    part = products((2, 1, 3, 0), third, even, ())
+    part = products((2,), half, odd, part[:2]) + products((1, 3, 0), half, odd, part[2:])
     far_up, far_down, pass_up, near_up, near_down, pass_down, low, high = part
     far_up, far_down = send_col(far_up, 0, 1), send_col(far_down, 0, -1)
     near_up, near_down = send_col(near_up, 0, 1), send_col(near_down, 0, -1)
@@ -259,29 +293,26 @@
     whole = pltpu.VMEM((rows, hidden), BF16)
     lhs = pltpu.VMEM((rows, width), BF16)
     work = 2 * rows * width * hidden
-    keep, give = call(
-        input_kernel,
-        [((4 * count, width), BF16)] * 2,
+    give, gg, ug = call(
+        give_kernel,
+        [((4 * count, width), BF16)] + [((rows, hidden), BF16)] * 2,
         (place, gate, up) + pieces,
-        scratch=[whole, whole],
-        flops=2 * work,
-    )
-    keep, give, pieces = lax.optimization_barrier((keep, give, pieces))
+        flops=work,
+    )
     swapped = swap_row(give)
+    keep = call(keep_kernel, [((4 * count, width), F32)], (gate, up, gg, ug), flops=work)[0]
     features = call(
         feature_kernel,
         [((width, hidden), BF16)] * 2,
-        (place, even, odd) + pieces,
-        scratch=[lhs, whole, whole],
+        (even, odd, gg, ug),
+        scratch=[lhs],
         flops=2 * work,
     )
-    swapped, *features = lax.optimization_barrier((swapped, *features))
+    swapped, keep, *features = lax.optimization_barrier((swapped, keep, *features))
     block = ((count, width), BF16)
-    sums = call(relay_kernel, [block] * 4, (keep, swapped))
+    sums = call(split_kernel, [block] * 4, (keep, swapped))
     sums, hids = lax.optimization_barrier((sums, hids))
-    outs = [
-        call(sum_kernel, [(term.shape, BF16)], (term, swap_dp(term)))[0] for term in features
-    ]
+    outs = [merge(term) for term in features]
     down_term = call(
         hidden_kernel,
         [((hidden, width), BF16)],
@@ -289,13 +320,10 @@
         scratch=[lhs, whole],
         flops=work,
     )[0]
-    got = [sums[0]] + [send_row(sums[i], 2 * i) for i in range(1, 3)]
-    last, *outs = lax.optimization_barrier((sums[3], *outs))
-    got.append(send_row(last, 6))
+    got = [sums[0]] + [send_row(sums[i], 2 * i) for i in range(1, 4)]
+    got, outs = lax.optimization_barrier((got, outs))
     input_grad = call(sum_kernel, [block], got)[0]
-    outs.append(
-        call(sum_kernel, [(down_term.shape, BF16)], (down_term, swap_dp(down_term)))[0]
-    )
+    outs = list(outs) + [merge(down_term)]
     return (input_grad,) + tuple(outs)
 
 

time: 146 us -> 142 us (0.973)
  waiting for transfers between devices: 63.8 us -> 59.7 us
    pallas_call x0 -> x3, Pallas kernels: none -> 4.02 us  [merge(): pl.pallas_call(merge_kernel, out_shape=jax.ShapeDtypeStruct(term.shape, B...]
    pallas_call x16 -> x15, Pallas kernels: 20 us -> 16.1 us  [call(): pl.pallas_call(kernel, out_shape=[jax.ShapeDtypeStruct(shape, kind) for s...]
    ppermute x6, waiting for transfers between devices: 11.9 us -> 10.1 us  [send_row(): return lax.ppermute(value, ('dp', 'row'), pairs)]
    ppermute x21, waiting for transfers between devices: 50 us -> 48.2 us  [send_col(): return lax.ppermute(value, ('dp', 'col'), pairs)]
  transfers between devices with their start and end apart: 32 -> 32, of which waited for: 20 -> 21; matrix products, arithmetic and copies ran while one was open for 0% -> 0% of each run, Pallas kernels for 10% -> 11%
where the time goes in v2:
time: 142 us; the launch traced here: 141 us
  waiting for transfers between devices  59.7 us (42%)
  starting transfers between devices  53.9 us (38%)
  Pallas kernels  20.1 us (14%)
  local copies, waits for them, and re-layouts  6.19 us (4%)
    ppermute x21, waiting for transfers between devices, send_col(): return lax.ppermute(value, ('dp', 'col'), pairs)  48.2 us
    ppermute x21, starting transfers between devices, send_col(): return lax.ppermute(value, ('dp', 'col'), pairs)  28.4 us
    ppermute x6, starting transfers between devices, send_row(): return lax.ppermute(value, ('dp', 'row'), pairs)  17.8 us
    pallas_call x15, Pallas kernels, call(): pl.pallas_call(kernel, out_shape=[jax.ShapeDtypeStruct(shape, kind) for s...  16.1 us
    ppermute x6, waiting for transfers between devices, send_row(): return lax.ppermute(value, ('dp', 'row'), pairs)  10.1 us
    ppermute x2, starting transfers between devices, swap_row(): return lax.ppermute(value, ('dp', 'row'), pairs)  7.06 us
    unnamed x16, local copies, waits for them, and re-layouts  6.19 us
    pallas_call x3, Pallas kernels, merge(): pl.pallas_call(merge_kernel, out_shape=jax.ShapeDtypeStruct(term.shape, B...  4.02 us
  transfers between devices with their start and end apart: 32, of which 21 were waited for; matrix products, arithmetic and copies ran while one was open for 0% of the time, Pallas kernels for 11%

profile of v2, /device:TPU:2, one launch (start us, length us, event | category | flops | bytes accessed | tf_op | source)
XLA Modules:
  0.0 141.0 jit_solution(1271217289848199419)
XLA Ops:
  0.6 0.8 copy-done.6
  1.5 0.8 copy-done.7
  2.3 6.4 %collective-permute-start = (bf16[64,1024]{1,0:T(8,128)(2,1)S(1)}, bf16[64,1024]{1,0:T(8,128)(2,1)S(1)}, u32[]{:S(2)}, u32[]{:S(2)}) collective-permute-start(bf16[64,1024]{1,0:T(8,128)(2,1)S(1)} %shard_map.84.refs_0_), channel_id=1, source_target_pairs={{0,96},{16,112},{32,0},{48,16},{64,32},{80,48},{96,64},{112,80},{1... | collective-permute-start | bytes 393224 | tf_op jit(solution)/shard_map/ppermute | solution.py:35
  8.7 1.0 collective-permute-start.1
  9.7 2.8 %collective-permute-start.2 = (bf16[64,1024]{1,0:T(8,128)(2,1)S(1)}, bf16[64,1024]{1,0:T(8,128)(2,1)S(1)}, u32[]{:S(2)}, u32[]{:S(2)}) collective-permute-start(bf16[64,1024]{1,0:T(8,128)(2,1)S(1)} %shard_map.84.refs_0_), channel_id=1, source_target_pairs={{0,32},{16,48},{32,64},{48,80},{64,96},{80,112},{96,0},{112,16},{1... | collective-permute-start | bytes 393224 | tf_op jit(solution)/shard_map/ppermute | solution.py:35
  12.5 6.0 %collective-permute-done.refs_1_ = bf16[64,1024]{1,0:T(8,128)(2,1)S(1)} collective-permute-done((bf16[64,1024]{1,0:T(8,128)(2,1)S(1)}, bf16[64,1024]{1,0:T(8,128)(2,1)S(1)}, u32[]{:S(2)}, u32[]{:S(2)}) %collective-permute-start) | collective-permute-done | bytes 131104 | tf_op jit(solution)/shard_map/ppermute | solution.py:35
  18.5 1.2 collective-permute-done.1.refs_2_
  19.8 3.3 %collective-permute-start.3 = (bf16[256,1024]{1,0:T(8,128)(2,1)S(1)}, bf16[256,1024]{1,0:T(8,128)(2,1)S(1)}, u32[]{:S(2)}, u32[]{:S(2)}) collective-permute-start(bf16[256,1024]{1,0:T(8,128)(2,1)S(1)} %shard_map.85.act.low), channel_id=1, source_target_pairs={{0,16},{16,0},{32,48},{48,32},{64,80},{80,64},{96,112},{112,96},{1... | collective-permute-start | bytes 1572872 | tf_op jit(solution)/shard_map/ppermute | solution.py:44
  23.2 1.5 %copy-done = bf16[512,1792]{1,0:T(8,128)(2,1)S(1)} copy-done((bf16[512,1792]{1,0:T(8,128)(2,1)S(1)}, bf16[512,1792]{1,0:T(8,128)(2,1)}, u32[]{:S(2)}) %copy-start) | copy-done | bytes 1835032
  24.7 1.5 %copy-done.2 = bf16[512,1792]{1,0:T(8,128)(2,1)S(1)} copy-done((bf16[512,1792]{1,0:T(8,128)(2,1)S(1)}, bf16[512,1792]{1,0:T(8,128)(2,1)}, u32[]{:S(2)}) %copy-start.2) | copy-done | bytes 1835032
  26.2 1.5 %copy-done.4 = bf16[1792,512]{1,0:T(8,128)(2,1)S(1)} copy-done((bf16[1792,512]{1,0:T(8,128)(2,1)S(1)}, bf16[1792,512]{1,0:T(8,128)(2,1)}, u32[]{:S(2)}) %copy-start.4) | copy-done | bytes 1835032
  27.7 2.1 %shard_map.86 = (bf16[3,32,1792]{2,1,0:T(8,128)(2,1)S(1)}, bf16[3,32,1792]{2,1,0:T(8,128)(2,1)S(1)}, bf16[3,32,1792]{2,1,0:T(8,128)(2,1)S(1)}, bf16[3,32,1792]{2...) custom-call(s32[2]{0:T(128)S(1)} %pad_add_fusion.place, ...), custom_call_target="tpu_custom_call" | custom-call | flops 1409286144 | bytes 6029320 | tf_op jit(solution)/shard_map/pallas_call | solution.py:56
  29.8 0.4 collective-permute-done.3.act.high
  30.3 1.9 %shard_map.88 = (bf16[3,64,1792]{2,1,0:T(8,128)(2,1)S(1)}, bf16[3,64,1792]{2,1,0:T(8,128)(2,1)S(1)}) custom-call(s32[2]{0:T(128)S(1)} %pad_add_fusion.place, bf16[256,1024]{1,0:T(8,128)(2,1)S(1)} %collective-permute-done.3.act.high, bf16[512,1792]{1,0:T(8,128)(2,1)S(1)} %copy-done.1, bf16[512,1792]{1,0:T(8,128)(2,1)S(1)} %copy-done.3, ...), custom_call_target="tpu_custom_call" | custom-call | flops 352321536 | bytes 6717448 | tf_op jit(solution)/shard_map/pallas_call | solution.py:56
  32.1 1.6 %collective-permute-start.4 = (bf16[3,64,1792]{2,1,0:T(8,128)(2,1)S(1)}, bf16[3,64,1792]{2,1,0:T(8,128)(2,1)S(1)}, u32[]{:S(2)}, u32[]{:S(2)}) collective-permute-start(bf16[3,64,1792]{2,1,0:T(8,128)(2,1)S(1)} %get-tuple-element.74), channel_id=1, source_target_pairs={{0,1},{1,2},{2,3},{3,0},{4,5},{5,6},{6,7},{7,4},{8,9},{9,10},{10,1... | collective-permute-start | bytes 2064392 | tf_op jit(solution)/shard_map/ppermute | solution.py:26
  33.7 0.5 collective-permute-start.5
  34.2 2.1 %shard_map.87 = (bf16[3,64,1792]{2,1,0:T(8,128)(2,1)S(1)}, bf16[3,64,1792]{2,1,0:T(8,128)(2,1)S(1)}, bf16[3,64,1792]{2,1,0:T(8,128)(2,1)S(1)}, bf16[3,64,1792]{2...) custom-call(s32[2]{0:T(128)S(1)} %pad_add_fusion.place, ...), custom_call_target="tpu_custom_call" | custom-call | flops 1056964608 | bytes 8093704 | tf_op jit(solution)/shard_map/pallas_call | solution.py:56
  36.3 2.2 %collective-permute-start.7 = (bf16[3,64,1792]{2,1,0:T(8,128)(2,1)S(1)}, bf16[3,64,1792]{2,1,0:T(8,128)(2,1)S(1)}, u32[]{:S(2)}, u32[]{:S(2)}) collective-permute-start(bf16[3,64,1792]{2,1,0:T(8,128)(2,1)S(1)} %get-tuple-element.77), channel_id=1, source_target_pairs={{0,3},{1,0},{2,1},{3,2},{4,7},{5,4},{6,5},{7,6},{8,11},{9,8},{10,9... | collective-permute-start | bytes 2064392 | tf_op jit(solution)/shard_map/ppermute | solution.py:26
  38.5 4.7 %collective-permute-done.4.refs_2_ = bf16[3,64,1792]{2,1,0:T(8,128)(2,1)S(1)} collective-permute-done((bf16[3,64,1792]{2,1,0:T(8,128)(2,1)S(1)}, bf16[3,64,1792]{2,1,0:T(8,128)(2,1)S(1)}, u32[]{:S(2)}, u32[]{:S(2)}) %collective-permute-start.4) | collective-permute-done | bytes 688160 | tf_op jit(solution)/shard_map/ppermute | solution.py:26
  43.1 1.5 %collective-permute-done.5.refs_3_ = bf16[3,64,1792]{2,1,0:T(8,128)(2,1)S(1)} collective-permute-done((bf16[3,64,1792]{2,1,0:T(8,128)(2,1)S(1)}, bf16[3,64,1792]{2,1,0:T(8,128)(2,1)S(1)}, u32[]{:S(2)}, u32[]{:S(2)}) %collective-permute-start.5) | collective-permute-done | bytes 688160 | tf_op jit(solution)/shard_map/ppermute | solution.py:26
  44.9 1.3 collective-permute-start.6
  46.2 0.8 collective-permute-start.8
  47.1 5.0 %collective-permute-done.7.refs_2_ = bf16[3,64,1792]{2,1,0:T(8,128)(2,1)S(1)} collective-permute-done((bf16[3,64,1792]{2,1,0:T(8,128)(2,1)S(1)}, bf16[3,64,1792]{2,1,0:T(8,128)(2,1)S(1)}, u32[]{:S(2)}, u32[]{:S(2)}) %collective-permute-start.7) | collective-permute-done | bytes 688160 | tf_op jit(solution)/shard_map/ppermute | solution.py:26
  52.0 5.9 %collective-permute-done.6.refs_1_ = bf16[3,64,1792]{2,1,0:T(8,128)(2,1)S(1)} collective-permute-done((bf16[3,64,1792]{2,1,0:T(8,128)(2,1)S(1)}, bf16[3,64,1792]{2,1,0:T(8,128)(2,1)S(1)}, u32[]{:S(2)}, u32[]{:S(2)}) %collective-permute-start.6) | collective-permute-done | bytes 688160 | tf_op jit(solution)/shard_map/ppermute | solution.py:26
  57.9 1.5 %collective-permute-done.8.refs_4_ = bf16[3,64,1792]{2,1,0:T(8,128)(2,1)S(1)} collective-permute-done((bf16[3,64,1792]{2,1,0:T(8,128)(2,1)S(1)}, bf16[3,64,1792]{2,1,0:T(8,128)(2,1)S(1)}, u32[]{:S(2)}, u32[]{:S(2)}) %collective-permute-start.8) | collective-permute-done | bytes 688160 | tf_op jit(solution)/shard_map/ppermute | solution.py:26
  59.4 1.7 %shard_map.90 = (bf16[3,32,1792]{2,1,0:T(8,128)(2,1)S(1)}, bf16[3,32,1792]{2,1,0:T(8,128)(2,1)S(1)}, bf16[3,32,1792]{2,1,0:T(8,128)(2,1)S(1)}, bf16[3,32,1792]{2,1,0:T(8,128)(2,1)S(1)}) custom-call(s32[2]{0:T(128)S(1)} %pad_add_fusion.place, bf16[3,64,1792]{2,1,0:T(8,128)(2,1)S(1)} %get-tuple-element.69.refs_0_, ...), custom_call_target="tpu_custom_call" | custom-call | bytes 4128776 | tf_op jit(solution)/shard_map/pallas_call | solution.py:56
  61.0 1.7 %collective-permute-start.10 = (bf16[3,32,1792]{2,1,0:T(8,128)(2,1)S(1)}, bf16[3,32,1792]{2,1,0:T(8,128)(2,1)S(1)}, u32[]{:S(2)}, u32[]{:S(2)}) collective-permute-start(bf16[3,32,1792]{2,1,0:T(8,128)(2,1)S(1)} %get-tuple-element.82), channel_id=1, source_target_pairs={{0,4},{1,5},{2,6},{3,7},{4,8},{5,9},{6,10},{7,11},{8,12},{9,13},{1... | collective-permute-start | bytes 1032200 | tf_op jit(solution)/shard_map/ppermute | solution.py:26
  62.7 2.9 %collective-permute-start.11 = (bf16[3,32,1792]{2,1,0:T(8,128)(2,1)S(1)}, bf16[3,32,1792]{2,1,0:T(8,128)(2,1)S(1)}, u32[]{:S(2)}, u32[]{:S(2)}) collective-permute-start(bf16[3,32,1792]{2,1,0:T(8,128)(2,1)S(1)} %get-tuple-element.83), channel_id=1, source_target_pairs={{0,8},{1,9},{2,10},{3,11},{4,12},{5,13},{6,14},{7,15},{8,0},{9,1},... | collective-permute-start | bytes 1032200 | tf_op jit(solution)/shard_map/ppermute | solution.py:26
  65.6 1.3 collective-permute-start.12
  67.0 2.6 %collective-permute-done.10.one = bf16[3,32,1792]{2,1,0:T(8,128)(2,1)S(1)} collective-permute-done((bf16[3,32,1792]{2,1,0:T(8,128)(2,1)S(1)}, bf16[3,32,1792]{2,1,0:T(8,128)(2,1)S(1)}, u32[]{:S(2)}, u32[]{:S(2)}) %collective-permute-start.10) | collective-permute-done | bytes 344096 | tf_op jit(solution)/shard_map/ppermute | solution.py:26
  69.6 4.9 %collective-permute-done.11.two = bf16[3,32,1792]{2,1,0:T(8,128)(2,1)S(1)} collective-permute-done((bf16[3,32,1792]{2,1,0:T(8,128)(2,1)S(1)}, bf16[3,32,1792]{2,1,0:T(8,128)(2,1)S(1)}, u32[]{:S(2)}, u32[]{:S(2)}) %collective-permute-start.11) | collective-permute-done | bytes 344096 | tf_op jit(solution)/shard_map/ppermute | solution.py:26
  74.8 1.7 %collective-permute-start.13 = (bf16[3,32,1792]{2,1,0:T(8,128)(2,1)S(1)}, bf16[3,32,1792]{2,1,0:T(8,128)(2,1)S(1)}, u32[]{:S(2)}, u32[]{:S(2)}) collective-permute-start(bf16[3,32,1792]{2,1,0:T(8,128)(2,1)S(1)} %shard_map.91.refs_0_), channel_id=1, source_target_pairs={{0,4},{1,5},{2,6},{3,7},{4,8},{5,9},{6,10},{7,11},{8,12},{9,13},{1... | collective-permute-start | bytes 1032200 | tf_op jit(solution)/shard_map/ppermute | solution.py:26
  76.5 2.1 %collective-permute-start.14 = (bf16[3,32,1792]{2,1,0:T(8,128)(2,1)S(1)}, bf16[3,32,1792]{2,1,0:T(8,128)(2,1)S(1)}, u32[]{:S(2)}, u32[]{:S(2)}) collective-permute-start(bf16[3,32,1792]{2,1,0:T(8,128)(2,1)S(1)} %shard_map.91.refs_0_), channel_id=1, source_target_pairs={{0,8},{1,9},{2,10},{3,11},{4,12},{5,13},{6,14},{7,15},{8,0},{9,1},... | collective-permute-start | bytes 1032200 | tf_op jit(solution)/shard_map/ppermute | solution.py:26
  78.6 1.7 %collective-permute-start.15 = (bf16[3,32,1792]{2,1,0:T(8,128)(2,1)S(1)}, bf16[3,32,1792]{2,1,0:T(8,128)(2,1)S(1)}, u32[]{:S(2)}, u32[]{:S(2)}) collective-permute-start(bf16[3,32,1792]{2,1,0:T(8,128)(2,1)S(1)} %shard_map.91.refs_0_), channel_id=1, source_target_pairs={{0,12},{1,13},{2,14},{3,15},{4,0},{5,1},{6,2},{7,3},{8,4},{9,5},{1... | collective-permute-start | bytes 1032200 | tf_op jit(solution)/shard_map/ppermute | solution.py:26
  80.3 3.0 %collective-permute-done.13.refs_1_ = bf16[3,32,1792]{2,1,0:T(8,128)(2,1)S(1)} collective-permute-done((bf16[3,32,1792]{2,1,0:T(8,128)(2,1)S(1)}, bf16[3,32,1792]{2,1,0:T(8,128)(2,1)S(1)}, u32[]{:S(2)}, u32[]{:S(2)}) %collective-permute-start.13) | collective-permute-done | bytes 344096 | tf_op jit(solution)/shard_map/ppermute | solution.py:26
  83.3 4.2 %collective-permute-done.14.refs_2_ = bf16[3,32,1792]{2,1,0:T(8,128)(2,1)S(1)} collective-permute-done((bf16[3,32,1792]{2,1,0:T(8,128)(2,1)S(1)}, bf16[3,32,1792]{2,1,0:T(8,128)(2,1)S(1)}, u32[]{:S(2)}, u32[]{:S(2)}) %collective-permute-start.14) | collective-permute-done | bytes 344096 | tf_op jit(solution)/shard_map/ppermute | solution.py:26
  87.5 0.4 collective-permute-done.15.refs_3_
  88.0 1.3 collective-permute-start.16
  89.3 0.8 collective-permute-start.17
  90.1 6.5 %collective-permute-done.16.refs_2_ = bf16[2,64,1792]{2,1,0:T(8,128)(2,1)S(1)} collective-permute-done((bf16[2,64,1792]{2,1,0:T(8,128)(2,1)S(1)}, bf16[2,64,1792]{2,1,0:T(8,128)(2,1)S(1)}, u32[]{:S(2)}, u32[]{:S(2)}) %collective-permute-start.16) | collective-permute-done | bytes 458784 | tf_op jit(solution)/shard_map/ppermute | solution.py:26
  96.5 1.2 collective-permute-done.17.refs_5_
  97.7 1.7 %collective-permute-start.18 = (bf16[2,64,1792]{2,1,0:T(8,128)(2,1)S(1)}, bf16[2,64,1792]{2,1,0:T(8,128)(2,1)S(1)}, u32[]{:S(2)}, u32[]{:S(2)}) collective-permute-start(bf16[2,64,1792]{2,1,0:T(8,128)(2,1)S(1)} %get-tuple-element.88.refs_1_), channel_id=1, source_target_pairs={{0,1},{1,2},{2,3},{3,0},{4,5},{5,6},{6,7},{7,4},{8,9},{9,10},{10,1... | collective-permute-start | bytes 1376264 | tf_op jit(solution)/shard_map/ppermute | solution.py:26
  99.8 1.7 %collective-permute-start.20 = (bf16[2,64,1792]{2,1,0:T(8,128)(2,1)S(1)}, bf16[2,64,1792]{2,1,0:T(8,128)(2,1)S(1)}, u32[]{:S(2)}, u32[]{:S(2)}) collective-permute-start(bf16[2,64,1792]{2,1,0:T(8,128)(2,1)S(1)} %collective-permute-done.16.refs_2_), channel_id=1, source_target_pairs={{0,1},{1,2},{2,3},{3,0},{4,5},{5,6},{6,7},{7,4},{8,9},{9,10},{10,1... | collective-permute-start | bytes 1376264 | tf_op jit(solution)/shard_map/ppermute | solution.py:26
  101.8 4.4 %collective-permute-done.18.refs_3_ = bf16[2,64,1792]{2,1,0:T(8,128)(2,1)S(1)} collective-permute-done((bf16[2,64,1792]{2,1,0:T(8,128)(2,1)S(1)}, bf16[2,64,1792]{2,1,0:T(8,128)(2,1)S(1)}, u32[]{:S(2)}, u32[]{:S(2)}) %collective-permute-start.18) | collective-permute-done | bytes 458784 | tf_op jit(solution)/shard_map/ppermute | solution.py:26
  106.2 1.7 %collective-permute-done.19.refs_4_ = bf16[2,64,1792]{2,1,0:T(8,128)(2,1)S(1)} collective-permute-done((bf16[2,64,1792]{2,1,0:T(8,128)(2,1)S(1)}, bf16[2,64,1792]{2,1,0:T(8,128)(2,1)S(1)}, u32[]{:S(2)}, u32[]{:S(2)}) %collective-permute-start.19) | collective-permute-done | bytes 458784 | tf_op jit(solution)/shard_map/ppermute | solution.py:26
  107.9 1.5 %collective-permute-start.23 = (bf16[128,1792]{1,0:T(8,128)(2,1)S(1)}, bf16[128,1792]{1,0:T(8,128)(2,1)S(1)}, u32[]{:S(2)}, u32[]{:S(2)}) collective-permute-start(bf16[128,1792]{1,0:T(8,128)(2,1)S(1)} %get-tuple-element.118.refs_0_), channel_id=1, source_target_pairs={{0,1},{1,2},{2,3},{3,0},{4,5},{5,6},{6,7},{7,4},{8,9},{9,10},{10,1... | collective-permute-start | bytes 1376264 | tf_op jit(solution)/shard_map/ppermute | solution.py:26
  109.4 0.5 collective-permute-start.24
  109.9 2.4 %collective-permute-start.25 = (bf16[128,1792]{1,0:T(8,128)(2,1)S(1)}, bf16[128,1792]{1,0:T(8,128)(2,1)S(1)}, u32[]{:S(2)}, u32[]{:S(2)}) collective-permute-start(bf16[128,1792]{1,0:T(8,128)(2,1)S(1)} %get-tuple-element.118.refs_0_), channel_id=1, source_target_pairs={{0,2},{1,3},{2,0},{3,1},{4,6},{5,7},{6,4},{7,5},{8,10},{9,11},{10,... | collective-permute-start | bytes 1376264 | tf_op jit(solution)/shard_map/ppermute | solution.py:26
  112.4 0.5 collective-permute-done.21.refs_7_
  112.8 1.8 %shard_map.93 = (bf16[256,512]{1,0:T(8,128)(2,1)S(1)}, bf16[512,1792]{1,0:T(8,128)(2,1)S(1)}, bf16[512,1792]{1,0:T(8,128)(2,1)S(1)}) custom-call(s32[2]{0:T(128)S(1)} %pad_add_fusion.place, bf16[512,1792]{1,0:T(8,128)(2,1)S(1)} %copy-done.1, bf16[512,1792]{1,0:T(8,128)(2,1)S(1)} %copy-done.3, bf16[2,64,1792]{2,1,0:T(8,128)(2,1)S(1)} %get-tuple-element.87.refs_0_, ...), custom_call_target="tpu_custom_call" | custom-call | flops 939524096 | bytes 7340040 | tf_op jit(solution)/shard_map/pallas_call | solution.py:56
  114.7 3.8 %collective-permute-start.22 = (bf16[256,512]{1,0:T(8,128)(2,1)S(1)}, bf16[256,512]{1,0:T(8,128)(2,1)S(1)}, u32[]{:S(2)}, u32[]{:S(2)}) collective-permute-start(bf16[256,512]{1,0:T(8,128)(2,1)S(1)} %get-tuple-element.94), channel_id=1, source_target_pairs={{0,16},{16,0},{32,48},{48,32},{64,80},{80,64},{96,112},{112,96},{1... | collective-permute-start | bytes 786440 | tf_op jit(solution)/shard_map/ppermute | solution.py:44
  118.4 1.1 shard_map.94.keep
  119.6 2.1 %shard_map.95 = (bf16[512,1792]{1,0:T(8,128)(2,1)S(1)}, bf16[512,1792]{1,0:T(8,128)(2,1)S(1)}) custom-call(bf16[256,1024]{1,0:T(8,128)(2,1)S(1)} %shard_map.85.act.low, bf16[256,1024]{1,0:T(8,128)(2,1)S(1)} %collective-permute-done.3.act.high, bf16[512,1792]{1,0:T(8,128)(2,1)S(1)} %get-tuple-element.95.gg, bf16[512,1792]{1,0:T(8,128)(2,1)S(1)} %get-tuple-element.96.ug), custom_call_target="tpu_custom_call" | custom-call | flops 1879048192 | bytes 4718592 | tf_op jit(solution)/shard_map/pallas_call | solution.py:56
  121.7 1.1 collective-permute-done.22.got
  122.8 0.5 collective-permute-start.29
  123.7 1.8 %shard_map.100.mine = bf16[1792,512]{1,0:T(8,128)(2,1)S(1)} custom-call(s32[2]{0:T(128)S(1)} %pad_add_fusion.place, bf16[256,1024]{1,0:T(8,128)(2,1)S(1)} %shard_map.85.act.low, bf16[256,1024]{1,0:T(8,128)(2,1)S(1)} %collective-permute-done.3.act.high, bf16[128,1792]{1,0:T(8,128)(2,1)S(1)} %get-tuple-element.118.refs_0_, ...), custom_call_target="tpu_custom_call" | custom-call | flops 939524096 | bytes 2883592 | tf_op jit(solution)/shard_map/pallas_call | solution.py:56
  125.7 1.1 collective-permute-start.26
  126.8 5.2 %collective-permute-start.27 = (bf16[64,512]{1,0:T(8,128)(2,1)S(1)}, bf16[64,512]{1,0:T(8,128)(2,1)S(1)}, u32[]{:S(2)}, u32[]{:S(2)}) collective-permute-start(bf16[64,512]{1,0:T(8,128)(2,1)S(1)} %get-tuple-element.108), channel_id=1, source_target_pairs={{0,64},{16,80},{32,96},{48,112},{64,0},{80,16},{96,32},{112,48},{1... | collective-permute-start | bytes 196616 | tf_op jit(solution)/shard_map/ppermute | solution.py:35
  132.0 1.3 collective-permute-start.28
  133.3 1.3 shard_map.98
  134.6 1.3 shard_map.97
  136.0 2.8 %collective-permute-done.28.refs_3_ = bf16[64,512]{1,0:T(8,128)(2,1)S(1)} collective-permute-done((bf16[64,512]{1,0:T(8,128)(2,1)S(1)}, bf16[64,512]{1,0:T(8,128)(2,1)S(1)}, u32[]{:S(2)}, u32[]{:S(2)}) %collective-permute-start.28) | collective-permute-done | bytes 65568 | tf_op jit(solution)/shard_map/ppermute | solution.py:35
  138.8 0.7 shard_map.99
  139.5 1.3 shard_map.101
  (35 shorter events, 2.0 us)
Async XLA Ops:
  0.6 0.8 copy-start.6
  1.5 0.8 copy-start.7
  2.3 16.2 %collective-permute-start = (bf16[64,1024]{1,0:T(8,128)(2,1)S(1)}, bf16[64,1024]{1,0:T(8,128)(2,1)S(1)}, u32[]{:S(2)}, u32[]{:S(2)}) collective-permute-start(bf16[64,1024]{1,0:T(8,128)(2,1)S(1)} %shard_map.84.refs_0_), channel_id=1, source_target_pairs={{0,96},{16,112},{32,0},{48,16},{64,32},{80,48},{96,64},{112,80},{1... | collective-permute-start | bytes 393224 | tf_op jit(solution)/shard_map/ppermute | solution.py:35
  8.7 11.1 %collective-permute-start.1 = (bf16[64,1024]{1,0:T(8,128)(2,1)S(1)}, bf16[64,1024]{1,0:T(8,128)(2,1)S(1)}, u32[]{:S(2)}, u32[]{:S(2)}) collective-permute-start(bf16[64,1024]{1,0:T(8,128)(2,1)S(1)} %shard_map.84.refs_0_), channel_id=1, source_target_pairs={{0,64},{16,80},{32,96},{48,112},{64,0},{80,16},{96,32},{112,48},{1... | collective-permute-start | bytes 393224 | tf_op jit(solution)/shard_map/ppermute | solution.py:35
  9.7 10.1 %collective-permute-start.2 = (bf16[64,1024]{1,0:T(8,128)(2,1)S(1)}, bf16[64,1024]{1,0:T(8,128)(2,1)S(1)}, u32[]{:S(2)}, u32[]{:S(2)}) collective-permute-start(bf16[64,1024]{1,0:T(8,128)(2,1)S(1)} %shard_map.84.refs_0_), channel_id=1, source_target_pairs={{0,32},{16,48},{32,64},{48,80},{64,96},{80,112},{96,0},{112,16},{1... | collective-permute-start | bytes 393224 | tf_op jit(solution)/shard_map/ppermute | solution.py:35
  19.8 10.5 %collective-permute-start.3 = (bf16[256,1024]{1,0:T(8,128)(2,1)S(1)}, bf16[256,1024]{1,0:T(8,128)(2,1)S(1)}, u32[]{:S(2)}, u32[]{:S(2)}) collective-permute-start(bf16[256,1024]{1,0:T(8,128)(2,1)S(1)} %shard_map.85.act.low), channel_id=1, source_target_pairs={{0,16},{16,0},{32,48},{48,32},{64,80},{80,64},{96,112},{112,96},{1... | collective-permute-start | bytes 1572872 | tf_op jit(solution)/shard_map/ppermute | solution.py:44
  23.2 1.5 %copy-start = (bf16[512,1792]{1,0:T(8,128)(2,1)S(1)}, bf16[512,1792]{1,0:T(8,128)(2,1)}, u32[]{:S(2)}) copy-start(bf16[512,1792]{1,0:T(8,128)(2,1)} %gate.9) | copy-start | bytes 5505028
  24.7 1.5 %copy-start.2 = (bf16[512,1792]{1,0:T(8,128)(2,1)S(1)}, bf16[512,1792]{1,0:T(8,128)(2,1)}, u32[]{:S(2)}) copy-start(bf16[512,1792]{1,0:T(8,128)(2,1)} %up.9) | copy-start | bytes 5505028
  26.2 1.5 %copy-start.4 = (bf16[1792,512]{1,0:T(8,128)(2,1)S(1)}, bf16[1792,512]{1,0:T(8,128)(2,1)}, u32[]{:S(2)}) copy-start(bf16[1792,512]{1,0:T(8,128)(2,1)} %down.5) | copy-start | bytes 5505028
  27.7 2.6 %copy-start.1 = (bf16[512,1792]{1,0:T(8,128)(2,1)S(1)}, bf16[512,1792]{1,0:T(8,128)(2,1)}, u32[]{:S(2)}) copy-start(bf16[512,1792]{1,0:T(8,128)(2,1)} %gate.9) | copy-start | bytes 5505028
  27.7 2.6 %copy-start.3 = (bf16[512,1792]{1,0:T(8,128)(2,1)S(1)}, bf16[512,1792]{1,0:T(8,128)(2,1)}, u32[]{:S(2)}) copy-start(bf16[512,1792]{1,0:T(8,128)(2,1)} %up.9) | copy-start | bytes 5505028
  27.7 2.6 %copy-start.5 = (bf16[1792,512]{1,0:T(8,128)(2,1)S(1)}, bf16[1792,512]{1,0:T(8,128)(2,1)}, u32[]{:S(2)}) copy-start(bf16[1792,512]{1,0:T(8,128)(2,1)} %down.5) | copy-start | bytes 5505028
  32.1 11.0 %collective-permute-start.4 = (bf16[3,64,1792]{2,1,0:T(8,128)(2,1)S(1)}, bf16[3,64,1792]{2,1,0:T(8,128)(2,1)S(1)}, u32[]{:S(2)}, u32[]{:S(2)}) collective-permute-start(bf16[3,64,1792]{2,1,0:T(8,128)(2,1)S(1)} %get-tuple-element.74), channel_id=1, source_target_pairs={{0,1},{1,2},{2,3},{3,0},{4,5},{5,6},{6,7},{7,4},{8,9},{9,10},{10,1... | collective-permute-start | bytes 2064392 | tf_op jit(solution)/shard_map/ppermute | solution.py:26
  33.7 10.9 %collective-permute-start.5 = (bf16[3,64,1792]{2,1,0:T(8,128)(2,1)S(1)}, bf16[3,64,1792]{2,1,0:T(8,128)(2,1)S(1)}, u32[]{:S(2)}, u32[]{:S(2)}) collective-permute-start(bf16[3,64,1792]{2,1,0:T(8,128)(2,1)S(1)} %get-tuple-element.75), channel_id=1, source_target_pairs={{0,3},{1,0},{2,1},{3,2},{4,7},{5,4},{6,5},{7,6},{8,11},{9,8},{10,9... | collective-permute-start | bytes 2064392 | tf_op jit(solution)/shard_map/ppermute | solution.py:26
  36.3 15.7 %collective-permute-start.7 = (bf16[3,64,1792]{2,1,0:T(8,128)(2,1)S(1)}, bf16[3,64,1792]{2,1,0:T(8,128)(2,1)S(1)}, u32[]{:S(2)}, u32[]{:S(2)}) collective-permute-start(bf16[3,64,1792]{2,1,0:T(8,128)(2,1)S(1)} %get-tuple-element.77), channel_id=1, source_target_pairs={{0,3},{1,0},{2,1},{3,2},{4,7},{5,4},{6,5},{7,6},{8,11},{9,8},{10,9... | collective-permute-start | bytes 2064392 | tf_op jit(solution)/shard_map/ppermute | solution.py:26
  38.5 13.5 %collective-permute-start.9 = (bf16[3,64,1792]{2,1,0:T(8,128)(2,1)S(1)}, bf16[3,64,1792]{2,1,0:T(8,128)(2,1)S(1)}, u32[]{:S(2)}, u32[]{:S(2)}) collective-permute-start(bf16[3,64,1792]{2,1,0:T(8,128)(2,1)S(1)} %get-tuple-element.80), channel_id=1, source_target_pairs={{0,1},{1,2},{2,3},{3,0},{4,5},{5,6},{6,7},{7,4},{8,9},{9,10},{10,1... | collective-permute-start | bytes 2064392 | tf_op jit(solution)/shard_map/ppermute | solution.py:26
  44.9 12.9 %collective-permute-start.6 = (bf16[3,64,1792]{2,1,0:T(8,128)(2,1)S(1)}, bf16[3,64,1792]{2,1,0:T(8,128)(2,1)S(1)}, u32[]{:S(2)}, u32[]{:S(2)}) collective-permute-start(bf16[3,64,1792]{2,1,0:T(8,128)(2,1)S(1)} %get-tuple-element.76), channel_id=1, source_target_pairs={{0,1},{1,2},{2,3},{3,0},{4,5},{5,6},{6,7},{7,4},{8,9},{9,10},{10,1... | collective-permute-start | bytes 2064392 | tf_op jit(solution)/shard_map/ppermute | solution.py:26
  46.2 13.2 %collective-permute-start.8 = (bf16[3,64,1792]{2,1,0:T(8,128)(2,1)S(1)}, bf16[3,64,1792]{2,1,0:T(8,128)(2,1)S(1)}, u32[]{:S(2)}, u32[]{:S(2)}) collective-permute-start(bf16[3,64,1792]{2,1,0:T(8,128)(2,1)S(1)} %get-tuple-element.79), channel_id=1, source_target_pairs={{0,3},{1,0},{2,1},{3,2},{4,7},{5,4},{6,5},{7,6},{8,11},{9,8},{10,9... | collective-permute-start | bytes 2064392 | tf_op jit(solution)/shard_map/ppermute | solution.py:26
  61.0 8.5 %collective-permute-start.10 = (bf16[3,32,1792]{2,1,0:T(8,128)(2,1)S(1)}, bf16[3,32,1792]{2,1,0:T(8,128)(2,1)S(1)}, u32[]{:S(2)}, u32[]{:S(2)}) collective-permute-start(bf16[3,32,1792]{2,1,0:T(8,128)(2,1)S(1)} %get-tuple-element.82), channel_id=1, source_target_pairs={{0,4},{1,5},{2,6},{3,7},{4,8},{5,9},{6,10},{7,11},{8,12},{9,13},{1... | collective-permute-start | bytes 1032200 | tf_op jit(solution)/shard_map/ppermute | solution.py:26
  62.7 11.8 %collective-permute-start.11 = (bf16[3,32,1792]{2,1,0:T(8,128)(2,1)S(1)}, bf16[3,32,1792]{2,1,0:T(8,128)(2,1)S(1)}, u32[]{:S(2)}, u32[]{:S(2)}) collective-permute-start(bf16[3,32,1792]{2,1,0:T(8,128)(2,1)S(1)} %get-tuple-element.83), channel_id=1, source_target_pairs={{0,8},{1,9},{2,10},{3,11},{4,12},{5,13},{6,14},{7,15},{8,0},{9,1},... | collective-permute-start | bytes 1032200 | tf_op jit(solution)/shard_map/ppermute | solution.py:26
  65.6 8.9 %collective-permute-start.12 = (bf16[3,32,1792]{2,1,0:T(8,128)(2,1)S(1)}, bf16[3,32,1792]{2,1,0:T(8,128)(2,1)S(1)}, u32[]{:S(2)}, u32[]{:S(2)}) collective-permute-start(bf16[3,32,1792]{2,1,0:T(8,128)(2,1)S(1)} %get-tuple-element.84), channel_id=1, source_target_pairs={{0,12},{1,13},{2,14},{3,15},{4,0},{5,1},{6,2},{7,3},{8,4},{9,5},{1... | collective-permute-start | bytes 1032200 | tf_op jit(solution)/shard_map/ppermute | solution.py:26
  74.8 8.5 %collective-permute-start.13 = (bf16[3,32,1792]{2,1,0:T(8,128)(2,1)S(1)}, bf16[3,32,1792]{2,1,0:T(8,128)(2,1)S(1)}, u32[]{:S(2)}, u32[]{:S(2)}) collective-permute-start(bf16[3,32,1792]{2,1,0:T(8,128)(2,1)S(1)} %shard_map.91.refs_0_), channel_id=1, source_target_pairs={{0,4},{1,5},{2,6},{3,7},{4,8},{5,9},{6,10},{7,11},{8,12},{9,13},{1... | collective-permute-start | bytes 1032200 | tf_op jit(solution)/shard_map/ppermute | solution.py:26
  76.5 11.0 %collective-permute-start.14 = (bf16[3,32,1792]{2,1,0:T(8,128)(2,1)S(1)}, bf16[3,32,1792]{2,1,0:T(8,128)(2,1)S(1)}, u32[]{:S(2)}, u32[]{:S(2)}) collective-permute-start(bf16[3,32,1792]{2,1,0:T(8,128)(2,1)S(1)} %shard_map.91.refs_0_), channel_id=1, source_target_pairs={{0,8},{1,9},{2,10},{3,11},{4,12},{5,13},{6,14},{7,15},{8,0},{9,1},... | collective-permute-start | bytes 1032200 | tf_op jit(solution)/shard_map/ppermute | solution.py:26
  78.6 9.3 %collective-permute-start.15 = (bf16[3,32,1792]{2,1,0:T(8,128)(2,1)S(1)}, bf16[3,32,1792]{2,1,0:T(8,128)(2,1)S(1)}, u32[]{:S(2)}, u32[]{:S(2)}) collective-permute-start(bf16[3,32,1792]{2,1,0:T(8,128)(2,1)S(1)} %shard_map.91.refs_0_), channel_id=1, source_target_pairs={{0,12},{1,13},{2,14},{3,15},{4,0},{5,1},{6,2},{7,3},{8,4},{9,5},{1... | collective-permute-start | bytes 1032200 | tf_op jit(solution)/shard_map/ppermute | solution.py:26
  88.0 8.6 %collective-permute-start.16 = (bf16[2,64,1792]{2,1,0:T(8,128)(2,1)S(1)}, bf16[2,64,1792]{2,1,0:T(8,128)(2,1)S(1)}, u32[]{:S(2)}, u32[]{:S(2)}) collective-permute-start(bf16[2,64,1792]{2,1,0:T(8,128)(2,1)S(1)} %get-tuple-element.87.refs_0_), channel_id=1, source_target_pairs={{0,1},{1,2},{2,3},{3,0},{4,5},{5,6},{6,7},{7,4},{8,9},{9,10},{10,1... | collective-permute-start | bytes 1376264 | tf_op jit(solution)/shard_map/ppermute | solution.py:26
  89.3 8.5 %collective-permute-start.17 = (bf16[2,64,1792]{2,1,0:T(8,128)(2,1)S(1)}, bf16[2,64,1792]{2,1,0:T(8,128)(2,1)S(1)}, u32[]{:S(2)}, u32[]{:S(2)}) collective-permute-start(bf16[2,64,1792]{2,1,0:T(8,128)(2,1)S(1)} %get-tuple-element.88.refs_1_), channel_id=1, source_target_pairs={{0,3},{1,0},{2,1},{3,2},{4,7},{5,4},{6,5},{7,6},{8,11},{9,8},{10,9... | collective-permute-start | bytes 1376264 | tf_op jit(solution)/shard_map/ppermute | solution.py:26
  97.7 8.5 %collective-permute-start.18 = (bf16[2,64,1792]{2,1,0:T(8,128)(2,1)S(1)}, bf16[2,64,1792]{2,1,0:T(8,128)(2,1)S(1)}, u32[]{:S(2)}, u32[]{:S(2)}) collective-permute-start(bf16[2,64,1792]{2,1,0:T(8,128)(2,1)S(1)} %get-tuple-element.88.refs_1_), channel_id=1, source_target_pairs={{0,1},{1,2},{2,3},{3,0},{4,5},{5,6},{6,7},{7,4},{8,9},{9,10},{10,1... | collective-permute-start | bytes 1376264 | tf_op jit(solution)/shard_map/ppermute | solution.py:26
  99.4 8.5 %collective-permute-start.19 = (bf16[2,64,1792]{2,1,0:T(8,128)(2,1)S(1)}, bf16[2,64,1792]{2,1,0:T(8,128)(2,1)S(1)}, u32[]{:S(2)}, u32[]{:S(2)}) collective-permute-start(bf16[2,64,1792]{2,1,0:T(8,128)(2,1)S(1)} %get-tuple-element.87.refs_0_), channel_id=1, source_target_pairs={{0,3},{1,0},{2,1},{3,2},{4,7},{5,4},{6,5},{7,6},{8,11},{9,8},{10,9... | collective-permute-start | bytes 1376264 | tf_op jit(solution)/shard_map/ppermute | solution.py:26
  99.8 12.6 %collective-permute-start.20 = (bf16[2,64,1792]{2,1,0:T(8,128)(2,1)S(1)}, bf16[2,64,1792]{2,1,0:T(8,128)(2,1)S(1)}, u32[]{:S(2)}, u32[]{:S(2)}) collective-permute-start(bf16[2,64,1792]{2,1,0:T(8,128)(2,1)S(1)} %collective-permute-done.16.refs_2_), channel_id=1, source_target_pairs={{0,1},{1,2},{2,3},{3,0},{4,5},{5,6},{6,7},{7,4},{8,9},{9,10},{10,1... | collective-permute-start | bytes 1376264 | tf_op jit(solution)/shard_map/ppermute | solution.py:26
  101.5 11.4 %collective-permute-start.21 = (bf16[2,64,1792]{2,1,0:T(8,128)(2,1)S(1)}, bf16[2,64,1792]{2,1,0:T(8,128)(2,1)S(1)}, u32[]{:S(2)}, u32[]{:S(2)}) collective-permute-start(bf16[2,64,1792]{2,1,0:T(8,128)(2,1)S(1)} %collective-permute-done.17.refs_5_), channel_id=1, source_target_pairs={{0,3},{1,0},{2,1},{3,2},{4,7},{5,4},{6,5},{7,6},{8,11},{9,8},{10,9... | collective-permute-start | bytes 1376264 | tf_op jit(solution)/shard_map/ppermute | solution.py:26
  107.9 15.4 %collective-permute-start.23 = (bf16[128,1792]{1,0:T(8,128)(2,1)S(1)}, bf16[128,1792]{1,0:T(8,128)(2,1)S(1)}, u32[]{:S(2)}, u32[]{:S(2)}) collective-permute-start(bf16[128,1792]{1,0:T(8,128)(2,1)S(1)} %get-tuple-element.118.refs_0_), channel_id=1, source_target_pairs={{0,1},{1,2},{2,3},{3,0},{4,5},{5,6},{6,7},{7,4},{8,9},{9,10},{10,1... | collective-permute-start | bytes 1376264 | tf_op jit(solution)/shard_map/ppermute | solution.py:26
  109.4 14.0 %collective-permute-start.24 = (bf16[128,1792]{1,0:T(8,128)(2,1)S(1)}, bf16[128,1792]{1,0:T(8,128)(2,1)S(1)}, u32[]{:S(2)}, u32[]{:S(2)}) collective-permute-start(bf16[128,1792]{1,0:T(8,128)(2,1)S(1)} %get-tuple-element.118.refs_0_), channel_id=1, source_target_pairs={{0,3},{1,0},{2,1},{3,2},{4,7},{5,4},{6,5},{7,6},{8,11},{9,8},{10,9... | collective-permute-start | bytes 1376264 | tf_op jit(solution)/shard_map/ppermute | solution.py:26
  109.9 13.8 %collective-permute-start.25 = (bf16[128,1792]{1,0:T(8,128)(2,1)S(1)}, bf16[128,1792]{1,0:T(8,128)(2,1)S(1)}, u32[]{:S(2)}, u32[]{:S(2)}) collective-permute-start(bf16[128,1792]{1,0:T(8,128)(2,1)S(1)} %get-tuple-element.118.refs_0_), channel_id=1, source_target_pairs={{0,2},{1,3},{2,0},{3,1},{4,6},{5,7},{6,4},{7,5},{8,10},{9,11},{10,... | collective-permute-start | bytes 1376264 | tf_op jit(solution)/shard_map/ppermute | solution.py:26
  114.7 8.1 %collective-permute-start.22 = (bf16[256,512]{1,0:T(8,128)(2,1)S(1)}, bf16[256,512]{1,0:T(8,128)(2,1)S(1)}, u32[]{:S(2)}, u32[]{:S(2)}) collective-permute-start(bf16[256,512]{1,0:T(8,128)(2,1)S(1)} %get-tuple-element.94), channel_id=1, source_target_pairs={{0,16},{16,0},{32,48},{48,32},{64,80},{80,64},{96,112},{112,96},{1... | collective-permute-start | bytes 786440 | tf_op jit(solution)/shard_map/ppermute | solution.py:44
  122.8 9.2 %collective-permute-start.30 = (bf16[512,1792]{1,0:T(8,128)(2,1)S(1)}, bf16[512,1792]{1,0:T(8,128)(2,1)S(1)}, u32[]{:S(2)}, u32[]{:S(2)}) collective-permute-start(bf16[512,1792]{1,0:T(8,128)(2,1)S(1)} %get-tuple-element.111.mine), channel_id=1, source_target_pairs={{0,128},{128,0},{1,129},{129,1},{2,130},{130,2},{3,131},{131,3},{4... | collective-permute-start | bytes 5505032 | tf_op jit(solution)/shard_map/ppermute | solution.py:48
  122.8 11.8 %collective-permute-start.29 = (bf16[512,1792]{1,0:T(8,128)(2,1)S(1)}, bf16[512,1792]{1,0:T(8,128)(2,1)S(1)}, u32[]{:S(2)}, u32[]{:S(2)}) collective-permute-start(bf16[512,1792]{1,0:T(8,128)(2,1)S(1)} %get-tuple-element.110.mine), channel_id=1, source_target_pairs={{0,128},{128,0},{1,129},{129,1},{2,130},{130,2},{3,131},{131,3},{4... | collective-permute-start | bytes 5505032 | tf_op jit(solution)/shard_map/ppermute | solution.py:48
  125.6 14.0 %collective-permute-start.31 = (bf16[1792,512]{1,0:T(8,128)(2,1)S(1)}, bf16[1792,512]{1,0:T(8,128)(2,1)S(1)}, u32[]{:S(2)}, u32[]{:S(2)}) collective-permute-start(bf16[1792,512]{1,0:T(8,128)(2,1)S(1)} %shard_map.100.mine), channel_id=1, source_target_pairs={{0,128},{128,0},{1,129},{129,1},{2,130},{130,2},{3,131},{131,3},{4... | collective-permute-start | bytes 5505032 | tf_op jit(solution)/shard_map/ppermute | solution.py:48
  125.7 10.3 %collective-permute-start.26 = (bf16[64,512]{1,0:T(8,128)(2,1)S(1)}, bf16[64,512]{1,0:T(8,128)(2,1)S(1)}, u32[]{:S(2)}, u32[]{:S(2)}) collective-permute-start(bf16[64,512]{1,0:T(8,128)(2,1)S(1)} %get-tuple-element.107), channel_id=1, source_target_pairs={{0,32},{16,48},{32,64},{48,80},{64,96},{80,112},{96,0},{112,16},{1... | collective-permute-start | bytes 196616 | tf_op jit(solution)/shard_map/ppermute | solution.py:35
  126.8 9.2 %collective-permute-start.27 = (bf16[64,512]{1,0:T(8,128)(2,1)S(1)}, bf16[64,512]{1,0:T(8,128)(2,1)S(1)}, u32[]{:S(2)}, u32[]{:S(2)}) collective-permute-start(bf16[64,512]{1,0:T(8,128)(2,1)S(1)} %get-tuple-element.108), channel_id=1, source_target_pairs={{0,64},{16,80},{32,96},{48,112},{64,0},{80,16},{96,32},{112,48},{1... | collective-permute-start | bytes 196616 | tf_op jit(solution)/shard_map/ppermute | solution.py:35
  132.0 6.9 %collective-permute-start.28 = (bf16[64,512]{1,0:T(8,128)(2,1)S(1)}, bf16[64,512]{1,0:T(8,128)(2,1)S(1)}, u32[]{:S(2)}, u32[]{:S(2)}) collective-permute-start(bf16[64,512]{1,0:T(8,128)(2,1)S(1)} %get-tuple-element.109), channel_id=1, source_target_pairs={{0,96},{16,112},{32,0},{48,16},{64,32},{80,48},{96,64},{112,80},{1... | collective-permute-start | bytes 196616 | tf_op jit(solution)/shard_map/ppermute | solution.py:35

commit v3 on v2

--- a/solution.py
+++ b/solution.py
@@ -283,9 +283,8 @@
         got,
     )
     low_left, high_right = send_col(low, 0, 1), send_col(high, 0, -1)
-    low, high, low_left, high_right = lax.optimization_barrier((low, high, low_left, high_right))
+    high_left, low_right = send_col(high, 0, 1), send_col(low, 0, -1)
     low_far, high_far = send_col(low_left, 0, 1), send_col(high_right, 0, -1)
-    high_left, low_right = send_col(high, 0, 1), send_col(low, 0, -1)
     hid, high_left, low_right = lax.optimization_barrier((hid, high_left, low_right))
     pieces = (low, high, low_left, high_left, low_right, high_right, low_far, high_far)
     hids = (hid, send_col(hid, 0, 1), send_col(hid, 0, -1), send_col(hid, 0, 2))

time: 142 us -> 138 us (0.972)
  waiting for transfers between devices: 59.7 us -> 55.2 us
    ppermute x21, waiting for transfers between devices: 48.2 us -> 43.8 us  [send_col(): return lax.ppermute(value, ('dp', 'col'), pairs)]
  transfers between devices with their start and end apart: 32 -> 32, of which waited for: 21 -> 20; matrix products, arithmetic and copies ran while one was open for 0% -> 0% of each run, Pallas kernels for 11% -> 11%
where the time goes in v3:
time: 138 us; the launch traced here: 136 us
  waiting for transfers between devices  55.2 us (40%)
  starting transfers between devices  53.8 us (39%)
  Pallas kernels  20.1 us (15%)
  local copies, waits for them, and re-layouts  6.19 us (4%)
    ppermute x21, waiting for transfers between devices, send_col(): return lax.ppermute(value, ('dp', 'col'), pairs)  43.8 us
    ppermute x21, starting transfers between devices, send_col(): return lax.ppermute(value, ('dp', 'col'), pairs)  28.6 us
    ppermute x6, starting transfers between devices, send_row(): return lax.ppermute(value, ('dp', 'row'), pairs)  17.8 us
    pallas_call x15, Pallas kernels, call(): pl.pallas_call(kernel, out_shape=[jax.ShapeDtypeStruct(shape, kind) for s...  16.1 us
    ppermute x6, waiting for transfers between devices, send_row(): return lax.ppermute(value, ('dp', 'row'), pairs)  9.92 us
    ppermute x2, starting transfers between devices, swap_row(): return lax.ppermute(value, ('dp', 'row'), pairs)  6.75 us
    unnamed x16, local copies, waits for them, and re-layouts  6.19 us
    pallas_call x3, Pallas kernels, merge(): pl.pallas_call(merge_kernel, out_shape=jax.ShapeDtypeStruct(term.shape, B...  4.02 us
  transfers between devices with their start and end apart: 32, of which 20 were waited for; matrix products, arithmetic and copies ran while one was open for 0% of the time, Pallas kernels for 11%

profile of v3, /device:TPU:2, one launch (start us, length us, event | category | flops | bytes accessed | tf_op | source)
XLA Modules:
  0.0 136.3 jit_solution(15271244664649180613)
XLA Ops:
  0.6 0.8 copy-done.6
  1.5 0.8 copy-done.7
  2.3 6.4 %collective-permute-start = (bf16[64,1024]{1,0:T(8,128)(2,1)S(1)}, bf16[64,1024]{1,0:T(8,128)(2,1)S(1)}, u32[]{:S(2)}, u32[]{:S(2)}) collective-permute-start(bf16[64,1024]{1,0:T(8,128)(2,1)S(1)} %shard_map.84.refs_0_), channel_id=1, source_target_pairs={{0,96},{16,112},{32,0},{48,16},{64,32},{80,48},{96,64},{112,80},{1... | collective-permute-start | bytes 393224 | tf_op jit(solution)/shard_map/ppermute | solution.py:35
  8.7 1.0 collective-permute-start.1
  9.7 2.8 %collective-permute-start.2 = (bf16[64,1024]{1,0:T(8,128)(2,1)S(1)}, bf16[64,1024]{1,0:T(8,128)(2,1)S(1)}, u32[]{:S(2)}, u32[]{:S(2)}) collective-permute-start(bf16[64,1024]{1,0:T(8,128)(2,1)S(1)} %shard_map.84.refs_0_), channel_id=1, source_target_pairs={{0,32},{16,48},{32,64},{48,80},{64,96},{80,112},{96,0},{112,16},{1... | collective-permute-start | bytes 393224 | tf_op jit(solution)/shard_map/ppermute | solution.py:35
  12.5 6.0 %collective-permute-done.refs_1_ = bf16[64,1024]{1,0:T(8,128)(2,1)S(1)} collective-permute-done((bf16[64,1024]{1,0:T(8,128)(2,1)S(1)}, bf16[64,1024]{1,0:T(8,128)(2,1)S(1)}, u32[]{:S(2)}, u32[]{:S(2)}) %collective-permute-start) | collective-permute-done | bytes 131104 | tf_op jit(solution)/shard_map/ppermute | solution.py:35
  18.5 1.2 collective-permute-done.1.refs_2_
  19.8 3.3 %collective-permute-start.3 = (bf16[256,1024]{1,0:T(8,128)(2,1)S(1)}, bf16[256,1024]{1,0:T(8,128)(2,1)S(1)}, u32[]{:S(2)}, u32[]{:S(2)}) collective-permute-start(bf16[256,1024]{1,0:T(8,128)(2,1)S(1)} %shard_map.85.act.low), channel_id=1, source_target_pairs={{0,16},{16,0},{32,48},{48,32},{64,80},{80,64},{96,112},{112,96},{1... | collective-permute-start | bytes 1572872 | tf_op jit(solution)/shard_map/ppermute | solution.py:44
  23.2 1.5 %copy-done = bf16[512,1792]{1,0:T(8,128)(2,1)S(1)} copy-done((bf16[512,1792]{1,0:T(8,128)(2,1)S(1)}, bf16[512,1792]{1,0:T(8,128)(2,1)}, u32[]{:S(2)}) %copy-start) | copy-done | bytes 1835032
  24.7 1.5 %copy-done.2 = bf16[512,1792]{1,0:T(8,128)(2,1)S(1)} copy-done((bf16[512,1792]{1,0:T(8,128)(2,1)S(1)}, bf16[512,1792]{1,0:T(8,128)(2,1)}, u32[]{:S(2)}) %copy-start.2) | copy-done | bytes 1835032
  26.2 1.5 %copy-done.4 = bf16[1792,512]{1,0:T(8,128)(2,1)S(1)} copy-done((bf16[1792,512]{1,0:T(8,128)(2,1)S(1)}, bf16[1792,512]{1,0:T(8,128)(2,1)}, u32[]{:S(2)}) %copy-start.4) | copy-done | bytes 1835032
  27.7 2.1 %shard_map.86 = (bf16[3,32,1792]{2,1,0:T(8,128)(2,1)S(1)}, bf16[3,32,1792]{2,1,0:T(8,128)(2,1)S(1)}, bf16[3,32,1792]{2,1,0:T(8,128)(2,1)S(1)}, bf16[3,32,1792]{2...) custom-call(s32[2]{0:T(128)S(1)} %pad_add_fusion.place, ...), custom_call_target="tpu_custom_call" | custom-call | flops 1409286144 | bytes 6029320 | tf_op jit(solution)/shard_map/pallas_call | solution.py:56
  29.8 0.4 collective-permute-done.3.act.high
  30.3 1.9 %shard_map.88 = (bf16[3,64,1792]{2,1,0:T(8,128)(2,1)S(1)}, bf16[3,64,1792]{2,1,0:T(8,128)(2,1)S(1)}) custom-call(s32[2]{0:T(128)S(1)} %pad_add_fusion.place, bf16[256,1024]{1,0:T(8,128)(2,1)S(1)} %collective-permute-done.3.act.high, bf16[512,1792]{1,0:T(8,128)(2,1)S(1)} %copy-done.1, bf16[512,1792]{1,0:T(8,128)(2,1)S(1)} %copy-done.3, ...), custom_call_target="tpu_custom_call" | custom-call | flops 352321536 | bytes 6717448 | tf_op jit(solution)/shard_map/pallas_call | solution.py:56
  32.1 1.6 %collective-permute-start.4 = (bf16[3,64,1792]{2,1,0:T(8,128)(2,1)S(1)}, bf16[3,64,1792]{2,1,0:T(8,128)(2,1)S(1)}, u32[]{:S(2)}, u32[]{:S(2)}) collective-permute-start(bf16[3,64,1792]{2,1,0:T(8,128)(2,1)S(1)} %get-tuple-element.70), channel_id=1, source_target_pairs={{0,1},{1,2},{2,3},{3,0},{4,5},{5,6},{6,7},{7,4},{8,9},{9,10},{10,1... | collective-permute-start | bytes 2064392 | tf_op jit(solution)/shard_map/ppermute | solution.py:26
  33.7 0.5 collective-permute-start.5
  34.2 2.1 %shard_map.87 = (bf16[3,64,1792]{2,1,0:T(8,128)(2,1)S(1)}, bf16[3,64,1792]{2,1,0:T(8,128)(2,1)S(1)}, bf16[3,64,1792]{2,1,0:T(8,128)(2,1)S(1)}, bf16[3,64,1792]{2...) custom-call(s32[2]{0:T(128)S(1)} %pad_add_fusion.place, ...), custom_call_target="tpu_custom_call" | custom-call | flops 1056964608 | bytes 8093704 | tf_op jit(solution)/shard_map/pallas_call | solution.py:56
  36.3 2.2 %collective-permute-start.7 = (bf16[3,64,1792]{2,1,0:T(8,128)(2,1)S(1)}, bf16[3,64,1792]{2,1,0:T(8,128)(2,1)S(1)}, u32[]{:S(2)}, u32[]{:S(2)}) collective-permute-start(bf16[3,64,1792]{2,1,0:T(8,128)(2,1)S(1)} %get-tuple-element.73), channel_id=1, source_target_pairs={{0,3},{1,0},{2,1},{3,2},{4,7},{5,4},{6,5},{7,6},{8,11},{9,8},{10,9... | collective-permute-start | bytes 2064392 | tf_op jit(solution)/shard_map/ppermute | solution.py:26
  38.5 4.7 %collective-permute-done.4.refs_2_ = bf16[3,64,1792]{2,1,0:T(8,128)(2,1)S(1)} collective-permute-done((bf16[3,64,1792]{2,1,0:T(8,128)(2,1)S(1)}, bf16[3,64,1792]{2,1,0:T(8,128)(2,1)S(1)}, u32[]{:S(2)}, u32[]{:S(2)}) %collective-permute-start.4) | collective-permute-done | bytes 688160 | tf_op jit(solution)/shard_map/ppermute | solution.py:26
  43.1 1.5 %collective-permute-done.5.refs_3_ = bf16[3,64,1792]{2,1,0:T(8,128)(2,1)S(1)} collective-permute-done((bf16[3,64,1792]{2,1,0:T(8,128)(2,1)S(1)}, bf16[3,64,1792]{2,1,0:T(8,128)(2,1)S(1)}, u32[]{:S(2)}, u32[]{:S(2)}) %collective-permute-start.5) | collective-permute-done | bytes 688160 | tf_op jit(solution)/shard_map/ppermute | solution.py:26
  44.9 1.3 collective-permute-start.6
  46.2 0.8 collective-permute-start.8
  47.1 5.0 %collective-permute-done.7.refs_2_ = bf16[3,64,1792]{2,1,0:T(8,128)(2,1)S(1)} collective-permute-done((bf16[3,64,1792]{2,1,0:T(8,128)(2,1)S(1)}, bf16[3,64,1792]{2,1,0:T(8,128)(2,1)S(1)}, u32[]{:S(2)}, u32[]{:S(2)}) %collective-permute-start.7) | collective-permute-done | bytes 688160 | tf_op jit(solution)/shard_map/ppermute | solution.py:26
  52.0 5.9 %collective-permute-done.6.refs_1_ = bf16[3,64,1792]{2,1,0:T(8,128)(2,1)S(1)} collective-permute-done((bf16[3,64,1792]{2,1,0:T(8,128)(2,1)S(1)}, bf16[3,64,1792]{2,1,0:T(8,128)(2,1)S(1)}, u32[]{:S(2)}, u32[]{:S(2)}) %collective-permute-start.6) | collective-permute-done | bytes 688160 | tf_op jit(solution)/shard_map/ppermute | solution.py:26
  57.9 1.5 %collective-permute-done.8.refs_4_ = bf16[3,64,1792]{2,1,0:T(8,128)(2,1)S(1)} collective-permute-done((bf16[3,64,1792]{2,1,0:T(8,128)(2,1)S(1)}, bf16[3,64,1792]{2,1,0:T(8,128)(2,1)S(1)}, u32[]{:S(2)}, u32[]{:S(2)}) %collective-permute-start.8) | collective-permute-done | bytes 688160 | tf_op jit(solution)/shard_map/ppermute | solution.py:26
  59.4 1.7 %shard_map.90 = (bf16[3,32,1792]{2,1,0:T(8,128)(2,1)S(1)}, bf16[3,32,1792]{2,1,0:T(8,128)(2,1)S(1)}, bf16[3,32,1792]{2,1,0:T(8,128)(2,1)S(1)}, bf16[3,32,1792]{2,1,0:T(8,128)(2,1)S(1)}) custom-call(s32[2]{0:T(128)S(1)} %pad_add_fusion.place, bf16[3,64,1792]{2,1,0:T(8,128)(2,1)S(1)} %get-tuple-element.65.refs_0_, ...), custom_call_target="tpu_custom_call" | custom-call | bytes 4128776 | tf_op jit(solution)/shard_map/pallas_call | solution.py:56
  61.0 1.7 %collective-permute-start.10 = (bf16[3,32,1792]{2,1,0:T(8,128)(2,1)S(1)}, bf16[3,32,1792]{2,1,0:T(8,128)(2,1)S(1)}, u32[]{:S(2)}, u32[]{:S(2)}) collective-permute-start(bf16[3,32,1792]{2,1,0:T(8,128)(2,1)S(1)} %get-tuple-element.78), channel_id=1, source_target_pairs={{0,4},{1,5},{2,6},{3,7},{4,8},{5,9},{6,10},{7,11},{8,12},{9,13},{1... | collective-permute-start | bytes 1032200 | tf_op jit(solution)/shard_map/ppermute | solution.py:26
  62.7 2.9 %collective-permute-start.11 = (bf16[3,32,1792]{2,1,0:T(8,128)(2,1)S(1)}, bf16[3,32,1792]{2,1,0:T(8,128)(2,1)S(1)}, u32[]{:S(2)}, u32[]{:S(2)}) collective-permute-start(bf16[3,32,1792]{2,1,0:T(8,128)(2,1)S(1)} %get-tuple-element.79), channel_id=1, source_target_pairs={{0,8},{1,9},{2,10},{3,11},{4,12},{5,13},{6,14},{7,15},{8,0},{9,1},... | collective-permute-start | bytes 1032200 | tf_op jit(solution)/shard_map/ppermute | solution.py:26
  65.6 1.3 collective-permute-start.12
  67.0 2.6 %collective-permute-done.10.one = bf16[3,32,1792]{2,1,0:T(8,128)(2,1)S(1)} collective-permute-done((bf16[3,32,1792]{2,1,0:T(8,128)(2,1)S(1)}, bf16[3,32,1792]{2,1,0:T(8,128)(2,1)S(1)}, u32[]{:S(2)}, u32[]{:S(2)}) %collective-permute-start.10) | collective-permute-done | bytes 344096 | tf_op jit(solution)/shard_map/ppermute | solution.py:26
  69.6 4.9 %collective-permute-done.11.two = bf16[3,32,1792]{2,1,0:T(8,128)(2,1)S(1)} collective-permute-done((bf16[3,32,1792]{2,1,0:T(8,128)(2,1)S(1)}, bf16[3,32,1792]{2,1,0:T(8,128)(2,1)S(1)}, u32[]{:S(2)}, u32[]{:S(2)}) %collective-permute-start.11) | collective-permute-done | bytes 344096 | tf_op jit(solution)/shard_map/ppermute | solution.py:26
  74.8 1.7 %collective-permute-start.13 = (bf16[3,32,1792]{2,1,0:T(8,128)(2,1)S(1)}, bf16[3,32,1792]{2,1,0:T(8,128)(2,1)S(1)}, u32[]{:S(2)}, u32[]{:S(2)}) collective-permute-start(bf16[3,32,1792]{2,1,0:T(8,128)(2,1)S(1)} %shard_map.91.refs_0_), channel_id=1, source_target_pairs={{0,4},{1,5},{2,6},{3,7},{4,8},{5,9},{6,10},{7,11},{8,12},{9,13},{1... | collective-permute-start | bytes 1032200 | tf_op jit(solution)/shard_map/ppermute | solution.py:26
  76.5 2.1 %collective-permute-start.14 = (bf16[3,32,1792]{2,1,0:T(8,128)(2,1)S(1)}, bf16[3,32,1792]{2,1,0:T(8,128)(2,1)S(1)}, u32[]{:S(2)}, u32[]{:S(2)}) collective-permute-start(bf16[3,32,1792]{2,1,0:T(8,128)(2,1)S(1)} %shard_map.91.refs_0_), channel_id=1, source_target_pairs={{0,8},{1,9},{2,10},{3,11},{4,12},{5,13},{6,14},{7,15},{8,0},{9,1},... | collective-permute-start | bytes 1032200 | tf_op jit(solution)/shard_map/ppermute | solution.py:26
  78.6 1.7 %collective-permute-start.15 = (bf16[3,32,1792]{2,1,0:T(8,128)(2,1)S(1)}, bf16[3,32,1792]{2,1,0:T(8,128)(2,1)S(1)}, u32[]{:S(2)}, u32[]{:S(2)}) collective-permute-start(bf16[3,32,1792]{2,1,0:T(8,128)(2,1)S(1)} %shard_map.91.refs_0_), channel_id=1, source_target_pairs={{0,12},{1,13},{2,14},{3,15},{4,0},{5,1},{6,2},{7,3},{8,4},{9,5},{1... | collective-permute-start | bytes 1032200 | tf_op jit(solution)/shard_map/ppermute | solution.py:26
  80.3 3.0 %collective-permute-done.13.refs_1_ = bf16[3,32,1792]{2,1,0:T(8,128)(2,1)S(1)} collective-permute-done((bf16[3,32,1792]{2,1,0:T(8,128)(2,1)S(1)}, bf16[3,32,1792]{2,1,0:T(8,128)(2,1)S(1)}, u32[]{:S(2)}, u32[]{:S(2)}) %collective-permute-start.13) | collective-permute-done | bytes 344096 | tf_op jit(solution)/shard_map/ppermute | solution.py:26
  83.3 4.2 %collective-permute-done.14.refs_2_ = bf16[3,32,1792]{2,1,0:T(8,128)(2,1)S(1)} collective-permute-done((bf16[3,32,1792]{2,1,0:T(8,128)(2,1)S(1)}, bf16[3,32,1792]{2,1,0:T(8,128)(2,1)S(1)}, u32[]{:S(2)}, u32[]{:S(2)}) %collective-permute-start.14) | collective-permute-done | bytes 344096 | tf_op jit(solution)/shard_map/ppermute | solution.py:26
  87.5 0.4 collective-permute-done.15.refs_3_
  88.0 1.3 collective-permute-start.16
  89.3 0.8 collective-permute-start.19
  90.1 1.2 collective-permute-start.17
  91.3 0.8 collective-permute-start.18
  92.1 4.4 %collective-permute-done.16.refs_2_ = bf16[2,64,1792]{2,1,0:T(8,128)(2,1)S(1)} collective-permute-done((bf16[2,64,1792]{2,1,0:T(8,128)(2,1)S(1)}, bf16[2,64,1792]{2,1,0:T(8,128)(2,1)S(1)}, u32[]{:S(2)}, u32[]{:S(2)}) %collective-permute-start.16) | collective-permute-done | bytes 458784 | tf_op jit(solution)/shard_map/ppermute | solution.py:26
  96.5 1.2 collective-permute-start.20
  97.7 0.8 collective-permute-start.21
  98.6 2.9 %collective-permute-done.17.refs_3_ = bf16[2,64,1792]{2,1,0:T(8,128)(2,1)S(1)} collective-permute-done((bf16[2,64,1792]{2,1,0:T(8,128)(2,1)S(1)}, bf16[2,64,1792]{2,1,0:T(8,128)(2,1)S(1)}, u32[]{:S(2)}, u32[]{:S(2)}) %collective-permute-start.17) | collective-permute-done | bytes 458784 | tf_op jit(solution)/shard_map/ppermute | solution.py:26
  101.5 1.2 collective-permute-done.18.refs_4_
  102.7 1.7 %collective-permute-start.23 = (bf16[128,1792]{1,0:T(8,128)(2,1)S(1)}, bf16[128,1792]{1,0:T(8,128)(2,1)S(1)}, u32[]{:S(2)}, u32[]{:S(2)}) collective-permute-start(bf16[128,1792]{1,0:T(8,128)(2,1)S(1)} %get-tuple-element.110.refs_0_), channel_id=1, source_target_pairs={{0,1},{1,2},{2,3},{3,0},{4,5},{5,6},{6,7},{7,4},{8,9},{9,10},{10,1... | collective-permute-start | bytes 1376264 | tf_op jit(solution)/shard_map/ppermute | solution.py:26
  104.7 2.6 %collective-permute-start.25 = (bf16[128,1792]{1,0:T(8,128)(2,1)S(1)}, bf16[128,1792]{1,0:T(8,128)(2,1)S(1)}, u32[]{:S(2)}, u32[]{:S(2)}) collective-permute-start(bf16[128,1792]{1,0:T(8,128)(2,1)S(1)} %get-tuple-element.110.refs_0_), channel_id=1, source_target_pairs={{0,2},{1,3},{2,0},{3,1},{4,6},{5,7},{6,4},{7,5},{8,10},{9,11},{10,... | collective-permute-start | bytes 1376264 | tf_op jit(solution)/shard_map/ppermute | solution.py:26
  107.6 1.8 %shard_map.93 = (bf16[256,512]{1,0:T(8,128)(2,1)S(1)}, bf16[512,1792]{1,0:T(8,128)(2,1)S(1)}, bf16[512,1792]{1,0:T(8,128)(2,1)S(1)}) custom-call(s32[2]{0:T(128)S(1)} %pad_add_fusion.place, bf16[512,1792]{1,0:T(8,128)(2,1)S(1)} %copy-done.1, bf16[512,1792]{1,0:T(8,128)(2,1)S(1)} %copy-done.3, bf16[2,64,1792]{2,1,0:T(8,128)(2,1)S(1)} %get-tuple-element.81.refs_0_, ...), custom_call_target="tpu_custom_call" | custom-call | flops 939524096 | bytes 7340040 | tf_op jit(solution)/shard_map/pallas_call | solution.py:56
  109.4 3.5 %collective-permute-start.22 = (bf16[256,512]{1,0:T(8,128)(2,1)S(1)}, bf16[256,512]{1,0:T(8,128)(2,1)S(1)}, u32[]{:S(2)}, u32[]{:S(2)}) collective-permute-start(bf16[256,512]{1,0:T(8,128)(2,1)S(1)} %get-tuple-element.86), channel_id=1, source_target_pairs={{0,16},{16,0},{32,48},{48,32},{64,80},{80,64},{96,112},{112,96},{1... | collective-permute-start | bytes 786440 | tf_op jit(solution)/shard_map/ppermute | solution.py:44
  112.9 1.1 shard_map.94.keep
  114.0 2.1 %shard_map.95 = (bf16[512,1792]{1,0:T(8,128)(2,1)S(1)}, bf16[512,1792]{1,0:T(8,128)(2,1)S(1)}) custom-call(bf16[256,1024]{1,0:T(8,128)(2,1)S(1)} %shard_map.85.act.low, bf16[256,1024]{1,0:T(8,128)(2,1)S(1)} %collective-permute-done.3.act.high, bf16[512,1792]{1,0:T(8,128)(2,1)S(1)} %get-tuple-element.87.gg, bf16[512,1792]{1,0:T(8,128)(2,1)S(1)} %get-tuple-element.88.ug), custom_call_target="tpu_custom_call" | custom-call | flops 1879048192 | bytes 4718592 | tf_op jit(solution)/shard_map/pallas_call | solution.py:56
  116.1 1.1 collective-permute-done.22.got
  117.3 1.4 %collective-permute-done.25.refs_3_ = bf16[128,1792]{1,0:T(8,128)(2,1)S(1)} collective-permute-done((bf16[128,1792]{1,0:T(8,128)(2,1)S(1)}, bf16[128,1792]{1,0:T(8,128)(2,1)S(1)}, u32[]{:S(2)}, u32[]{:S(2)}) %collective-permute-start.25) | collective-permute-done | bytes 458784 | tf_op jit(solution)/shard_map/ppermute | solution.py:26
  118.7 0.5 collective-permute-start.29
  119.2 1.8 %shard_map.100.mine = bf16[1792,512]{1,0:T(8,128)(2,1)S(1)} custom-call(s32[2]{0:T(128)S(1)} %pad_add_fusion.place, bf16[256,1024]{1,0:T(8,128)(2,1)S(1)} %shard_map.85.act.low, bf16[256,1024]{1,0:T(8,128)(2,1)S(1)} %collective-permute-done.3.act.high, bf16[128,1792]{1,0:T(8,128)(2,1)S(1)} %get-tuple-element.110.refs_0_, ...), custom_call_target="tpu_custom_call" | custom-call | flops 939524096 | bytes 2883592 | tf_op jit(solution)/shard_map/pallas_call | solution.py:56
  121.1 1.1 collective-permute-start.26
  122.2 5.2 %collective-permute-start.27 = (bf16[64,512]{1,0:T(8,128)(2,1)S(1)}, bf16[64,512]{1,0:T(8,128)(2,1)S(1)}, u32[]{:S(2)}, u32[]{:S(2)}) collective-permute-start(bf16[64,512]{1,0:T(8,128)(2,1)S(1)} %get-tuple-element.100), channel_id=1, source_target_pairs={{0,64},{16,80},{32,96},{48,112},{64,0},{80,16},{96,32},{112,48},{1... | collective-permute-start | bytes 196616 | tf_op jit(solution)/shard_map/ppermute | solution.py:35
  127.5 1.3 collective-permute-start.28
  128.7 1.3 shard_map.98
  130.1 1.3 shard_map.97
  131.5 2.7 %collective-permute-done.28.refs_3_ = bf16[64,512]{1,0:T(8,128)(2,1)S(1)} collective-permute-done((bf16[64,512]{1,0:T(8,128)(2,1)S(1)}, bf16[64,512]{1,0:T(8,128)(2,1)S(1)}, u32[]{:S(2)}, u32[]{:S(2)}) %collective-permute-start.28) | collective-permute-done | bytes 65568 | tf_op jit(solution)/shard_map/ppermute | solution.py:35
  134.1 0.7 shard_map.99
  134.8 1.3 shard_map.101
  (35 shorter events, 1.6 us)
Async XLA Ops:
  0.6 0.8 copy-start.6
  1.5 0.8 copy-start.7
  2.3 16.2 %collective-permute-start = (bf16[64,1024]{1,0:T(8,128)(2,1)S(1)}, bf16[64,1024]{1,0:T(8,128)(2,1)S(1)}, u32[]{:S(2)}, u32[]{:S(2)}) collective-permute-start(bf16[64,1024]{1,0:T(8,128)(2,1)S(1)} %shard_map.84.refs_0_), channel_id=1, source_target_pairs={{0,96},{16,112},{32,0},{48,16},{64,32},{80,48},{96,64},{112,80},{1... | collective-permute-start | bytes 393224 | tf_op jit(solution)/shard_map/ppermute | solution.py:35
  8.7 11.1 %collective-permute-start.1 = (bf16[64,1024]{1,0:T(8,128)(2,1)S(1)}, bf16[64,1024]{1,0:T(8,128)(2,1)S(1)}, u32[]{:S(2)}, u32[]{:S(2)}) collective-permute-start(bf16[64,1024]{1,0:T(8,128)(2,1)S(1)} %shard_map.84.refs_0_), channel_id=1, source_target_pairs={{0,64},{16,80},{32,96},{48,112},{64,0},{80,16},{96,32},{112,48},{1... | collective-permute-start | bytes 393224 | tf_op jit(solution)/shard_map/ppermute | solution.py:35
  9.7 10.1 %collective-permute-start.2 = (bf16[64,1024]{1,0:T(8,128)(2,1)S(1)}, bf16[64,1024]{1,0:T(8,128)(2,1)S(1)}, u32[]{:S(2)}, u32[]{:S(2)}) collective-permute-start(bf16[64,1024]{1,0:T(8,128)(2,1)S(1)} %shard_map.84.refs_0_), channel_id=1, source_target_pairs={{0,32},{16,48},{32,64},{48,80},{64,96},{80,112},{96,0},{112,16},{1... | collective-permute-start | bytes 393224 | tf_op jit(solution)/shard_map/ppermute | solution.py:35
  19.8 10.5 %collective-permute-start.3 = (bf16[256,1024]{1,0:T(8,128)(2,1)S(1)}, bf16[256,1024]{1,0:T(8,128)(2,1)S(1)}, u32[]{:S(2)}, u32[]{:S(2)}) collective-permute-start(bf16[256,1024]{1,0:T(8,128)(2,1)S(1)} %shard_map.85.act.low), channel_id=1, source_target_pairs={{0,16},{16,0},{32,48},{48,32},{64,80},{80,64},{96,112},{112,96},{1... | collective-permute-start | bytes 1572872 | tf_op jit(solution)/shard_map/ppermute | solution.py:44
  23.2 1.5 %copy-start = (bf16[512,1792]{1,0:T(8,128)(2,1)S(1)}, bf16[512,1792]{1,0:T(8,128)(2,1)}, u32[]{:S(2)}) copy-start(bf16[512,1792]{1,0:T(8,128)(2,1)} %gate.9) | copy-start | bytes 5505028
  24.7 1.5 %copy-start.2 = (bf16[512,1792]{1,0:T(8,128)(2,1)S(1)}, bf16[512,1792]{1,0:T(8,128)(2,1)}, u32[]{:S(2)}) copy-start(bf16[512,1792]{1,0:T(8,128)(2,1)} %up.9) | copy-start | bytes 5505028
  26.2 1.5 %copy-start.4 = (bf16[1792,512]{1,0:T(8,128)(2,1)S(1)}, bf16[1792,512]{1,0:T(8,128)(2,1)}, u32[]{:S(2)}) copy-start(bf16[1792,512]{1,0:T(8,128)(2,1)} %down.5) | copy-start | bytes 5505028
  27.7 2.6 %copy-start.1 = (bf16[512,1792]{1,0:T(8,128)(2,1)S(1)}, bf16[512,1792]{1,0:T(8,128)(2,1)}, u32[]{:S(2)}) copy-start(bf16[512,1792]{1,0:T(8,128)(2,1)} %gate.9) | copy-start | bytes 5505028
  27.7 2.6 %copy-start.3 = (bf16[512,1792]{1,0:T(8,128)(2,1)S(1)}, bf16[512,1792]{1,0:T(8,128)(2,1)}, u32[]{:S(2)}) copy-start(bf16[512,1792]{1,0:T(8,128)(2,1)} %up.9) | copy-start | bytes 5505028
  27.7 2.6 %copy-start.5 = (bf16[1792,512]{1,0:T(8,128)(2,1)S(1)}, bf16[1792,512]{1,0:T(8,128)(2,1)}, u32[]{:S(2)}) copy-start(bf16[1792,512]{1,0:T(8,128)(2,1)} %down.5) | copy-start | bytes 5505028
  32.1 11.0 %collective-permute-start.4 = (bf16[3,64,1792]{2,1,0:T(8,128)(2,1)S(1)}, bf16[3,64,1792]{2,1,0:T(8,128)(2,1)S(1)}, u32[]{:S(2)}, u32[]{:S(2)}) collective-permute-start(bf16[3,64,1792]{2,1,0:T(8,128)(2,1)S(1)} %get-tuple-element.70), channel_id=1, source_target_pairs={{0,1},{1,2},{2,3},{3,0},{4,5},{5,6},{6,7},{7,4},{8,9},{9,10},{10,1... | collective-permute-start | bytes 2064392 | tf_op jit(solution)/shard_map/ppermute | solution.py:26
  33.7 10.9 %collective-permute-start.5 = (bf16[3,64,1792]{2,1,0:T(8,128)(2,1)S(1)}, bf16[3,64,1792]{2,1,0:T(8,128)(2,1)S(1)}, u32[]{:S(2)}, u32[]{:S(2)}) collective-permute-start(bf16[3,64,1792]{2,1,0:T(8,128)(2,1)S(1)} %get-tuple-element.71), channel_id=1, source_target_pairs={{0,3},{1,0},{2,1},{3,2},{4,7},{5,4},{6,5},{7,6},{8,11},{9,8},{10,9... | collective-permute-start | bytes 2064392 | tf_op jit(solution)/shard_map/ppermute | solution.py:26
  36.3 15.7 %collective-permute-start.7 = (bf16[3,64,1792]{2,1,0:T(8,128)(2,1)S(1)}, bf16[3,64,1792]{2,1,0:T(8,128)(2,1)S(1)}, u32[]{:S(2)}, u32[]{:S(2)}) collective-permute-start(bf16[3,64,1792]{2,1,0:T(8,128)(2,1)S(1)} %get-tuple-element.73), channel_id=1, source_target_pairs={{0,3},{1,0},{2,1},{3,2},{4,7},{5,4},{6,5},{7,6},{8,11},{9,8},{10,9... | collective-permute-start | bytes 2064392 | tf_op jit(solution)/shard_map/ppermute | solution.py:26
  38.5 13.5 %collective-permute-start.9 = (bf16[3,64,1792]{2,1,0:T(8,128)(2,1)S(1)}, bf16[3,64,1792]{2,1,0:T(8,128)(2,1)S(1)}, u32[]{:S(2)}, u32[]{:S(2)}) collective-permute-start(bf16[3,64,1792]{2,1,0:T(8,128)(2,1)S(1)} %get-tuple-element.76), channel_id=1, source_target_pairs={{0,1},{1,2},{2,3},{3,0},{4,5},{5,6},{6,7},{7,4},{8,9},{9,10},{10,1... | collective-permute-start | bytes 2064392 | tf_op jit(solution)/shard_map/ppermute | solution.py:26
  44.9 12.9 %collective-permute-start.6 = (bf16[3,64,1792]{2,1,0:T(8,128)(2,1)S(1)}, bf16[3,64,1792]{2,1,0:T(8,128)(2,1)S(1)}, u32[]{:S(2)}, u32[]{:S(2)}) collective-permute-start(bf16[3,64,1792]{2,1,0:T(8,128)(2,1)S(1)} %get-tuple-element.72), channel_id=1, source_target_pairs={{0,1},{1,2},{2,3},{3,0},{4,5},{5,6},{6,7},{7,4},{8,9},{9,10},{10,1... | collective-permute-start | bytes 2064392 | tf_op jit(solution)/shard_map/ppermute | solution.py:26
  46.2 13.2 %collective-permute-start.8 = (bf16[3,64,1792]{2,1,0:T(8,128)(2,1)S(1)}, bf16[3,64,1792]{2,1,0:T(8,128)(2,1)S(1)}, u32[]{:S(2)}, u32[]{:S(2)}) collective-permute-start(bf16[3,64,1792]{2,1,0:T(8,128)(2,1)S(1)} %get-tuple-element.75), channel_id=1, source_target_pairs={{0,3},{1,0},{2,1},{3,2},{4,7},{5,4},{6,5},{7,6},{8,11},{9,8},{10,9... | collective-permute-start | bytes 2064392 | tf_op jit(solution)/shard_map/ppermute | solution.py:26
  61.0 8.5 %collective-permute-start.10 = (bf16[3,32,1792]{2,1,0:T(8,128)(2,1)S(1)}, bf16[3,32,1792]{2,1,0:T(8,128)(2,1)S(1)}, u32[]{:S(2)}, u32[]{:S(2)}) collective-permute-start(bf16[3,32,1792]{2,1,0:T(8,128)(2,1)S(1)} %get-tuple-element.78), channel_id=1, source_target_pairs={{0,4},{1,5},{2,6},{3,7},{4,8},{5,9},{6,10},{7,11},{8,12},{9,13},{1... | collective-permute-start | bytes 1032200 | tf_op jit(solution)/shard_map/ppermute | solution.py:26
  62.7 11.8 %collective-permute-start.11 = (bf16[3,32,1792]{2,1,0:T(8,128)(2,1)S(1)}, bf16[3,32,1792]{2,1,0:T(8,128)(2,1)S(1)}, u32[]{:S(2)}, u32[]{:S(2)}) collective-permute-start(bf16[3,32,1792]{2,1,0:T(8,128)(2,1)S(1)} %get-tuple-element.79), channel_id=1, source_target_pairs={{0,8},{1,9},{2,10},{3,11},{4,12},{5,13},{6,14},{7,15},{8,0},{9,1},... | collective-permute-start | bytes 1032200 | tf_op jit(solution)/shard_map/ppermute | solution.py:26
  65.6 8.9 %collective-permute-start.12 = (bf16[3,32,1792]{2,1,0:T(8,128)(2,1)S(1)}, bf16[3,32,1792]{2,1,0:T(8,128)(2,1)S(1)}, u32[]{:S(2)}, u32[]{:S(2)}) collective-permute-start(bf16[3,32,1792]{2,1,0:T(8,128)(2,1)S(1)} %get-tuple-element.80), channel_id=1, source_target_pairs={{0,12},{1,13},{2,14},{3,15},{4,0},{5,1},{6,2},{7,3},{8,4},{9,5},{1... | collective-permute-start | bytes 1032200 | tf_op jit(solution)/shard_map/ppermute | solution.py:26
  74.8 8.5 %collective-permute-start.13 = (bf16[3,32,1792]{2,1,0:T(8,128)(2,1)S(1)}, bf16[3,32,1792]{2,1,0:T(8,128)(2,1)S(1)}, u32[]{:S(2)}, u32[]{:S(2)}) collective-permute-start(bf16[3,32,1792]{2,1,0:T(8,128)(2,1)S(1)} %shard_map.91.refs_0_), channel_id=1, source_target_pairs={{0,4},{1,5},{2,6},{3,7},{4,8},{5,9},{6,10},{7,11},{8,12},{9,13},{1... | collective-permute-start | bytes 1032200 | tf_op jit(solution)/shard_map/ppermute | solution.py:26
  76.5 11.0 %collective-permute-start.14 = (bf16[3,32,1792]{2,1,0:T(8,128)(2,1)S(1)}, bf16[3,32,1792]{2,1,0:T(8,128)(2,1)S(1)}, u32[]{:S(2)}, u32[]{:S(2)}) collective-permute-start(bf16[3,32,1792]{2,1,0:T(8,128)(2,1)S(1)} %shard_map.91.refs_0_), channel_id=1, source_target_pairs={{0,8},{1,9},{2,10},{3,11},{4,12},{5,13},{6,14},{7,15},{8,0},{9,1},... | collective-permute-start | bytes 1032200 | tf_op jit(solution)/shard_map/ppermute | solution.py:26
  78.6 9.3 %collective-permute-start.15 = (bf16[3,32,1792]{2,1,0:T(8,128)(2,1)S(1)}, bf16[3,32,1792]{2,1,0:T(8,128)(2,1)S(1)}, u32[]{:S(2)}, u32[]{:S(2)}) collective-permute-start(bf16[3,32,1792]{2,1,0:T(8,128)(2,1)S(1)} %shard_map.91.refs_0_), channel_id=1, source_target_pairs={{0,12},{1,13},{2,14},{3,15},{4,0},{5,1},{6,2},{7,3},{8,4},{9,5},{1... | collective-permute-start | bytes 1032200 | tf_op jit(solution)/shard_map/ppermute | solution.py:26
  88.0 8.6 %collective-permute-start.16 = (bf16[2,64,1792]{2,1,0:T(8,128)(2,1)S(1)}, bf16[2,64,1792]{2,1,0:T(8,128)(2,1)S(1)}, u32[]{:S(2)}, u32[]{:S(2)}) collective-permute-start(bf16[2,64,1792]{2,1,0:T(8,128)(2,1)S(1)} %get-tuple-element.81.refs_0_), channel_id=1, source_target_pairs={{0,1},{1,2},{2,3},{3,0},{4,5},{5,6},{6,7},{7,4},{8,9},{9,10},{10,1... | collective-permute-start | bytes 1376264 | tf_op jit(solution)/shard_map/ppermute | solution.py:26
  89.3 8.5 %collective-permute-start.19 = (bf16[2,64,1792]{2,1,0:T(8,128)(2,1)S(1)}, bf16[2,64,1792]{2,1,0:T(8,128)(2,1)S(1)}, u32[]{:S(2)}, u32[]{:S(2)}) collective-permute-start(bf16[2,64,1792]{2,1,0:T(8,128)(2,1)S(1)} %get-tuple-element.82.refs_1_), channel_id=1, source_target_pairs={{0,3},{1,0},{2,1},{3,2},{4,7},{5,4},{6,5},{7,6},{8,11},{9,8},{10,9... | collective-permute-start | bytes 1376264 | tf_op jit(solution)/shard_map/ppermute | solution.py:26
  90.1 11.4 %collective-permute-start.17 = (bf16[2,64,1792]{2,1,0:T(8,128)(2,1)S(1)}, bf16[2,64,1792]{2,1,0:T(8,128)(2,1)S(1)}, u32[]{:S(2)}, u32[]{:S(2)}) collective-permute-start(bf16[2,64,1792]{2,1,0:T(8,128)(2,1)S(1)} %get-tuple-element.82.refs_1_), channel_id=1, source_target_pairs={{0,1},{1,2},{2,3},{3,0},{4,5},{5,6},{6,7},{7,4},{8,9},{9,10},{10,1... | collective-permute-start | bytes 1376264 | tf_op jit(solution)/shard_map/ppermute | solution.py:26
  91.3 11.4 %collective-permute-start.18 = (bf16[2,64,1792]{2,1,0:T(8,128)(2,1)S(1)}, bf16[2,64,1792]{2,1,0:T(8,128)(2,1)S(1)}, u32[]{:S(2)}, u32[]{:S(2)}) collective-permute-start(bf16[2,64,1792]{2,1,0:T(8,128)(2,1)S(1)} %get-tuple-element.81.refs_0_), channel_id=1, source_target_pairs={{0,3},{1,0},{2,1},{3,2},{4,7},{5,4},{6,5},{7,6},{8,11},{9,8},{10,9... | collective-permute-start | bytes 1376264 | tf_op jit(solution)/shard_map/ppermute | solution.py:26
  96.5 10.8 %collective-permute-start.20 = (bf16[2,64,1792]{2,1,0:T(8,128)(2,1)S(1)}, bf16[2,64,1792]{2,1,0:T(8,128)(2,1)S(1)}, u32[]{:S(2)}, u32[]{:S(2)}) collective-permute-start(bf16[2,64,1792]{2,1,0:T(8,128)(2,1)S(1)} %collective-permute-done.16.refs_2_), channel_id=1, source_target_pairs={{0,1},{1,2},{2,3},{3,0},{4,5},{5,6},{6,7},{7,4},{8,9},{9,10},{10,1... | collective-permute-start | bytes 1376264 | tf_op jit(solution)/shard_map/ppermute | solution.py:26
  97.7 9.8 %collective-permute-start.21 = (bf16[2,64,1792]{2,1,0:T(8,128)(2,1)S(1)}, bf16[2,64,1792]{2,1,0:T(8,128)(2,1)S(1)}, u32[]{:S(2)}, u32[]{:S(2)}) collective-permute-start(bf16[2,64,1792]{2,1,0:T(8,128)(2,1)S(1)} %collective-permute-done.19.refs_5_), channel_id=1, source_target_pairs={{0,3},{1,0},{2,1},{3,2},{4,7},{5,4},{6,5},{7,6},{8,11},{9,8},{10,9... | collective-permute-start | bytes 1376264 | tf_op jit(solution)/shard_map/ppermute | solution.py:26
  102.7 14.6 %collective-permute-start.23 = (bf16[128,1792]{1,0:T(8,128)(2,1)S(1)}, bf16[128,1792]{1,0:T(8,128)(2,1)S(1)}, u32[]{:S(2)}, u32[]{:S(2)}) collective-permute-start(bf16[128,1792]{1,0:T(8,128)(2,1)S(1)} %get-tuple-element.110.refs_0_), channel_id=1, source_target_pairs={{0,1},{1,2},{2,3},{3,0},{4,5},{5,6},{6,7},{7,4},{8,9},{9,10},{10,1... | collective-permute-start | bytes 1376264 | tf_op jit(solution)/shard_map/ppermute | solution.py:26
  104.3 12.9 %collective-permute-start.24 = (bf16[128,1792]{1,0:T(8,128)(2,1)S(1)}, bf16[128,1792]{1,0:T(8,128)(2,1)S(1)}, u32[]{:S(2)}, u32[]{:S(2)}) collective-permute-start(bf16[128,1792]{1,0:T(8,128)(2,1)S(1)} %get-tuple-element.110.refs_0_), channel_id=1, source_target_pairs={{0,3},{1,0},{2,1},{3,2},{4,7},{5,4},{6,5},{7,6},{8,11},{9,8},{10,9... | collective-permute-start | bytes 1376264 | tf_op jit(solution)/shard_map/ppermute | solution.py:26
  104.7 14.0 %collective-permute-start.25 = (bf16[128,1792]{1,0:T(8,128)(2,1)S(1)}, bf16[128,1792]{1,0:T(8,128)(2,1)S(1)}, u32[]{:S(2)}, u32[]{:S(2)}) collective-permute-start(bf16[128,1792]{1,0:T(8,128)(2,1)S(1)} %get-tuple-element.110.refs_0_), channel_id=1, source_target_pairs={{0,2},{1,3},{2,0},{3,1},{4,6},{5,7},{6,4},{7,5},{8,10},{9,11},{10,... | collective-permute-start | bytes 1376264 | tf_op jit(solution)/shard_map/ppermute | solution.py:26
  109.4 7.8 %collective-permute-start.22 = (bf16[256,512]{1,0:T(8,128)(2,1)S(1)}, bf16[256,512]{1,0:T(8,128)(2,1)S(1)}, u32[]{:S(2)}, u32[]{:S(2)}) collective-permute-start(bf16[256,512]{1,0:T(8,128)(2,1)S(1)} %get-tuple-element.86), channel_id=1, source_target_pairs={{0,16},{16,0},{32,48},{48,32},{64,80},{80,64},{96,112},{112,96},{1... | collective-permute-start | bytes 786440 | tf_op jit(solution)/shard_map/ppermute | solution.py:44
  118.7 8.8 %collective-permute-start.30 = (bf16[512,1792]{1,0:T(8,128)(2,1)S(1)}, bf16[512,1792]{1,0:T(8,128)(2,1)S(1)}, u32[]{:S(2)}, u32[]{:S(2)}) collective-permute-start(bf16[512,1792]{1,0:T(8,128)(2,1)S(1)} %get-tuple-element.103.mine), channel_id=1, source_target_pairs={{0,128},{128,0},{1,129},{129,1},{2,130},{130,2},{3,131},{131,3},{4... | collective-permute-start | bytes 5505032 | tf_op jit(solution)/shard_map/ppermute | solution.py:48
  118.7 11.4 %collective-permute-start.29 = (bf16[512,1792]{1,0:T(8,128)(2,1)S(1)}, bf16[512,1792]{1,0:T(8,128)(2,1)S(1)}, u32[]{:S(2)}, u32[]{:S(2)}) collective-permute-start(bf16[512,1792]{1,0:T(8,128)(2,1)S(1)} %get-tuple-element.102.mine), channel_id=1, source_target_pairs={{0,128},{128,0},{1,129},{129,1},{2,130},{130,2},{3,131},{131,3},{4... | collective-permute-start | bytes 5505032 | tf_op jit(solution)/shard_map/ppermute | solution.py:48
  121.0 13.8 %collective-permute-start.31 = (bf16[1792,512]{1,0:T(8,128)(2,1)S(1)}, bf16[1792,512]{1,0:T(8,128)(2,1)S(1)}, u32[]{:S(2)}, u32[]{:S(2)}) collective-permute-start(bf16[1792,512]{1,0:T(8,128)(2,1)S(1)} %shard_map.100.mine), channel_id=1, source_target_pairs={{0,128},{128,0},{1,129},{129,1},{2,130},{130,2},{3,131},{131,3},{4... | collective-permute-start | bytes 5505032 | tf_op jit(solution)/shard_map/ppermute | solution.py:48
  121.1 10.3 %collective-permute-start.26 = (bf16[64,512]{1,0:T(8,128)(2,1)S(1)}, bf16[64,512]{1,0:T(8,128)(2,1)S(1)}, u32[]{:S(2)}, u32[]{:S(2)}) collective-permute-start(bf16[64,512]{1,0:T(8,128)(2,1)S(1)} %get-tuple-element.99), channel_id=1, source_target_pairs={{0,32},{16,48},{32,64},{48,80},{64,96},{80,112},{96,0},{112,16},{1... | collective-permute-start | bytes 196616 | tf_op jit(solution)/shard_map/ppermute | solution.py:35
  122.2 9.2 %collective-permute-start.27 = (bf16[64,512]{1,0:T(8,128)(2,1)S(1)}, bf16[64,512]{1,0:T(8,128)(2,1)S(1)}, u32[]{:S(2)}, u32[]{:S(2)}) collective-permute-start(bf16[64,512]{1,0:T(8,128)(2,1)S(1)} %get-tuple-element.100), channel_id=1, source_target_pairs={{0,64},{16,80},{32,96},{48,112},{64,0},{80,16},{96,32},{112,48},{1... | collective-permute-start | bytes 196616 | tf_op jit(solution)/shard_map/ppermute | solution.py:35
  127.5 6.7 %collective-permute-start.28 = (bf16[64,512]{1,0:T(8,128)(2,1)S(1)}, bf16[64,512]{1,0:T(8,128)(2,1)S(1)}, u32[]{:S(2)}, u32[]{:S(2)}) collective-permute-start(bf16[64,512]{1,0:T(8,128)(2,1)S(1)} %get-tuple-element.101), channel_id=1, source_target_pairs={{0,96},{16,112},{32,0},{48,16},{64,32},{80,48},{96,64},{112,80},{1... | collective-permute-start | bytes 196616 | tf_op jit(solution)/shard_map/ppermute | solution.py:35

commit v4 on v3

--- a/solution.py
+++ b/solution.py
@@ -8,6 +8,7 @@
 from jax.sharding import PartitionSpec as P
 
 RING = 4
+STEPS = (2, 1, 3)
 MERGE = 8
 BF16 = jnp.bfloat16
 F32 = jnp.float32
@@ -136,10 +137,10 @@
 
 def join_kernel(*refs):
     low, high, hid = refs[4:]
-    for j in range(4):
+    for j, ref in zip((0,) + STEPS, refs):
         rows = slice(32 * (j % 2), 32 * (j % 2) + 32)
-        (low if j < 2 else high)[:, rows] = refs[j][:2]
-        hid[32 * j : 32 * j + 32] = refs[j][2]
+        (low if j < 2 else high)[:, rows] = ref[:2]
+        hid[32 * j : 32 * j + 32] = ref[2]
 
 
 def rows_at(place, step, j):
@@ -187,7 +188,7 @@
 
 def hidden_kernel(place, low, high, *refs):
     pieces, down_out, act, hid = refs[:4], *refs[4:]
-    for i, step in enumerate((0, 3, 1, 2)):
+    for i, step in enumerate((0, 2, 3, 1)):
         for j in range(4):
             hid[rows_at(place, step, j)] = pieces[i][32 * j : 32 * j + 32]
     width, rows = down_out.shape[1], low.shape[0]
@@ -274,9 +275,9 @@
         (place, low, relay_up, near_down, high, relay_down, near_up),
         scratch=[pltpu.VMEM((4, 3, 32, hidden), BF16)],
     )
-    got = [own[0]] + [send_col(own[step], 1, step) for step in range(1, RING)]
+    got = [own[0]] + [send_col(own[step], 1, step) for step in STEPS]
     unit = call(unit_kernel, [third], got)[0]
-    got = [unit] + [send_col(unit, 1, step) for step in range(1, RING)]
+    got = [unit] + [send_col(unit, 1, step) for step in STEPS]
     low, high, hid = call(
         join_kernel,
         [((2, 64, hidden), BF16)] * 2 + [((128, hidden), BF16)],
@@ -287,7 +288,7 @@
     low_far, high_far = send_col(low_left, 0, 1), send_col(high_right, 0, -1)
     hid, high_left, low_right = lax.optimization_barrier((hid, high_left, low_right))
     pieces = (low, high, low_left, high_left, low_right, high_right, low_far, high_far)
-    hids = (hid, send_col(hid, 0, 1), send_col(hid, 0, -1), send_col(hid, 0, 2))
+    hids = (hid, *(send_col(hid, 0, step) for step in STEPS))
 
     whole = pltpu.VMEM((rows, hidden), BF16)
     lhs = pltpu.VMEM((rows, width), BF16)

time: 138 us -> 136 us (0.986)
    ppermute x21, waiting for transfers between devices: 43.8 us -> 42 us  [send_col(): return lax.ppermute(value, ('dp', 'col'), pairs)]
  transfers between devices with their start and end apart: 32 -> 32, of which waited for: 20 -> 21; matrix products, arithmetic and copies ran while one was open for 0% -> 0% of each run, Pallas kernels for 11% -> 11%
where the time goes in v4:
time: 136 us; the launch traced here: 135 us
  starting transfers between devices  54.2 us (40%)
  waiting for transfers between devices  53.9 us (40%)
  Pallas kernels  20.1 us (15%)
  local copies, waits for them, and re-layouts  6.19 us (5%)
    ppermute x21, waiting for transfers between devices, send_col(): return lax.ppermute(value, ('dp', 'col'), pairs)  42 us
    ppermute x21, starting transfers between devices, send_col(): return lax.ppermute(value, ('dp', 'col'), pairs)  29.1 us
    ppermute x6, starting transfers between devices, send_row(): return lax.ppermute(value, ('dp', 'row'), pairs)  17.8 us
    pallas_call x15, Pallas kernels, call(): pl.pallas_call(kernel, out_shape=[jax.ShapeDtypeStruct(shape, kind) for s...  16.1 us
    ppermute x6, waiting for transfers between devices, send_row(): return lax.ppermute(value, ('dp', 'row'), pairs)  10.4 us
    ppermute x2, starting transfers between devices, swap_row(): return lax.ppermute(value, ('dp', 'row'), pairs)  6.7 us
    unnamed x16, local copies, waits for them, and re-layouts  6.19 us
    pallas_call x3, Pallas kernels, merge(): pl.pallas_call(merge_kernel, out_shape=jax.ShapeDtypeStruct(term.shape, B...  4.02 us
  transfers between devices with their start and end apart: 32, of which 21 were waited for; matrix products, arithmetic and copies ran while one was open for 0% of the time, Pallas kernels for 11%

profile of v4, /device:TPU:2, one launch (start us, length us, event | category | flops | bytes accessed | tf_op | source)
XLA Modules:
  0.0 135.5 jit_solution(11601376934721365454)
XLA Ops:
  0.6 0.8 copy-done.6
  1.5 0.8 copy-done.7
  2.3 6.4 %collective-permute-start = (bf16[64,1024]{1,0:T(8,128)(2,1)S(1)}, bf16[64,1024]{1,0:T(8,128)(2,1)S(1)}, u32[]{:S(2)}, u32[]{:S(2)}) collective-permute-start(bf16[64,1024]{1,0:T(8,128)(2,1)S(1)} %shard_map.84.refs_0_), channel_id=1, source_target_pairs={{0,96},{16,112},{32,0},{48,16},{64,32},{80,48},{96,64},{112,80},{1... | collective-permute-start | bytes 393224 | tf_op jit(solution)/shard_map/ppermute | solution.py:36
  8.7 1.0 collective-permute-start.1
  9.7 2.8 %collective-permute-start.2 = (bf16[64,1024]{1,0:T(8,128)(2,1)S(1)}, bf16[64,1024]{1,0:T(8,128)(2,1)S(1)}, u32[]{:S(2)}, u32[]{:S(2)}) collective-permute-start(bf16[64,1024]{1,0:T(8,128)(2,1)S(1)} %shard_map.84.refs_0_), channel_id=1, source_target_pairs={{0,32},{16,48},{32,64},{48,80},{64,96},{80,112},{96,0},{112,16},{1... | collective-permute-start | bytes 393224 | tf_op jit(solution)/shard_map/ppermute | solution.py:36
  12.5 6.0 %collective-permute-done.refs_1_ = bf16[64,1024]{1,0:T(8,128)(2,1)S(1)} collective-permute-done((bf16[64,1024]{1,0:T(8,128)(2,1)S(1)}, bf16[64,1024]{1,0:T(8,128)(2,1)S(1)}, u32[]{:S(2)}, u32[]{:S(2)}) %collective-permute-start) | collective-permute-done | bytes 131104 | tf_op jit(solution)/shard_map/ppermute | solution.py:36
  18.5 1.2 collective-permute-done.1.refs_2_
  19.8 3.3 %collective-permute-start.3 = (bf16[256,1024]{1,0:T(8,128)(2,1)S(1)}, bf16[256,1024]{1,0:T(8,128)(2,1)S(1)}, u32[]{:S(2)}, u32[]{:S(2)}) collective-permute-start(bf16[256,1024]{1,0:T(8,128)(2,1)S(1)} %shard_map.85.act.low), channel_id=1, source_target_pairs={{0,16},{16,0},{32,48},{48,32},{64,80},{80,64},{96,112},{112,96},{1... | collective-permute-start | bytes 1572872 | tf_op jit(solution)/shard_map/ppermute | solution.py:45
  23.2 1.5 %copy-done = bf16[512,1792]{1,0:T(8,128)(2,1)S(1)} copy-done((bf16[512,1792]{1,0:T(8,128)(2,1)S(1)}, bf16[512,1792]{1,0:T(8,128)(2,1)}, u32[]{:S(2)}) %copy-start) | copy-done | bytes 1835032
  24.7 1.5 %copy-done.2 = bf16[512,1792]{1,0:T(8,128)(2,1)S(1)} copy-done((bf16[512,1792]{1,0:T(8,128)(2,1)S(1)}, bf16[512,1792]{1,0:T(8,128)(2,1)}, u32[]{:S(2)}) %copy-start.2) | copy-done | bytes 1835032
  26.2 1.5 %copy-done.4 = bf16[1792,512]{1,0:T(8,128)(2,1)S(1)} copy-done((bf16[1792,512]{1,0:T(8,128)(2,1)S(1)}, bf16[1792,512]{1,0:T(8,128)(2,1)}, u32[]{:S(2)}) %copy-start.4) | copy-done | bytes 1835032
  27.7 2.1 %shard_map.86 = (bf16[3,32,1792]{2,1,0:T(8,128)(2,1)S(1)}, bf16[3,32,1792]{2,1,0:T(8,128)(2,1)S(1)}, bf16[3,32,1792]{2,1,0:T(8,128)(2,1)S(1)}, bf16[3,32,1792]{2...) custom-call(s32[2]{0:T(128)S(1)} %pad_add_fusion.place, ...), custom_call_target="tpu_custom_call" | custom-call | flops 1409286144 | bytes 6029320 | tf_op jit(solution)/shard_map/pallas_call | solution.py:57
  29.8 0.4 collective-permute-done.3.act.high
  30.3 1.9 %shard_map.88 = (bf16[3,64,1792]{2,1,0:T(8,128)(2,1)S(1)}, bf16[3,64,1792]{2,1,0:T(8,128)(2,1)S(1)}) custom-call(s32[2]{0:T(128)S(1)} %pad_add_fusion.place, bf16[256,1024]{1,0:T(8,128)(2,1)S(1)} %collective-permute-done.3.act.high, bf16[512,1792]{1,0:T(8,128)(2,1)S(1)} %copy-done.1, bf16[512,1792]{1,0:T(8,128)(2,1)S(1)} %copy-done.3, ...), custom_call_target="tpu_custom_call" | custom-call | flops 352321536 | bytes 6717448 | tf_op jit(solution)/shard_map/pallas_call | solution.py:57
  32.1 1.6 %collective-permute-start.4 = (bf16[3,64,1792]{2,1,0:T(8,128)(2,1)S(1)}, bf16[3,64,1792]{2,1,0:T(8,128)(2,1)S(1)}, u32[]{:S(2)}, u32[]{:S(2)}) collective-permute-start(bf16[3,64,1792]{2,1,0:T(8,128)(2,1)S(1)} %get-tuple-element.70), channel_id=1, source_target_pairs={{0,1},{1,2},{2,3},{3,0},{4,5},{5,6},{6,7},{7,4},{8,9},{9,10},{10,1... | collective-permute-start | bytes 2064392 | tf_op jit(solution)/shard_map/ppermute | solution.py:27
  33.7 0.5 collective-permute-start.5
  34.2 2.1 %shard_map.87 = (bf16[3,64,1792]{2,1,0:T(8,128)(2,1)S(1)}, bf16[3,64,1792]{2,1,0:T(8,128)(2,1)S(1)}, bf16[3,64,1792]{2,1,0:T(8,128)(2,1)S(1)}, bf16[3,64,1792]{2...) custom-call(s32[2]{0:T(128)S(1)} %pad_add_fusion.place, ...), custom_call_target="tpu_custom_call" | custom-call | flops 1056964608 | bytes 8093704 | tf_op jit(solution)/shard_map/pallas_call | solution.py:57
  36.3 2.2 %collective-permute-start.7 = (bf16[3,64,1792]{2,1,0:T(8,128)(2,1)S(1)}, bf16[3,64,1792]{2,1,0:T(8,128)(2,1)S(1)}, u32[]{:S(2)}, u32[]{:S(2)}) collective-permute-start(bf16[3,64,1792]{2,1,0:T(8,128)(2,1)S(1)} %get-tuple-element.73), channel_id=1, source_target_pairs={{0,3},{1,0},{2,1},{3,2},{4,7},{5,4},{6,5},{7,6},{8,11},{9,8},{10,9... | collective-permute-start | bytes 2064392 | tf_op jit(solution)/shard_map/ppermute | solution.py:27
  38.5 4.7 %collective-permute-done.4.refs_2_ = bf16[3,64,1792]{2,1,0:T(8,128)(2,1)S(1)} collective-permute-done((bf16[3,64,1792]{2,1,0:T(8,128)(2,1)S(1)}, bf16[3,64,1792]{2,1,0:T(8,128)(2,1)S(1)}, u32[]{:S(2)}, u32[]{:S(2)}) %collective-permute-start.4) | collective-permute-done | bytes 688160 | tf_op jit(solution)/shard_map/ppermute | solution.py:27
  43.1 1.5 %collective-permute-done.5.refs_3_ = bf16[3,64,1792]{2,1,0:T(8,128)(2,1)S(1)} collective-permute-done((bf16[3,64,1792]{2,1,0:T(8,128)(2,1)S(1)}, bf16[3,64,1792]{2,1,0:T(8,128)(2,1)S(1)}, u32[]{:S(2)}, u32[]{:S(2)}) %collective-permute-start.5) | collective-permute-done | bytes 688160 | tf_op jit(solution)/shard_map/ppermute | solution.py:27
  44.9 1.3 collective-permute-start.6
  46.2 0.8 collective-permute-start.8
  47.1 5.0 %collective-permute-done.7.refs_2_ = bf16[3,64,1792]{2,1,0:T(8,128)(2,1)S(1)} collective-permute-done((bf16[3,64,1792]{2,1,0:T(8,128)(2,1)S(1)}, bf16[3,64,1792]{2,1,0:T(8,128)(2,1)S(1)}, u32[]{:S(2)}, u32[]{:S(2)}) %collective-permute-start.7) | collective-permute-done | bytes 688160 | tf_op jit(solution)/shard_map/ppermute | solution.py:27
  52.0 5.9 %collective-permute-done.6.refs_1_ = bf16[3,64,1792]{2,1,0:T(8,128)(2,1)S(1)} collective-permute-done((bf16[3,64,1792]{2,1,0:T(8,128)(2,1)S(1)}, bf16[3,64,1792]{2,1,0:T(8,128)(2,1)S(1)}, u32[]{:S(2)}, u32[]{:S(2)}) %collective-permute-start.6) | collective-permute-done | bytes 688160 | tf_op jit(solution)/shard_map/ppermute | solution.py:27
  57.9 1.5 %collective-permute-done.8.refs_4_ = bf16[3,64,1792]{2,1,0:T(8,128)(2,1)S(1)} collective-permute-done((bf16[3,64,1792]{2,1,0:T(8,128)(2,1)S(1)}, bf16[3,64,1792]{2,1,0:T(8,128)(2,1)S(1)}, u32[]{:S(2)}, u32[]{:S(2)}) %collective-permute-start.8) | collective-permute-done | bytes 688160 | tf_op jit(solution)/shard_map/ppermute | solution.py:27
  59.4 1.7 %shard_map.90 = (bf16[3,32,1792]{2,1,0:T(8,128)(2,1)S(1)}, bf16[3,32,1792]{2,1,0:T(8,128)(2,1)S(1)}, bf16[3,32,1792]{2,1,0:T(8,128)(2,1)S(1)}, bf16[3,32,1792]{2,1,0:T(8,128)(2,1)S(1)}) custom-call(s32[2]{0:T(128)S(1)} %pad_add_fusion.place, bf16[3,64,1792]{2,1,0:T(8,128)(2,1)S(1)} %get-tuple-element.65.refs_0_, ...), custom_call_target="tpu_custom_call" | custom-call | bytes 4128776 | tf_op jit(solution)/shard_map/pallas_call | solution.py:57
  61.0 3.3 %collective-permute-start.10 = (bf16[3,32,1792]{2,1,0:T(8,128)(2,1)S(1)}, bf16[3,32,1792]{2,1,0:T(8,128)(2,1)S(1)}, u32[]{:S(2)}, u32[]{:S(2)}) collective-permute-start(bf16[3,32,1792]{2,1,0:T(8,128)(2,1)S(1)} %get-tuple-element.78), channel_id=1, source_target_pairs={{0,8},{1,9},{2,10},{3,11},{4,12},{5,13},{6,14},{7,15},{8,0},{9,1},... | collective-permute-start | bytes 1032200 | tf_op jit(solution)/shard_map/ppermute | solution.py:27
  64.3 0.7 collective-permute-start.11
  65.0 2.6 %collective-permute-start.12 = (bf16[3,32,1792]{2,1,0:T(8,128)(2,1)S(1)}, bf16[3,32,1792]{2,1,0:T(8,128)(2,1)S(1)}, u32[]{:S(2)}, u32[]{:S(2)}) collective-permute-start(bf16[3,32,1792]{2,1,0:T(8,128)(2,1)S(1)} %get-tuple-element.80), channel_id=1, source_target_pairs={{0,12},{1,13},{2,14},{3,15},{4,0},{5,1},{6,2},{7,3},{8,4},{9,5},{1... | collective-permute-start | bytes 1032200 | tf_op jit(solution)/shard_map/ppermute | solution.py:27
  67.6 2.4 %collective-permute-done.10.one = bf16[3,32,1792]{2,1,0:T(8,128)(2,1)S(1)} collective-permute-done((bf16[3,32,1792]{2,1,0:T(8,128)(2,1)S(1)}, bf16[3,32,1792]{2,1,0:T(8,128)(2,1)S(1)}, u32[]{:S(2)}, u32[]{:S(2)}) %collective-permute-start.10) | collective-permute-done | bytes 344096 | tf_op jit(solution)/shard_map/ppermute | solution.py:27
  70.0 3.6 %collective-permute-done.11.two = bf16[3,32,1792]{2,1,0:T(8,128)(2,1)S(1)} collective-permute-done((bf16[3,32,1792]{2,1,0:T(8,128)(2,1)S(1)}, bf16[3,32,1792]{2,1,0:T(8,128)(2,1)S(1)}, u32[]{:S(2)}, u32[]{:S(2)}) %collective-permute-start.11) | collective-permute-done | bytes 344096 | tf_op jit(solution)/shard_map/ppermute | solution.py:27
  74.2 2.2 %collective-permute-start.13 = (bf16[3,32,1792]{2,1,0:T(8,128)(2,1)S(1)}, bf16[3,32,1792]{2,1,0:T(8,128)(2,1)S(1)}, u32[]{:S(2)}, u32[]{:S(2)}) collective-permute-start(bf16[3,32,1792]{2,1,0:T(8,128)(2,1)S(1)} %shard_map.91.refs_0_), channel_id=1, source_target_pairs={{0,8},{1,9},{2,10},{3,11},{4,12},{5,13},{6,14},{7,15},{8,0},{9,1},... | collective-permute-start | bytes 1032200 | tf_op jit(solution)/shard_map/ppermute | solution.py:27
  76.3 1.5 %collective-permute-start.14 = (bf16[3,32,1792]{2,1,0:T(8,128)(2,1)S(1)}, bf16[3,32,1792]{2,1,0:T(8,128)(2,1)S(1)}, u32[]{:S(2)}, u32[]{:S(2)}) collective-permute-start(bf16[3,32,1792]{2,1,0:T(8,128)(2,1)S(1)} %shard_map.91.refs_0_), channel_id=1, source_target_pairs={{0,4},{1,5},{2,6},{3,7},{4,8},{5,9},{6,10},{7,11},{8,12},{9,13},{1... | collective-permute-start | bytes 1032200 | tf_op jit(solution)/shard_map/ppermute | solution.py:27
  77.8 1.8 %collective-permute-start.15 = (bf16[3,32,1792]{2,1,0:T(8,128)(2,1)S(1)}, bf16[3,32,1792]{2,1,0:T(8,128)(2,1)S(1)}, u32[]{:S(2)}, u32[]{:S(2)}) collective-permute-start(bf16[3,32,1792]{2,1,0:T(8,128)(2,1)S(1)} %shard_map.91.refs_0_), channel_id=1, source_target_pairs={{0,12},{1,13},{2,14},{3,15},{4,0},{5,1},{6,2},{7,3},{8,4},{9,5},{1... | collective-permute-start | bytes 1032200 | tf_op jit(solution)/shard_map/ppermute | solution.py:27
  79.6 3.5 %collective-permute-done.13.refs_1_ = bf16[3,32,1792]{2,1,0:T(8,128)(2,1)S(1)} collective-permute-done((bf16[3,32,1792]{2,1,0:T(8,128)(2,1)S(1)}, bf16[3,32,1792]{2,1,0:T(8,128)(2,1)S(1)}, u32[]{:S(2)}, u32[]{:S(2)}) %collective-permute-start.13) | collective-permute-done | bytes 344096 | tf_op jit(solution)/shard_map/ppermute | solution.py:27
  83.1 3.6 %collective-permute-done.14.refs_2_ = bf16[3,32,1792]{2,1,0:T(8,128)(2,1)S(1)} collective-permute-done((bf16[3,32,1792]{2,1,0:T(8,128)(2,1)S(1)}, bf16[3,32,1792]{2,1,0:T(8,128)(2,1)S(1)}, u32[]{:S(2)}, u32[]{:S(2)}) %collective-permute-start.14) | collective-permute-done | bytes 344096 | tf_op jit(solution)/shard_map/ppermute | solution.py:27
  86.8 1.3 collective-permute-start.16
  88.1 0.8 collective-permute-start.19
  88.9 1.2 collective-permute-start.17
  90.1 0.8 collective-permute-start.18
  90.9 4.4 %collective-permute-done.16.refs_2_ = bf16[2,64,1792]{2,1,0:T(8,128)(2,1)S(1)} collective-permute-done((bf16[2,64,1792]{2,1,0:T(8,128)(2,1)S(1)}, bf16[2,64,1792]{2,1,0:T(8,128)(2,1)S(1)}, u32[]{:S(2)}, u32[]{:S(2)}) %collective-permute-start.16) | collective-permute-done | bytes 458784 | tf_op jit(solution)/shard_map/ppermute | solution.py:27
  95.4 1.2 collective-permute-start.20
  96.6 0.8 collective-permute-start.21
  97.4 2.9 %collective-permute-done.17.refs_3_ = bf16[2,64,1792]{2,1,0:T(8,128)(2,1)S(1)} collective-permute-done((bf16[2,64,1792]{2,1,0:T(8,128)(2,1)S(1)}, bf16[2,64,1792]{2,1,0:T(8,128)(2,1)S(1)}, u32[]{:S(2)}, u32[]{:S(2)}) %collective-permute-start.17) | collective-permute-done | bytes 458784 | tf_op jit(solution)/shard_map/ppermute | solution.py:27
  100.3 1.2 collective-permute-done.18.refs_4_
  101.5 2.6 %collective-permute-start.23 = (bf16[128,1792]{1,0:T(8,128)(2,1)S(1)}, bf16[128,1792]{1,0:T(8,128)(2,1)S(1)}, u32[]{:S(2)}, u32[]{:S(2)}) collective-permute-start(bf16[128,1792]{1,0:T(8,128)(2,1)S(1)} %get-tuple-element.110.refs_0_), channel_id=1, source_target_pairs={{0,2},{1,3},{2,0},{3,1},{4,6},{5,7},{6,4},{7,5},{8,10},{9,11},{10,... | collective-permute-start | bytes 1376264 | tf_op jit(solution)/shard_map/ppermute | solution.py:27
  104.1 2.0 %collective-permute-start.25 = (bf16[128,1792]{1,0:T(8,128)(2,1)S(1)}, bf16[128,1792]{1,0:T(8,128)(2,1)S(1)}, u32[]{:S(2)}, u32[]{:S(2)}) collective-permute-start(bf16[128,1792]{1,0:T(8,128)(2,1)S(1)} %get-tuple-element.110.refs_0_), channel_id=1, source_target_pairs={{0,3},{1,0},{2,1},{3,2},{4,7},{5,4},{6,5},{7,6},{8,11},{9,8},{10,9... | collective-permute-start | bytes 1376264 | tf_op jit(solution)/shard_map/ppermute | solution.py:27
  106.4 1.8 %shard_map.93 = (bf16[256,512]{1,0:T(8,128)(2,1)S(1)}, bf16[512,1792]{1,0:T(8,128)(2,1)S(1)}, bf16[512,1792]{1,0:T(8,128)(2,1)S(1)}) custom-call(s32[2]{0:T(128)S(1)} %pad_add_fusion.place, bf16[512,1792]{1,0:T(8,128)(2,1)S(1)} %copy-done.1, bf16[512,1792]{1,0:T(8,128)(2,1)S(1)} %copy-done.3, bf16[2,64,1792]{2,1,0:T(8,128)(2,1)S(1)} %get-tuple-element.81.refs_0_, ...), custom_call_target="tpu_custom_call" | custom-call | flops 939524096 | bytes 7340040 | tf_op jit(solution)/shard_map/pallas_call | solution.py:57
  108.2 3.4 %collective-permute-start.22 = (bf16[256,512]{1,0:T(8,128)(2,1)S(1)}, bf16[256,512]{1,0:T(8,128)(2,1)S(1)}, u32[]{:S(2)}, u32[]{:S(2)}) collective-permute-start(bf16[256,512]{1,0:T(8,128)(2,1)S(1)} %get-tuple-element.86), channel_id=1, source_target_pairs={{0,16},{16,0},{32,48},{48,32},{64,80},{80,64},{96,112},{112,96},{1... | collective-permute-start | bytes 786440 | tf_op jit(solution)/shard_map/ppermute | solution.py:45
  111.6 1.1 shard_map.94.keep
  112.8 2.1 %shard_map.95 = (bf16[512,1792]{1,0:T(8,128)(2,1)S(1)}, bf16[512,1792]{1,0:T(8,128)(2,1)S(1)}) custom-call(bf16[256,1024]{1,0:T(8,128)(2,1)S(1)} %shard_map.85.act.low, bf16[256,1024]{1,0:T(8,128)(2,1)S(1)} %collective-permute-done.3.act.high, bf16[512,1792]{1,0:T(8,128)(2,1)S(1)} %get-tuple-element.87.gg, bf16[512,1792]{1,0:T(8,128)(2,1)S(1)} %get-tuple-element.88.ug), custom_call_target="tpu_custom_call" | custom-call | flops 1879048192 | bytes 4718592 | tf_op jit(solution)/shard_map/pallas_call | solution.py:57
  114.9 1.1 collective-permute-done.22.got
  116.1 0.6 collective-permute-done.24.refs_2_
  116.7 0.7 collective-permute-done.25.refs_3_
  117.4 0.5 collective-permute-start.29
  117.9 1.8 %shard_map.100.mine = bf16[1792,512]{1,0:T(8,128)(2,1)S(1)} custom-call(s32[2]{0:T(128)S(1)} %pad_add_fusion.place, bf16[256,1024]{1,0:T(8,128)(2,1)S(1)} %shard_map.85.act.low, bf16[256,1024]{1,0:T(8,128)(2,1)S(1)} %collective-permute-done.3.act.high, bf16[128,1792]{1,0:T(8,128)(2,1)S(1)} %get-tuple-element.110.refs_0_, ...), custom_call_target="tpu_custom_call" | custom-call | flops 939524096 | bytes 2883592 | tf_op jit(solution)/shard_map/pallas_call | solution.py:57
  119.8 1.1 collective-permute-start.26
  120.9 5.2 %collective-permute-start.27 = (bf16[64,512]{1,0:T(8,128)(2,1)S(1)}, bf16[64,512]{1,0:T(8,128)(2,1)S(1)}, u32[]{:S(2)}, u32[]{:S(2)}) collective-permute-start(bf16[64,512]{1,0:T(8,128)(2,1)S(1)} %get-tuple-element.100), channel_id=1, source_target_pairs={{0,64},{16,80},{32,96},{48,112},{64,0},{80,16},{96,32},{112,48},{1... | collective-permute-start | bytes 196616 | tf_op jit(solution)/shard_map/ppermute | solution.py:36
  126.1 1.3 collective-permute-start.28
  127.4 1.3 shard_map.98
  128.8 1.3 shard_map.97
  130.2 3.1 %collective-permute-done.28.refs_3_ = bf16[64,512]{1,0:T(8,128)(2,1)S(1)} collective-permute-done((bf16[64,512]{1,0:T(8,128)(2,1)S(1)}, bf16[64,512]{1,0:T(8,128)(2,1)S(1)}, u32[]{:S(2)}, u32[]{:S(2)}) %collective-permute-start.28) | collective-permute-done | bytes 65568 | tf_op jit(solution)/shard_map/ppermute | solution.py:36
  133.3 0.7 shard_map.99
  133.9 1.3 shard_map.101
  (35 shorter events, 1.6 us)
Async XLA Ops:
  0.6 0.8 copy-start.6
  1.5 0.8 copy-start.7
  2.3 16.2 %collective-permute-start = (bf16[64,1024]{1,0:T(8,128)(2,1)S(1)}, bf16[64,1024]{1,0:T(8,128)(2,1)S(1)}, u32[]{:S(2)}, u32[]{:S(2)}) collective-permute-start(bf16[64,1024]{1,0:T(8,128)(2,1)S(1)} %shard_map.84.refs_0_), channel_id=1, source_target_pairs={{0,96},{16,112},{32,0},{48,16},{64,32},{80,48},{96,64},{112,80},{1... | collective-permute-start | bytes 393224 | tf_op jit(solution)/shard_map/ppermute | solution.py:36
  8.7 11.1 %collective-permute-start.1 = (bf16[64,1024]{1,0:T(8,128)(2,1)S(1)}, bf16[64,1024]{1,0:T(8,128)(2,1)S(1)}, u32[]{:S(2)}, u32[]{:S(2)}) collective-permute-start(bf16[64,1024]{1,0:T(8,128)(2,1)S(1)} %shard_map.84.refs_0_), channel_id=1, source_target_pairs={{0,64},{16,80},{32,96},{48,112},{64,0},{80,16},{96,32},{112,48},{1... | collective-permute-start | bytes 393224 | tf_op jit(solution)/shard_map/ppermute | solution.py:36
  9.7 10.1 %collective-permute-start.2 = (bf16[64,1024]{1,0:T(8,128)(2,1)S(1)}, bf16[64,1024]{1,0:T(8,128)(2,1)S(1)}, u32[]{:S(2)}, u32[]{:S(2)}) collective-permute-start(bf16[64,1024]{1,0:T(8,128)(2,1)S(1)} %shard_map.84.refs_0_), channel_id=1, source_target_pairs={{0,32},{16,48},{32,64},{48,80},{64,96},{80,112},{96,0},{112,16},{1... | collective-permute-start | bytes 393224 | tf_op jit(solution)/shard_map/ppermute | solution.py:36
  19.8 10.5 %collective-permute-start.3 = (bf16[256,1024]{1,0:T(8,128)(2,1)S(1)}, bf16[256,1024]{1,0:T(8,128)(2,1)S(1)}, u32[]{:S(2)}, u32[]{:S(2)}) collective-permute-start(bf16[256,1024]{1,0:T(8,128)(2,1)S(1)} %shard_map.85.act.low), channel_id=1, source_target_pairs={{0,16},{16,0},{32,48},{48,32},{64,80},{80,64},{96,112},{112,96},{1... | collective-permute-start | bytes 1572872 | tf_op jit(solution)/shard_map/ppermute | solution.py:45
  23.2 1.5 %copy-start = (bf16[512,1792]{1,0:T(8,128)(2,1)S(1)}, bf16[512,1792]{1,0:T(8,128)(2,1)}, u32[]{:S(2)}) copy-start(bf16[512,1792]{1,0:T(8,128)(2,1)} %gate.9) | copy-start | bytes 5505028
  24.7 1.5 %copy-start.2 = (bf16[512,1792]{1,0:T(8,128)(2,1)S(1)}, bf16[512,1792]{1,0:T(8,128)(2,1)}, u32[]{:S(2)}) copy-start(bf16[512,1792]{1,0:T(8,128)(2,1)} %up.9) | copy-start | bytes 5505028
  26.2 1.5 %copy-start.4 = (bf16[1792,512]{1,0:T(8,128)(2,1)S(1)}, bf16[1792,512]{1,0:T(8,128)(2,1)}, u32[]{:S(2)}) copy-start(bf16[1792,512]{1,0:T(8,128)(2,1)} %down.5) | copy-start | bytes 5505028
  27.7 2.6 %copy-start.1 = (bf16[512,1792]{1,0:T(8,128)(2,1)S(1)}, bf16[512,1792]{1,0:T(8,128)(2,1)}, u32[]{:S(2)}) copy-start(bf16[512,1792]{1,0:T(8,128)(2,1)} %gate.9) | copy-start | bytes 5505028
  27.7 2.6 %copy-start.3 = (bf16[512,1792]{1,0:T(8,128)(2,1)S(1)}, bf16[512,1792]{1,0:T(8,128)(2,1)}, u32[]{:S(2)}) copy-start(bf16[512,1792]{1,0:T(8,128)(2,1)} %up.9) | copy-start | bytes 5505028
  27.7 2.6 %copy-start.5 = (bf16[1792,512]{1,0:T(8,128)(2,1)S(1)}, bf16[1792,512]{1,0:T(8,128)(2,1)}, u32[]{:S(2)}) copy-start(bf16[1792,512]{1,0:T(8,128)(2,1)} %down.5) | copy-start | bytes 5505028
  32.1 11.0 %collective-permute-start.4 = (bf16[3,64,1792]{2,1,0:T(8,128)(2,1)S(1)}, bf16[3,64,1792]{2,1,0:T(8,128)(2,1)S(1)}, u32[]{:S(2)}, u32[]{:S(2)}) collective-permute-start(bf16[3,64,1792]{2,1,0:T(8,128)(2,1)S(1)} %get-tuple-element.70), channel_id=1, source_target_pairs={{0,1},{1,2},{2,3},{3,0},{4,5},{5,6},{6,7},{7,4},{8,9},{9,10},{10,1... | collective-permute-start | bytes 2064392 | tf_op jit(solution)/shard_map/ppermute | solution.py:27
  33.7 10.9 %collective-permute-start.5 = (bf16[3,64,1792]{2,1,0:T(8,128)(2,1)S(1)}, bf16[3,64,1792]{2,1,0:T(8,128)(2,1)S(1)}, u32[]{:S(2)}, u32[]{:S(2)}) collective-permute-start(bf16[3,64,1792]{2,1,0:T(8,128)(2,1)S(1)} %get-tuple-element.71), channel_id=1, source_target_pairs={{0,3},{1,0},{2,1},{3,2},{4,7},{5,4},{6,5},{7,6},{8,11},{9,8},{10,9... | collective-permute-start | bytes 2064392 | tf_op jit(solution)/shard_map/ppermute | solution.py:27
  36.3 15.7 %collective-permute-start.7 = (bf16[3,64,1792]{2,1,0:T(8,128)(2,1)S(1)}, bf16[3,64,1792]{2,1,0:T(8,128)(2,1)S(1)}, u32[]{:S(2)}, u32[]{:S(2)}) collective-permute-start(bf16[3,64,1792]{2,1,0:T(8,128)(2,1)S(1)} %get-tuple-element.73), channel_id=1, source_target_pairs={{0,3},{1,0},{2,1},{3,2},{4,7},{5,4},{6,5},{7,6},{8,11},{9,8},{10,9... | collective-permute-start | bytes 2064392 | tf_op jit(solution)/shard_map/ppermute | solution.py:27
  38.5 13.5 %collective-permute-start.9 = (bf16[3,64,1792]{2,1,0:T(8,128)(2,1)S(1)}, bf16[3,64,1792]{2,1,0:T(8,128)(2,1)S(1)}, u32[]{:S(2)}, u32[]{:S(2)}) collective-permute-start(bf16[3,64,1792]{2,1,0:T(8,128)(2,1)S(1)} %get-tuple-element.76), channel_id=1, source_target_pairs={{0,1},{1,2},{2,3},{3,0},{4,5},{5,6},{6,7},{7,4},{8,9},{9,10},{10,1... | collective-permute-start | bytes 2064392 | tf_op jit(solution)/shard_map/ppermute | solution.py:27
  44.9 12.9 %collective-permute-start.6 = (bf16[3,64,1792]{2,1,0:T(8,128)(2,1)S(1)}, bf16[3,64,1792]{2,1,0:T(8,128)(2,1)S(1)}, u32[]{:S(2)}, u32[]{:S(2)}) collective-permute-start(bf16[3,64,1792]{2,1,0:T(8,128)(2,1)S(1)} %get-tuple-element.72), channel_id=1, source_target_pairs={{0,1},{1,2},{2,3},{3,0},{4,5},{5,6},{6,7},{7,4},{8,9},{9,10},{10,1... | collective-permute-start | bytes 2064392 | tf_op jit(solution)/shard_map/ppermute | solution.py:27
  46.2 13.2 %collective-permute-start.8 = (bf16[3,64,1792]{2,1,0:T(8,128)(2,1)S(1)}, bf16[3,64,1792]{2,1,0:T(8,128)(2,1)S(1)}, u32[]{:S(2)}, u32[]{:S(2)}) collective-permute-start(bf16[3,64,1792]{2,1,0:T(8,128)(2,1)S(1)} %get-tuple-element.75), channel_id=1, source_target_pairs={{0,3},{1,0},{2,1},{3,2},{4,7},{5,4},{6,5},{7,6},{8,11},{9,8},{10,9... | collective-permute-start | bytes 2064392 | tf_op jit(solution)/shard_map/ppermute | solution.py:27
  61.0 8.9 %collective-permute-start.10 = (bf16[3,32,1792]{2,1,0:T(8,128)(2,1)S(1)}, bf16[3,32,1792]{2,1,0:T(8,128)(2,1)S(1)}, u32[]{:S(2)}, u32[]{:S(2)}) collective-permute-start(bf16[3,32,1792]{2,1,0:T(8,128)(2,1)S(1)} %get-tuple-element.78), channel_id=1, source_target_pairs={{0,8},{1,9},{2,10},{3,11},{4,12},{5,13},{6,14},{7,15},{8,0},{9,1},... | collective-permute-start | bytes 1032200 | tf_op jit(solution)/shard_map/ppermute | solution.py:27
  64.3 9.2 %collective-permute-start.11 = (bf16[3,32,1792]{2,1,0:T(8,128)(2,1)S(1)}, bf16[3,32,1792]{2,1,0:T(8,128)(2,1)S(1)}, u32[]{:S(2)}, u32[]{:S(2)}) collective-permute-start(bf16[3,32,1792]{2,1,0:T(8,128)(2,1)S(1)} %get-tuple-element.79), channel_id=1, source_target_pairs={{0,4},{1,5},{2,6},{3,7},{4,8},{5,9},{6,10},{7,11},{8,12},{9,13},{1... | collective-permute-start | bytes 1032200 | tf_op jit(solution)/shard_map/ppermute | solution.py:27
  65.0 8.9 %collective-permute-start.12 = (bf16[3,32,1792]{2,1,0:T(8,128)(2,1)S(1)}, bf16[3,32,1792]{2,1,0:T(8,128)(2,1)S(1)}, u32[]{:S(2)}, u32[]{:S(2)}) collective-permute-start(bf16[3,32,1792]{2,1,0:T(8,128)(2,1)S(1)} %get-tuple-element.80), channel_id=1, source_target_pairs={{0,12},{1,13},{2,14},{3,15},{4,0},{5,1},{6,2},{7,3},{8,4},{9,5},{1... | collective-permute-start | bytes 1032200 | tf_op jit(solution)/shard_map/ppermute | solution.py:27
  74.2 8.9 %collective-permute-start.13 = (bf16[3,32,1792]{2,1,0:T(8,128)(2,1)S(1)}, bf16[3,32,1792]{2,1,0:T(8,128)(2,1)S(1)}, u32[]{:S(2)}, u32[]{:S(2)}) collective-permute-start(bf16[3,32,1792]{2,1,0:T(8,128)(2,1)S(1)} %shard_map.91.refs_0_), channel_id=1, source_target_pairs={{0,8},{1,9},{2,10},{3,11},{4,12},{5,13},{6,14},{7,15},{8,0},{9,1},... | collective-permute-start | bytes 1032200 | tf_op jit(solution)/shard_map/ppermute | solution.py:27
  76.3 10.4 %collective-permute-start.14 = (bf16[3,32,1792]{2,1,0:T(8,128)(2,1)S(1)}, bf16[3,32,1792]{2,1,0:T(8,128)(2,1)S(1)}, u32[]{:S(2)}, u32[]{:S(2)}) collective-permute-start(bf16[3,32,1792]{2,1,0:T(8,128)(2,1)S(1)} %shard_map.91.refs_0_), channel_id=1, source_target_pairs={{0,4},{1,5},{2,6},{3,7},{4,8},{5,9},{6,10},{7,11},{8,12},{9,13},{1... | collective-permute-start | bytes 1032200 | tf_op jit(solution)/shard_map/ppermute | solution.py:27
  77.8 8.9 %collective-permute-start.15 = (bf16[3,32,1792]{2,1,0:T(8,128)(2,1)S(1)}, bf16[3,32,1792]{2,1,0:T(8,128)(2,1)S(1)}, u32[]{:S(2)}, u32[]{:S(2)}) collective-permute-start(bf16[3,32,1792]{2,1,0:T(8,128)(2,1)S(1)} %shard_map.91.refs_0_), channel_id=1, source_target_pairs={{0,12},{1,13},{2,14},{3,15},{4,0},{5,1},{6,2},{7,3},{8,4},{9,5},{1... | collective-permute-start | bytes 1032200 | tf_op jit(solution)/shard_map/ppermute | solution.py:27
  86.8 8.6 %collective-permute-start.16 = (bf16[2,64,1792]{2,1,0:T(8,128)(2,1)S(1)}, bf16[2,64,1792]{2,1,0:T(8,128)(2,1)S(1)}, u32[]{:S(2)}, u32[]{:S(2)}) collective-permute-start(bf16[2,64,1792]{2,1,0:T(8,128)(2,1)S(1)} %get-tuple-element.81.refs_0_), channel_id=1, source_target_pairs={{0,1},{1,2},{2,3},{3,0},{4,5},{5,6},{6,7},{7,4},{8,9},{9,10},{10,1... | collective-permute-start | bytes 1376264 | tf_op jit(solution)/shard_map/ppermute | solution.py:27
  88.1 8.5 %collective-permute-start.19 = (bf16[2,64,1792]{2,1,0:T(8,128)(2,1)S(1)}, bf16[2,64,1792]{2,1,0:T(8,128)(2,1)S(1)}, u32[]{:S(2)}, u32[]{:S(2)}) collective-permute-start(bf16[2,64,1792]{2,1,0:T(8,128)(2,1)S(1)} %get-tuple-element.82.refs_1_), channel_id=1, source_target_pairs={{0,3},{1,0},{2,1},{3,2},{4,7},{5,4},{6,5},{7,6},{8,11},{9,8},{10,9... | collective-permute-start | bytes 1376264 | tf_op jit(solution)/shard_map/ppermute | solution.py:27
  88.9 11.4 %collective-permute-start.17 = (bf16[2,64,1792]{2,1,0:T(8,128)(2,1)S(1)}, bf16[2,64,1792]{2,1,0:T(8,128)(2,1)S(1)}, u32[]{:S(2)}, u32[]{:S(2)}) collective-permute-start(bf16[2,64,1792]{2,1,0:T(8,128)(2,1)S(1)} %get-tuple-element.82.refs_1_), channel_id=1, source_target_pairs={{0,1},{1,2},{2,3},{3,0},{4,5},{5,6},{6,7},{7,4},{8,9},{9,10},{10,1... | collective-permute-start | bytes 1376264 | tf_op jit(solution)/shard_map/ppermute | solution.py:27
  90.1 11.4 %collective-permute-start.18 = (bf16[2,64,1792]{2,1,0:T(8,128)(2,1)S(1)}, bf16[2,64,1792]{2,1,0:T(8,128)(2,1)S(1)}, u32[]{:S(2)}, u32[]{:S(2)}) collective-permute-start(bf16[2,64,1792]{2,1,0:T(8,128)(2,1)S(1)} %get-tuple-element.81.refs_0_), channel_id=1, source_target_pairs={{0,3},{1,0},{2,1},{3,2},{4,7},{5,4},{6,5},{7,6},{8,11},{9,8},{10,9... | collective-permute-start | bytes 1376264 | tf_op jit(solution)/shard_map/ppermute | solution.py:27
  95.4 10.8 %collective-permute-start.20 = (bf16[2,64,1792]{2,1,0:T(8,128)(2,1)S(1)}, bf16[2,64,1792]{2,1,0:T(8,128)(2,1)S(1)}, u32[]{:S(2)}, u32[]{:S(2)}) collective-permute-start(bf16[2,64,1792]{2,1,0:T(8,128)(2,1)S(1)} %collective-permute-done.16.refs_2_), channel_id=1, source_target_pairs={{0,1},{1,2},{2,3},{3,0},{4,5},{5,6},{6,7},{7,4},{8,9},{9,10},{10,1... | collective-permute-start | bytes 1376264 | tf_op jit(solution)/shard_map/ppermute | solution.py:27
  96.6 9.8 %collective-permute-start.21 = (bf16[2,64,1792]{2,1,0:T(8,128)(2,1)S(1)}, bf16[2,64,1792]{2,1,0:T(8,128)(2,1)S(1)}, u32[]{:S(2)}, u32[]{:S(2)}) collective-permute-start(bf16[2,64,1792]{2,1,0:T(8,128)(2,1)S(1)} %collective-permute-done.19.refs_5_), channel_id=1, source_target_pairs={{0,3},{1,0},{2,1},{3,2},{4,7},{5,4},{6,5},{7,6},{8,11},{9,8},{10,9... | collective-permute-start | bytes 1376264 | tf_op jit(solution)/shard_map/ppermute | solution.py:27
  101.5 14.6 %collective-permute-start.23 = (bf16[128,1792]{1,0:T(8,128)(2,1)S(1)}, bf16[128,1792]{1,0:T(8,128)(2,1)S(1)}, u32[]{:S(2)}, u32[]{:S(2)}) collective-permute-start(bf16[128,1792]{1,0:T(8,128)(2,1)S(1)} %get-tuple-element.110.refs_0_), channel_id=1, source_target_pairs={{0,2},{1,3},{2,0},{3,1},{4,6},{5,7},{6,4},{7,5},{8,10},{9,11},{10,... | collective-permute-start | bytes 1376264 | tf_op jit(solution)/shard_map/ppermute | solution.py:27
  104.1 12.6 %collective-permute-start.24 = (bf16[128,1792]{1,0:T(8,128)(2,1)S(1)}, bf16[128,1792]{1,0:T(8,128)(2,1)S(1)}, u32[]{:S(2)}, u32[]{:S(2)}) collective-permute-start(bf16[128,1792]{1,0:T(8,128)(2,1)S(1)} %get-tuple-element.110.refs_0_), channel_id=1, source_target_pairs={{0,1},{1,2},{2,3},{3,0},{4,5},{5,6},{6,7},{7,4},{8,9},{9,10},{10,1... | collective-permute-start | bytes 1376264 | tf_op jit(solution)/shard_map/ppermute | solution.py:27
  104.1 13.3 %collective-permute-start.25 = (bf16[128,1792]{1,0:T(8,128)(2,1)S(1)}, bf16[128,1792]{1,0:T(8,128)(2,1)S(1)}, u32[]{:S(2)}, u32[]{:S(2)}) collective-permute-start(bf16[128,1792]{1,0:T(8,128)(2,1)S(1)} %get-tuple-element.110.refs_0_), channel_id=1, source_target_pairs={{0,3},{1,0},{2,1},{3,2},{4,7},{5,4},{6,5},{7,6},{8,11},{9,8},{10,9... | collective-permute-start | bytes 1376264 | tf_op jit(solution)/shard_map/ppermute | solution.py:27
  108.2 7.8 %collective-permute-start.22 = (bf16[256,512]{1,0:T(8,128)(2,1)S(1)}, bf16[256,512]{1,0:T(8,128)(2,1)S(1)}, u32[]{:S(2)}, u32[]{:S(2)}) collective-permute-start(bf16[256,512]{1,0:T(8,128)(2,1)S(1)} %get-tuple-element.86), channel_id=1, source_target_pairs={{0,16},{16,0},{32,48},{48,32},{64,80},{80,64},{96,112},{112,96},{1... | collective-permute-start | bytes 786440 | tf_op jit(solution)/shard_map/ppermute | solution.py:45
  117.4 8.8 %collective-permute-start.30 = (bf16[512,1792]{1,0:T(8,128)(2,1)S(1)}, bf16[512,1792]{1,0:T(8,128)(2,1)S(1)}, u32[]{:S(2)}, u32[]{:S(2)}) collective-permute-start(bf16[512,1792]{1,0:T(8,128)(2,1)S(1)} %get-tuple-element.103.mine), channel_id=1, source_target_pairs={{0,128},{128,0},{1,129},{129,1},{2,130},{130,2},{3,131},{131,3},{4... | collective-permute-start | bytes 5505032 | tf_op jit(solution)/shard_map/ppermute | solution.py:49
  117.4 11.4 %collective-permute-start.29 = (bf16[512,1792]{1,0:T(8,128)(2,1)S(1)}, bf16[512,1792]{1,0:T(8,128)(2,1)S(1)}, u32[]{:S(2)}, u32[]{:S(2)}) collective-permute-start(bf16[512,1792]{1,0:T(8,128)(2,1)S(1)} %get-tuple-element.102.mine), channel_id=1, source_target_pairs={{0,128},{128,0},{1,129},{129,1},{2,130},{130,2},{3,131},{131,3},{4... | collective-permute-start | bytes 5505032 | tf_op jit(solution)/shard_map/ppermute | solution.py:49
  119.7 14.2 %collective-permute-start.31 = (bf16[1792,512]{1,0:T(8,128)(2,1)S(1)}, bf16[1792,512]{1,0:T(8,128)(2,1)S(1)}, u32[]{:S(2)}, u32[]{:S(2)}) collective-permute-start(bf16[1792,512]{1,0:T(8,128)(2,1)S(1)} %shard_map.100.mine), channel_id=1, source_target_pairs={{0,128},{128,0},{1,129},{129,1},{2,130},{130,2},{3,131},{131,3},{4... | collective-permute-start | bytes 5505032 | tf_op jit(solution)/shard_map/ppermute | solution.py:49
  119.8 10.3 %collective-permute-start.26 = (bf16[64,512]{1,0:T(8,128)(2,1)S(1)}, bf16[64,512]{1,0:T(8,128)(2,1)S(1)}, u32[]{:S(2)}, u32[]{:S(2)}) collective-permute-start(bf16[64,512]{1,0:T(8,128)(2,1)S(1)} %get-tuple-element.99), channel_id=1, source_target_pairs={{0,32},{16,48},{32,64},{48,80},{64,96},{80,112},{96,0},{112,16},{1... | collective-permute-start | bytes 196616 | tf_op jit(solution)/shard_map/ppermute | solution.py:36
  120.9 9.2 %collective-permute-start.27 = (bf16[64,512]{1,0:T(8,128)(2,1)S(1)}, bf16[64,512]{1,0:T(8,128)(2,1)S(1)}, u32[]{:S(2)}, u32[]{:S(2)}) collective-permute-start(bf16[64,512]{1,0:T(8,128)(2,1)S(1)} %get-tuple-element.100), channel_id=1, source_target_pairs={{0,64},{16,80},{32,96},{48,112},{64,0},{80,16},{96,32},{112,48},{1... | collective-permute-start | bytes 196616 | tf_op jit(solution)/shard_map/ppermute | solution.py:36
  126.1 7.2 %collective-permute-start.28 = (bf16[64,512]{1,0:T(8,128)(2,1)S(1)}, bf16[64,512]{1,0:T(8,128)(2,1)S(1)}, u32[]{:S(2)}, u32[]{:S(2)}) collective-permute-start(bf16[64,512]{1,0:T(8,128)(2,1)S(1)} %get-tuple-element.101), channel_id=1, source_target_pairs={{0,96},{16,112},{32,0},{48,16},{64,32},{80,48},{96,64},{112,80},{1... | collective-permute-start | bytes 196616 | tf_op jit(solution)/shard_map/ppermute | solution.py:36

commit v5 on v4

--- a/solution.py
+++ b/solution.py
@@ -247,7 +247,8 @@
     place = jnp.stack([here, other]).astype(jnp.int32)
 
     mine = call(pack_kernel, [((count, 2 * width), BF16)], (tokens, cotangent))[0]
-    evens = [mine] + [send_row(mine, -2 * i) for i in range(1, 4)]
+    evens = {i: send_row(mine, -2 * i) for i in STEPS}
+    evens = (mine, evens[1], evens[2], evens[3])
     even = call(bundle_kernel, [((4 * count, 2 * width), BF16)], evens)[0]
     odd = swap_row(even)
 
@@ -320,7 +321,7 @@
         scratch=[lhs, whole],
         flops=work,
     )[0]
-    got = [sums[0]] + [send_row(sums[i], 2 * i) for i in range(1, 4)]
+    got = [sums[0]] + [send_row(sums[i], 2 * i) for i in STEPS]
     got, outs = lax.optimization_barrier((got, outs))
     input_grad = call(sum_kernel, [block], got)[0]
     outs = list(outs) + [merge(down_term)]

time: 136 us -> 136 us (level)
  transfers between devices with their start and end apart: 32 -> 32, of which waited for: 21 -> 22; matrix products, arithmetic and copies ran while one was open for 0% -> 0% of each run, Pallas kernels for 11% -> 11%
where the time goes in v5:
time: 136 us; the launch traced here: 135 us
  starting transfers between devices  54.2 us (40%)
  waiting for transfers between devices  53.8 us (40%)
  Pallas kernels  20.1 us (15%)
  local copies, waits for them, and re-layouts  6.19 us (5%)
    ppermute x21, waiting for transfers between devices, send_col(): return lax.ppermute(value, ('dp', 'col'), pairs)  42 us
    ppermute x21, starting transfers between devices, send_col(): return lax.ppermute(value, ('dp', 'col'), pairs)  29.1 us
    ppermute x6, starting transfers between devices, send_row(): return lax.ppermute(value, ('dp', 'row'), pairs)  17.8 us
    pallas_call x15, Pallas kernels, call(): pl.pallas_call(kernel, out_shape=[jax.ShapeDtypeStruct(shape, kind) for s...  16.1 us
    ppermute x6, waiting for transfers between devices, send_row(): return lax.ppermute(value, ('dp', 'row'), pairs)  10.3 us
    ppermute x2, starting transfers between devices, swap_row(): return lax.ppermute(value, ('dp', 'row'), pairs)  6.7 us
    unnamed x16, local copies, waits for them, and re-layouts  6.19 us
    pallas_call x3, Pallas kernels, merge(): pl.pallas_call(merge_kernel, out_shape=jax.ShapeDtypeStruct(term.shape, B...  4.02 us
  transfers between devices with their start and end apart: 32, of which 22 were waited for; matrix products, arithmetic and copies ran while one was open for 0% of the time, Pallas kernels for 11%

profile of v5, /device:TPU:2, one launch (start us, length us, event | category | flops | bytes accessed | tf_op | source)
XLA Modules:
  0.0 135.4 jit_solution(10799779640906635584)
XLA Ops:
  0.6 0.8 copy-done.6
  1.5 0.8 copy-done.7
  2.3 6.4 %collective-permute-start = (bf16[64,1024]{1,0:T(8,128)(2,1)S(1)}, bf16[64,1024]{1,0:T(8,128)(2,1)S(1)}, u32[]{:S(2)}, u32[]{:S(2)}) collective-permute-start(bf16[64,1024]{1,0:T(8,128)(2,1)S(1)} %shard_map.84.refs_0_), channel_id=1, source_target_pairs={{0,96},{16,112},{32,0},{48,16},{64,32},{80,48},{96,64},{112,80},{1... | collective-permute-start | bytes 393224 | tf_op jit(solution)/shard_map/ppermute | solution.py:36
  8.7 1.0 collective-permute-start.1
  9.7 2.8 %collective-permute-start.2 = (bf16[64,1024]{1,0:T(8,128)(2,1)S(1)}, bf16[64,1024]{1,0:T(8,128)(2,1)S(1)}, u32[]{:S(2)}, u32[]{:S(2)}) collective-permute-start(bf16[64,1024]{1,0:T(8,128)(2,1)S(1)} %shard_map.84.refs_0_), channel_id=1, source_target_pairs={{0,32},{16,48},{32,64},{48,80},{64,96},{80,112},{96,0},{112,16},{1... | collective-permute-start | bytes 393224 | tf_op jit(solution)/shard_map/ppermute | solution.py:36
  12.5 6.0 %collective-permute-done.refs_1_ = bf16[64,1024]{1,0:T(8,128)(2,1)S(1)} collective-permute-done((bf16[64,1024]{1,0:T(8,128)(2,1)S(1)}, bf16[64,1024]{1,0:T(8,128)(2,1)S(1)}, u32[]{:S(2)}, u32[]{:S(2)}) %collective-permute-start) | collective-permute-done | bytes 131104 | tf_op jit(solution)/shard_map/ppermute | solution.py:36
  18.5 1.2 collective-permute-done.1.refs_2_
  19.8 3.3 %collective-permute-start.3 = (bf16[256,1024]{1,0:T(8,128)(2,1)S(1)}, bf16[256,1024]{1,0:T(8,128)(2,1)S(1)}, u32[]{:S(2)}, u32[]{:S(2)}) collective-permute-start(bf16[256,1024]{1,0:T(8,128)(2,1)S(1)} %shard_map.85.act.low), channel_id=1, source_target_pairs={{0,16},{16,0},{32,48},{48,32},{64,80},{80,64},{96,112},{112,96},{1... | collective-permute-start | bytes 1572872 | tf_op jit(solution)/shard_map/ppermute | solution.py:45
  23.2 1.5 %copy-done = bf16[512,1792]{1,0:T(8,128)(2,1)S(1)} copy-done((bf16[512,1792]{1,0:T(8,128)(2,1)S(1)}, bf16[512,1792]{1,0:T(8,128)(2,1)}, u32[]{:S(2)}) %copy-start) | copy-done | bytes 1835032
  24.7 1.5 %copy-done.2 = bf16[512,1792]{1,0:T(8,128)(2,1)S(1)} copy-done((bf16[512,1792]{1,0:T(8,128)(2,1)S(1)}, bf16[512,1792]{1,0:T(8,128)(2,1)}, u32[]{:S(2)}) %copy-start.2) | copy-done | bytes 1835032
  26.2 1.5 %copy-done.4 = bf16[1792,512]{1,0:T(8,128)(2,1)S(1)} copy-done((bf16[1792,512]{1,0:T(8,128)(2,1)S(1)}, bf16[1792,512]{1,0:T(8,128)(2,1)}, u32[]{:S(2)}) %copy-start.4) | copy-done | bytes 1835032
  27.7 2.1 %shard_map.86 = (bf16[3,32,1792]{2,1,0:T(8,128)(2,1)S(1)}, bf16[3,32,1792]{2,1,0:T(8,128)(2,1)S(1)}, bf16[3,32,1792]{2,1,0:T(8,128)(2,1)S(1)}, bf16[3,32,1792]{2...) custom-call(s32[2]{0:T(128)S(1)} %pad_add_fusion.place, ...), custom_call_target="tpu_custom_call" | custom-call | flops 1409286144 | bytes 6029320 | tf_op jit(solution)/shard_map/pallas_call | solution.py:57
  30.3 1.9 %shard_map.88 = (bf16[3,64,1792]{2,1,0:T(8,128)(2,1)S(1)}, bf16[3,64,1792]{2,1,0:T(8,128)(2,1)S(1)}) custom-call(s32[2]{0:T(128)S(1)} %pad_add_fusion.place, bf16[256,1024]{1,0:T(8,128)(2,1)S(1)} %collective-permute-done.3.act.high, bf16[512,1792]{1,0:T(8,128)(2,1)S(1)} %copy-done.1, bf16[512,1792]{1,0:T(8,128)(2,1)S(1)} %copy-done.3, ...), custom_call_target="tpu_custom_call" | custom-call | flops 352321536 | bytes 6717448 | tf_op jit(solution)/shard_map/pallas_call | solution.py:57
  32.1 1.6 %collective-permute-start.4 = (bf16[3,64,1792]{2,1,0:T(8,128)(2,1)S(1)}, bf16[3,64,1792]{2,1,0:T(8,128)(2,1)S(1)}, u32[]{:S(2)}, u32[]{:S(2)}) collective-permute-start(bf16[3,64,1792]{2,1,0:T(8,128)(2,1)S(1)} %get-tuple-element.70), channel_id=1, source_target_pairs={{0,1},{1,2},{2,3},{3,0},{4,5},{5,6},{6,7},{7,4},{8,9},{9,10},{10,1... | collective-permute-start | bytes 2064392 | tf_op jit(solution)/shard_map/ppermute | solution.py:27
  33.7 0.5 collective-permute-start.5
  34.2 2.1 %shard_map.87 = (bf16[3,64,1792]{2,1,0:T(8,128)(2,1)S(1)}, bf16[3,64,1792]{2,1,0:T(8,128)(2,1)S(1)}, bf16[3,64,1792]{2,1,0:T(8,128)(2,1)S(1)}, bf16[3,64,1792]{2...) custom-call(s32[2]{0:T(128)S(1)} %pad_add_fusion.place, ...), custom_call_target="tpu_custom_call" | custom-call | flops 1056964608 | bytes 8093704 | tf_op jit(solution)/shard_map/pallas_call | solution.py:57
  36.3 2.2 %collective-permute-start.7 = (bf16[3,64,1792]{2,1,0:T(8,128)(2,1)S(1)}, bf16[3,64,1792]{2,1,0:T(8,128)(2,1)S(1)}, u32[]{:S(2)}, u32[]{:S(2)}) collective-permute-start(bf16[3,64,1792]{2,1,0:T(8,128)(2,1)S(1)} %get-tuple-element.73), channel_id=1, source_target_pairs={{0,3},{1,0},{2,1},{3,2},{4,7},{5,4},{6,5},{7,6},{8,11},{9,8},{10,9... | collective-permute-start | bytes 2064392 | tf_op jit(solution)/shard_map/ppermute | solution.py:27
  38.5 4.7 %collective-permute-done.4.refs_2_ = bf16[3,64,1792]{2,1,0:T(8,128)(2,1)S(1)} collective-permute-done((bf16[3,64,1792]{2,1,0:T(8,128)(2,1)S(1)}, bf16[3,64,1792]{2,1,0:T(8,128)(2,1)S(1)}, u32[]{:S(2)}, u32[]{:S(2)}) %collective-permute-start.4) | collective-permute-done | bytes 688160 | tf_op jit(solution)/shard_map/ppermute | solution.py:27
  43.1 1.5 %collective-permute-done.5.refs_3_ = bf16[3,64,1792]{2,1,0:T(8,128)(2,1)S(1)} collective-permute-done((bf16[3,64,1792]{2,1,0:T(8,128)(2,1)S(1)}, bf16[3,64,1792]{2,1,0:T(8,128)(2,1)S(1)}, u32[]{:S(2)}, u32[]{:S(2)}) %collective-permute-start.5) | collective-permute-done | bytes 688160 | tf_op jit(solution)/shard_map/ppermute | solution.py:27
  44.9 1.3 collective-permute-start.6
  46.2 0.8 collective-permute-start.8
  47.1 5.0 %collective-permute-done.7.refs_2_ = bf16[3,64,1792]{2,1,0:T(8,128)(2,1)S(1)} collective-permute-done((bf16[3,64,1792]{2,1,0:T(8,128)(2,1)S(1)}, bf16[3,64,1792]{2,1,0:T(8,128)(2,1)S(1)}, u32[]{:S(2)}, u32[]{:S(2)}) %collective-permute-start.7) | collective-permute-done | bytes 688160 | tf_op jit(solution)/shard_map/ppermute | solution.py:27
  52.0 5.9 %collective-permute-done.6.refs_1_ = bf16[3,64,1792]{2,1,0:T(8,128)(2,1)S(1)} collective-permute-done((bf16[3,64,1792]{2,1,0:T(8,128)(2,1)S(1)}, bf16[3,64,1792]{2,1,0:T(8,128)(2,1)S(1)}, u32[]{:S(2)}, u32[]{:S(2)}) %collective-permute-start.6) | collective-permute-done | bytes 688160 | tf_op jit(solution)/shard_map/ppermute | solution.py:27
  57.9 1.5 %collective-permute-done.8.refs_4_ = bf16[3,64,1792]{2,1,0:T(8,128)(2,1)S(1)} collective-permute-done((bf16[3,64,1792]{2,1,0:T(8,128)(2,1)S(1)}, bf16[3,64,1792]{2,1,0:T(8,128)(2,1)S(1)}, u32[]{:S(2)}, u32[]{:S(2)}) %collective-permute-start.8) | collective-permute-done | bytes 688160 | tf_op jit(solution)/shard_map/ppermute | solution.py:27
  59.4 1.7 %shard_map.90 = (bf16[3,32,1792]{2,1,0:T(8,128)(2,1)S(1)}, bf16[3,32,1792]{2,1,0:T(8,128)(2,1)S(1)}, bf16[3,32,1792]{2,1,0:T(8,128)(2,1)S(1)}, bf16[3,32,1792]{2,1,0:T(8,128)(2,1)S(1)}) custom-call(s32[2]{0:T(128)S(1)} %pad_add_fusion.place, bf16[3,64,1792]{2,1,0:T(8,128)(2,1)S(1)} %get-tuple-element.65.refs_0_, ...), custom_call_target="tpu_custom_call" | custom-call | bytes 4128776 | tf_op jit(solution)/shard_map/pallas_call | solution.py:57
  61.0 3.3 %collective-permute-start.10 = (bf16[3,32,1792]{2,1,0:T(8,128)(2,1)S(1)}, bf16[3,32,1792]{2,1,0:T(8,128)(2,1)S(1)}, u32[]{:S(2)}, u32[]{:S(2)}) collective-permute-start(bf16[3,32,1792]{2,1,0:T(8,128)(2,1)S(1)} %get-tuple-element.78), channel_id=1, source_target_pairs={{0,8},{1,9},{2,10},{3,11},{4,12},{5,13},{6,14},{7,15},{8,0},{9,1},... | collective-permute-start | bytes 1032200 | tf_op jit(solution)/shard_map/ppermute | solution.py:27
  64.3 0.7 collective-permute-start.11
  65.0 2.6 %collective-permute-start.12 = (bf16[3,32,1792]{2,1,0:T(8,128)(2,1)S(1)}, bf16[3,32,1792]{2,1,0:T(8,128)(2,1)S(1)}, u32[]{:S(2)}, u32[]{:S(2)}) collective-permute-start(bf16[3,32,1792]{2,1,0:T(8,128)(2,1)S(1)} %get-tuple-element.80), channel_id=1, source_target_pairs={{0,12},{1,13},{2,14},{3,15},{4,0},{5,1},{6,2},{7,3},{8,4},{9,5},{1... | collective-permute-start | bytes 1032200 | tf_op jit(solution)/shard_map/ppermute | solution.py:27
  67.6 2.4 %collective-permute-done.10.one = bf16[3,32,1792]{2,1,0:T(8,128)(2,1)S(1)} collective-permute-done((bf16[3,32,1792]{2,1,0:T(8,128)(2,1)S(1)}, bf16[3,32,1792]{2,1,0:T(8,128)(2,1)S(1)}, u32[]{:S(2)}, u32[]{:S(2)}) %collective-permute-start.10) | collective-permute-done | bytes 344096 | tf_op jit(solution)/shard_map/ppermute | solution.py:27
  70.0 3.6 %collective-permute-done.11.two = bf16[3,32,1792]{2,1,0:T(8,128)(2,1)S(1)} collective-permute-done((bf16[3,32,1792]{2,1,0:T(8,128)(2,1)S(1)}, bf16[3,32,1792]{2,1,0:T(8,128)(2,1)S(1)}, u32[]{:S(2)}, u32[]{:S(2)}) %collective-permute-start.11) | collective-permute-done | bytes 344096 | tf_op jit(solution)/shard_map/ppermute | solution.py:27
  74.2 2.2 %collective-permute-start.13 = (bf16[3,32,1792]{2,1,0:T(8,128)(2,1)S(1)}, bf16[3,32,1792]{2,1,0:T(8,128)(2,1)S(1)}, u32[]{:S(2)}, u32[]{:S(2)}) collective-permute-start(bf16[3,32,1792]{2,1,0:T(8,128)(2,1)S(1)} %shard_map.91.refs_0_), channel_id=1, source_target_pairs={{0,8},{1,9},{2,10},{3,11},{4,12},{5,13},{6,14},{7,15},{8,0},{9,1},... | collective-permute-start | bytes 1032200 | tf_op jit(solution)/shard_map/ppermute | solution.py:27
  76.3 1.5 %collective-permute-start.14 = (bf16[3,32,1792]{2,1,0:T(8,128)(2,1)S(1)}, bf16[3,32,1792]{2,1,0:T(8,128)(2,1)S(1)}, u32[]{:S(2)}, u32[]{:S(2)}) collective-permute-start(bf16[3,32,1792]{2,1,0:T(8,128)(2,1)S(1)} %shard_map.91.refs_0_), channel_id=1, source_target_pairs={{0,4},{1,5},{2,6},{3,7},{4,8},{5,9},{6,10},{7,11},{8,12},{9,13},{1... | collective-permute-start | bytes 1032200 | tf_op jit(solution)/shard_map/ppermute | solution.py:27
  77.8 1.8 %collective-permute-start.15 = (bf16[3,32,1792]{2,1,0:T(8,128)(2,1)S(1)}, bf16[3,32,1792]{2,1,0:T(8,128)(2,1)S(1)}, u32[]{:S(2)}, u32[]{:S(2)}) collective-permute-start(bf16[3,32,1792]{2,1,0:T(8,128)(2,1)S(1)} %shard_map.91.refs_0_), channel_id=1, source_target_pairs={{0,12},{1,13},{2,14},{3,15},{4,0},{5,1},{6,2},{7,3},{8,4},{9,5},{1... | collective-permute-start | bytes 1032200 | tf_op jit(solution)/shard_map/ppermute | solution.py:27
  79.6 3.5 %collective-permute-done.13.refs_1_ = bf16[3,32,1792]{2,1,0:T(8,128)(2,1)S(1)} collective-permute-done((bf16[3,32,1792]{2,1,0:T(8,128)(2,1)S(1)}, bf16[3,32,1792]{2,1,0:T(8,128)(2,1)S(1)}, u32[]{:S(2)}, u32[]{:S(2)}) %collective-permute-start.13) | collective-permute-done | bytes 344096 | tf_op jit(solution)/shard_map/ppermute | solution.py:27
  83.1 3.6 %collective-permute-done.14.refs_2_ = bf16[3,32,1792]{2,1,0:T(8,128)(2,1)S(1)} collective-permute-done((bf16[3,32,1792]{2,1,0:T(8,128)(2,1)S(1)}, bf16[3,32,1792]{2,1,0:T(8,128)(2,1)S(1)}, u32[]{:S(2)}, u32[]{:S(2)}) %collective-permute-start.14) | collective-permute-done | bytes 344096 | tf_op jit(solution)/shard_map/ppermute | solution.py:27
  86.8 1.3 collective-permute-start.16
  88.1 0.8 collective-permute-start.19
  88.9 1.2 collective-permute-start.17
  90.1 0.8 collective-permute-start.18
  90.9 4.4 %collective-permute-done.16.refs_2_ = bf16[2,64,1792]{2,1,0:T(8,128)(2,1)S(1)} collective-permute-done((bf16[2,64,1792]{2,1,0:T(8,128)(2,1)S(1)}, bf16[2,64,1792]{2,1,0:T(8,128)(2,1)S(1)}, u32[]{:S(2)}, u32[]{:S(2)}) %collective-permute-start.16) | collective-permute-done | bytes 458784 | tf_op jit(solution)/shard_map/ppermute | solution.py:27
  95.4 1.2 collective-permute-start.20
  96.6 0.8 collective-permute-start.21
  97.4 2.9 %collective-permute-done.17.refs_3_ = bf16[2,64,1792]{2,1,0:T(8,128)(2,1)S(1)} collective-permute-done((bf16[2,64,1792]{2,1,0:T(8,128)(2,1)S(1)}, bf16[2,64,1792]{2,1,0:T(8,128)(2,1)S(1)}, u32[]{:S(2)}, u32[]{:S(2)}) %collective-permute-start.17) | collective-permute-done | bytes 458784 | tf_op jit(solution)/shard_map/ppermute | solution.py:27
  100.3 1.2 collective-permute-done.18.refs_4_
  101.5 2.6 %collective-permute-start.23 = (bf16[128,1792]{1,0:T(8,128)(2,1)S(1)}, bf16[128,1792]{1,0:T(8,128)(2,1)S(1)}, u32[]{:S(2)}, u32[]{:S(2)}) collective-permute-start(bf16[128,1792]{1,0:T(8,128)(2,1)S(1)} %get-tuple-element.110.refs_0_), channel_id=1, source_target_pairs={{0,2},{1,3},{2,0},{3,1},{4,6},{5,7},{6,4},{7,5},{8,10},{9,11},{10,... | collective-permute-start | bytes 1376264 | tf_op jit(solution)/shard_map/ppermute | solution.py:27
  104.1 2.0 %collective-permute-start.25 = (bf16[128,1792]{1,0:T(8,128)(2,1)S(1)}, bf16[128,1792]{1,0:T(8,128)(2,1)S(1)}, u32[]{:S(2)}, u32[]{:S(2)}) collective-permute-start(bf16[128,1792]{1,0:T(8,128)(2,1)S(1)} %get-tuple-element.110.refs_0_), channel_id=1, source_target_pairs={{0,3},{1,0},{2,1},{3,2},{4,7},{5,4},{6,5},{7,6},{8,11},{9,8},{10,9... | collective-permute-start | bytes 1376264 | tf_op jit(solution)/shard_map/ppermute | solution.py:27
  106.4 1.8 %shard_map.93 = (bf16[256,512]{1,0:T(8,128)(2,1)S(1)}, bf16[512,1792]{1,0:T(8,128)(2,1)S(1)}, bf16[512,1792]{1,0:T(8,128)(2,1)S(1)}) custom-call(s32[2]{0:T(128)S(1)} %pad_add_fusion.place, bf16[512,1792]{1,0:T(8,128)(2,1)S(1)} %copy-done.1, bf16[512,1792]{1,0:T(8,128)(2,1)S(1)} %copy-done.3, bf16[2,64,1792]{2,1,0:T(8,128)(2,1)S(1)} %get-tuple-element.81.refs_0_, ...), custom_call_target="tpu_custom_call" | custom-call | flops 939524096 | bytes 7340040 | tf_op jit(solution)/shard_map/pallas_call | solution.py:57
  108.2 3.4 %collective-permute-start.22 = (bf16[256,512]{1,0:T(8,128)(2,1)S(1)}, bf16[256,512]{1,0:T(8,128)(2,1)S(1)}, u32[]{:S(2)}, u32[]{:S(2)}) collective-permute-start(bf16[256,512]{1,0:T(8,128)(2,1)S(1)} %get-tuple-element.86), channel_id=1, source_target_pairs={{0,16},{16,0},{32,48},{48,32},{64,80},{80,64},{96,112},{112,96},{1... | collective-permute-start | bytes 786440 | tf_op jit(solution)/shard_map/ppermute | solution.py:45
  111.6 1.1 shard_map.94.keep
  112.8 2.1 %shard_map.95 = (bf16[512,1792]{1,0:T(8,128)(2,1)S(1)}, bf16[512,1792]{1,0:T(8,128)(2,1)S(1)}) custom-call(bf16[256,1024]{1,0:T(8,128)(2,1)S(1)} %shard_map.85.act.low, bf16[256,1024]{1,0:T(8,128)(2,1)S(1)} %collective-permute-done.3.act.high, bf16[512,1792]{1,0:T(8,128)(2,1)S(1)} %get-tuple-element.87.gg, bf16[512,1792]{1,0:T(8,128)(2,1)S(1)} %get-tuple-element.88.ug), custom_call_target="tpu_custom_call" | custom-call | flops 1879048192 | bytes 4718592 | tf_op jit(solution)/shard_map/pallas_call | solution.py:57
  114.9 1.1 collective-permute-done.22.got
  116.1 0.6 collective-permute-done.24.refs_2_
  116.7 0.7 collective-permute-done.25.refs_3_
  117.4 0.5 collective-permute-start.29
  117.9 1.8 %shard_map.100.mine = bf16[1792,512]{1,0:T(8,128)(2,1)S(1)} custom-call(s32[2]{0:T(128)S(1)} %pad_add_fusion.place, bf16[256,1024]{1,0:T(8,128)(2,1)S(1)} %shard_map.85.act.low, bf16[256,1024]{1,0:T(8,128)(2,1)S(1)} %collective-permute-done.3.act.high, bf16[128,1792]{1,0:T(8,128)(2,1)S(1)} %get-tuple-element.110.refs_0_, ...), custom_call_target="tpu_custom_call" | custom-call | flops 939524096 | bytes 2883592 | tf_op jit(solution)/shard_map/pallas_call | solution.py:57
  119.8 3.5 %collective-permute-start.26 = (bf16[64,512]{1,0:T(8,128)(2,1)S(1)}, bf16[64,512]{1,0:T(8,128)(2,1)S(1)}, u32[]{:S(2)}, u32[]{:S(2)}) collective-permute-start(bf16[64,512]{1,0:T(8,128)(2,1)S(1)} %get-tuple-element.99), channel_id=1, source_target_pairs={{0,64},{16,80},{32,96},{48,112},{64,0},{80,16},{96,32},{112,48},{1... | collective-permute-start | bytes 196616 | tf_op jit(solution)/shard_map/ppermute | solution.py:36
  123.3 2.8 %collective-permute-start.27 = (bf16[64,512]{1,0:T(8,128)(2,1)S(1)}, bf16[64,512]{1,0:T(8,128)(2,1)S(1)}, u32[]{:S(2)}, u32[]{:S(2)}) collective-permute-start(bf16[64,512]{1,0:T(8,128)(2,1)S(1)} %get-tuple-element.100), channel_id=1, source_target_pairs={{0,32},{16,48},{32,64},{48,80},{64,96},{80,112},{96,0},{112,16},{1... | collective-permute-start | bytes 196616 | tf_op jit(solution)/shard_map/ppermute | solution.py:36
  126.1 1.3 collective-permute-start.28
  127.4 1.3 shard_map.98
  128.8 1.3 shard_map.97
  130.2 0.9 collective-permute-done.27.refs_2_
  131.1 2.1 %collective-permute-done.28.refs_3_ = bf16[64,512]{1,0:T(8,128)(2,1)S(1)} collective-permute-done((bf16[64,512]{1,0:T(8,128)(2,1)S(1)}, bf16[64,512]{1,0:T(8,128)(2,1)S(1)}, u32[]{:S(2)}, u32[]{:S(2)}) %collective-permute-start.28) | collective-permute-done | bytes 65568 | tf_op jit(solution)/shard_map/ppermute | solution.py:36
  133.2 0.7 shard_map.99
  133.8 1.3 shard_map.101
  (35 shorter events, 2.0 us)
Async XLA Ops:
  0.6 0.8 copy-start.6
  1.5 0.8 copy-start.7
  2.3 16.2 %collective-permute-start = (bf16[64,1024]{1,0:T(8,128)(2,1)S(1)}, bf16[64,1024]{1,0:T(8,128)(2,1)S(1)}, u32[]{:S(2)}, u32[]{:S(2)}) collective-permute-start(bf16[64,1024]{1,0:T(8,128)(2,1)S(1)} %shard_map.84.refs_0_), channel_id=1, source_target_pairs={{0,96},{16,112},{32,0},{48,16},{64,32},{80,48},{96,64},{112,80},{1... | collective-permute-start | bytes 393224 | tf_op jit(solution)/shard_map/ppermute | solution.py:36
  8.7 11.1 %collective-permute-start.1 = (bf16[64,1024]{1,0:T(8,128)(2,1)S(1)}, bf16[64,1024]{1,0:T(8,128)(2,1)S(1)}, u32[]{:S(2)}, u32[]{:S(2)}) collective-permute-start(bf16[64,1024]{1,0:T(8,128)(2,1)S(1)} %shard_map.84.refs_0_), channel_id=1, source_target_pairs={{0,64},{16,80},{32,96},{48,112},{64,0},{80,16},{96,32},{112,48},{1... | collective-permute-start | bytes 393224 | tf_op jit(solution)/shard_map/ppermute | solution.py:36
  9.7 10.1 %collective-permute-start.2 = (bf16[64,1024]{1,0:T(8,128)(2,1)S(1)}, bf16[64,1024]{1,0:T(8,128)(2,1)S(1)}, u32[]{:S(2)}, u32[]{:S(2)}) collective-permute-start(bf16[64,1024]{1,0:T(8,128)(2,1)S(1)} %shard_map.84.refs_0_), channel_id=1, source_target_pairs={{0,32},{16,48},{32,64},{48,80},{64,96},{80,112},{96,0},{112,16},{1... | collective-permute-start | bytes 393224 | tf_op jit(solution)/shard_map/ppermute | solution.py:36
  19.8 10.5 %collective-permute-start.3 = (bf16[256,1024]{1,0:T(8,128)(2,1)S(1)}, bf16[256,1024]{1,0:T(8,128)(2,1)S(1)}, u32[]{:S(2)}, u32[]{:S(2)}) collective-permute-start(bf16[256,1024]{1,0:T(8,128)(2,1)S(1)} %shard_map.85.act.low), channel_id=1, source_target_pairs={{0,16},{16,0},{32,48},{48,32},{64,80},{80,64},{96,112},{112,96},{1... | collective-permute-start | bytes 1572872 | tf_op jit(solution)/shard_map/ppermute | solution.py:45
  23.2 1.5 %copy-start = (bf16[512,1792]{1,0:T(8,128)(2,1)S(1)}, bf16[512,1792]{1,0:T(8,128)(2,1)}, u32[]{:S(2)}) copy-start(bf16[512,1792]{1,0:T(8,128)(2,1)} %gate.9) | copy-start | bytes 5505028
  24.7 1.5 %copy-start.2 = (bf16[512,1792]{1,0:T(8,128)(2,1)S(1)}, bf16[512,1792]{1,0:T(8,128)(2,1)}, u32[]{:S(2)}) copy-start(bf16[512,1792]{1,0:T(8,128)(2,1)} %up.9) | copy-start | bytes 5505028
  26.2 1.5 %copy-start.4 = (bf16[1792,512]{1,0:T(8,128)(2,1)S(1)}, bf16[1792,512]{1,0:T(8,128)(2,1)}, u32[]{:S(2)}) copy-start(bf16[1792,512]{1,0:T(8,128)(2,1)} %down.5) | copy-start | bytes 5505028
  27.7 2.6 %copy-start.1 = (bf16[512,1792]{1,0:T(8,128)(2,1)S(1)}, bf16[512,1792]{1,0:T(8,128)(2,1)}, u32[]{:S(2)}) copy-start(bf16[512,1792]{1,0:T(8,128)(2,1)} %gate.9) | copy-start | bytes 5505028
  27.7 2.6 %copy-start.3 = (bf16[512,1792]{1,0:T(8,128)(2,1)S(1)}, bf16[512,1792]{1,0:T(8,128)(2,1)}, u32[]{:S(2)}) copy-start(bf16[512,1792]{1,0:T(8,128)(2,1)} %up.9) | copy-start | bytes 5505028
  27.7 2.6 %copy-start.5 = (bf16[1792,512]{1,0:T(8,128)(2,1)S(1)}, bf16[1792,512]{1,0:T(8,128)(2,1)}, u32[]{:S(2)}) copy-start(bf16[1792,512]{1,0:T(8,128)(2,1)} %down.5) | copy-start | bytes 5505028
  32.1 11.0 %collective-permute-start.4 = (bf16[3,64,1792]{2,1,0:T(8,128)(2,1)S(1)}, bf16[3,64,1792]{2,1,0:T(8,128)(2,1)S(1)}, u32[]{:S(2)}, u32[]{:S(2)}) collective-permute-start(bf16[3,64,1792]{2,1,0:T(8,128)(2,1)S(1)} %get-tuple-element.70), channel_id=1, source_target_pairs={{0,1},{1,2},{2,3},{3,0},{4,5},{5,6},{6,7},{7,4},{8,9},{9,10},{10,1... | collective-permute-start | bytes 2064392 | tf_op jit(solution)/shard_map/ppermute | solution.py:27
  33.7 10.9 %collective-permute-start.5 = (bf16[3,64,1792]{2,1,0:T(8,128)(2,1)S(1)}, bf16[3,64,1792]{2,1,0:T(8,128)(2,1)S(1)}, u32[]{:S(2)}, u32[]{:S(2)}) collective-permute-start(bf16[3,64,1792]{2,1,0:T(8,128)(2,1)S(1)} %get-tuple-element.71), channel_id=1, source_target_pairs={{0,3},{1,0},{2,1},{3,2},{4,7},{5,4},{6,5},{7,6},{8,11},{9,8},{10,9... | collective-permute-start | bytes 2064392 | tf_op jit(solution)/shard_map/ppermute | solution.py:27
  36.3 15.7 %collective-permute-start.7 = (bf16[3,64,1792]{2,1,0:T(8,128)(2,1)S(1)}, bf16[3,64,1792]{2,1,0:T(8,128)(2,1)S(1)}, u32[]{:S(2)}, u32[]{:S(2)}) collective-permute-start(bf16[3,64,1792]{2,1,0:T(8,128)(2,1)S(1)} %get-tuple-element.73), channel_id=1, source_target_pairs={{0,3},{1,0},{2,1},{3,2},{4,7},{5,4},{6,5},{7,6},{8,11},{9,8},{10,9... | collective-permute-start | bytes 2064392 | tf_op jit(solution)/shard_map/ppermute | solution.py:27
  38.5 13.5 %collective-permute-start.9 = (bf16[3,64,1792]{2,1,0:T(8,128)(2,1)S(1)}, bf16[3,64,1792]{2,1,0:T(8,128)(2,1)S(1)}, u32[]{:S(2)}, u32[]{:S(2)}) collective-permute-start(bf16[3,64,1792]{2,1,0:T(8,128)(2,1)S(1)} %get-tuple-element.76), channel_id=1, source_target_pairs={{0,1},{1,2},{2,3},{3,0},{4,5},{5,6},{6,7},{7,4},{8,9},{9,10},{10,1... | collective-permute-start | bytes 2064392 | tf_op jit(solution)/shard_map/ppermute | solution.py:27
  44.9 12.9 %collective-permute-start.6 = (bf16[3,64,1792]{2,1,0:T(8,128)(2,1)S(1)}, bf16[3,64,1792]{2,1,0:T(8,128)(2,1)S(1)}, u32[]{:S(2)}, u32[]{:S(2)}) collective-permute-start(bf16[3,64,1792]{2,1,0:T(8,128)(2,1)S(1)} %get-tuple-element.72), channel_id=1, source_target_pairs={{0,1},{1,2},{2,3},{3,0},{4,5},{5,6},{6,7},{7,4},{8,9},{9,10},{10,1... | collective-permute-start | bytes 2064392 | tf_op jit(solution)/shard_map/ppermute | solution.py:27
  46.2 13.2 %collective-permute-start.8 = (bf16[3,64,1792]{2,1,0:T(8,128)(2,1)S(1)}, bf16[3,64,1792]{2,1,0:T(8,128)(2,1)S(1)}, u32[]{:S(2)}, u32[]{:S(2)}) collective-permute-start(bf16[3,64,1792]{2,1,0:T(8,128)(2,1)S(1)} %get-tuple-element.75), channel_id=1, source_target_pairs={{0,3},{1,0},{2,1},{3,2},{4,7},{5,4},{6,5},{7,6},{8,11},{9,8},{10,9... | collective-permute-start | bytes 2064392 | tf_op jit(solution)/shard_map/ppermute | solution.py:27
  61.0 8.9 %collective-permute-start.10 = (bf16[3,32,1792]{2,1,0:T(8,128)(2,1)S(1)}, bf16[3,32,1792]{2,1,0:T(8,128)(2,1)S(1)}, u32[]{:S(2)}, u32[]{:S(2)}) collective-permute-start(bf16[3,32,1792]{2,1,0:T(8,128)(2,1)S(1)} %get-tuple-element.78), channel_id=1, source_target_pairs={{0,8},{1,9},{2,10},{3,11},{4,12},{5,13},{6,14},{7,15},{8,0},{9,1},... | collective-permute-start | bytes 1032200 | tf_op jit(solution)/shard_map/ppermute | solution.py:27
  64.3 9.2 %collective-permute-start.11 = (bf16[3,32,1792]{2,1,0:T(8,128)(2,1)S(1)}, bf16[3,32,1792]{2,1,0:T(8,128)(2,1)S(1)}, u32[]{:S(2)}, u32[]{:S(2)}) collective-permute-start(bf16[3,32,1792]{2,1,0:T(8,128)(2,1)S(1)} %get-tuple-element.79), channel_id=1, source_target_pairs={{0,4},{1,5},{2,6},{3,7},{4,8},{5,9},{6,10},{7,11},{8,12},{9,13},{1... | collective-permute-start | bytes 1032200 | tf_op jit(solution)/shard_map/ppermute | solution.py:27
  65.0 8.9 %collective-permute-start.12 = (bf16[3,32,1792]{2,1,0:T(8,128)(2,1)S(1)}, bf16[3,32,1792]{2,1,0:T(8,128)(2,1)S(1)}, u32[]{:S(2)}, u32[]{:S(2)}) collective-permute-start(bf16[3,32,1792]{2,1,0:T(8,128)(2,1)S(1)} %get-tuple-element.80), channel_id=1, source_target_pairs={{0,12},{1,13},{2,14},{3,15},{4,0},{5,1},{6,2},{7,3},{8,4},{9,5},{1... | collective-permute-start | bytes 1032200 | tf_op jit(solution)/shard_map/ppermute | solution.py:27
  74.2 8.9 %collective-permute-start.13 = (bf16[3,32,1792]{2,1,0:T(8,128)(2,1)S(1)}, bf16[3,32,1792]{2,1,0:T(8,128)(2,1)S(1)}, u32[]{:S(2)}, u32[]{:S(2)}) collective-permute-start(bf16[3,32,1792]{2,1,0:T(8,128)(2,1)S(1)} %shard_map.91.refs_0_), channel_id=1, source_target_pairs={{0,8},{1,9},{2,10},{3,11},{4,12},{5,13},{6,14},{7,15},{8,0},{9,1},... | collective-permute-start | bytes 1032200 | tf_op jit(solution)/shard_map/ppermute | solution.py:27
  76.3 10.4 %collective-permute-start.14 = (bf16[3,32,1792]{2,1,0:T(8,128)(2,1)S(1)}, bf16[3,32,1792]{2,1,0:T(8,128)(2,1)S(1)}, u32[]{:S(2)}, u32[]{:S(2)}) collective-permute-start(bf16[3,32,1792]{2,1,0:T(8,128)(2,1)S(1)} %shard_map.91.refs_0_), channel_id=1, source_target_pairs={{0,4},{1,5},{2,6},{3,7},{4,8},{5,9},{6,10},{7,11},{8,12},{9,13},{1... | collective-permute-start | bytes 1032200 | tf_op jit(solution)/shard_map/ppermute | solution.py:27
  77.8 8.9 %collective-permute-start.15 = (bf16[3,32,1792]{2,1,0:T(8,128)(2,1)S(1)}, bf16[3,32,1792]{2,1,0:T(8,128)(2,1)S(1)}, u32[]{:S(2)}, u32[]{:S(2)}) collective-permute-start(bf16[3,32,1792]{2,1,0:T(8,128)(2,1)S(1)} %shard_map.91.refs_0_), channel_id=1, source_target_pairs={{0,12},{1,13},{2,14},{3,15},{4,0},{5,1},{6,2},{7,3},{8,4},{9,5},{1... | collective-permute-start | bytes 1032200 | tf_op jit(solution)/shard_map/ppermute | solution.py:27
  86.8 8.6 %collective-permute-start.16 = (bf16[2,64,1792]{2,1,0:T(8,128)(2,1)S(1)}, bf16[2,64,1792]{2,1,0:T(8,128)(2,1)S(1)}, u32[]{:S(2)}, u32[]{:S(2)}) collective-permute-start(bf16[2,64,1792]{2,1,0:T(8,128)(2,1)S(1)} %get-tuple-element.81.refs_0_), channel_id=1, source_target_pairs={{0,1},{1,2},{2,3},{3,0},{4,5},{5,6},{6,7},{7,4},{8,9},{9,10},{10,1... | collective-permute-start | bytes 1376264 | tf_op jit(solution)/shard_map/ppermute | solution.py:27
  88.1 8.5 %collective-permute-start.19 = (bf16[2,64,1792]{2,1,0:T(8,128)(2,1)S(1)}, bf16[2,64,1792]{2,1,0:T(8,128)(2,1)S(1)}, u32[]{:S(2)}, u32[]{:S(2)}) collective-permute-start(bf16[2,64,1792]{2,1,0:T(8,128)(2,1)S(1)} %get-tuple-element.82.refs_1_), channel_id=1, source_target_pairs={{0,3},{1,0},{2,1},{3,2},{4,7},{5,4},{6,5},{7,6},{8,11},{9,8},{10,9... | collective-permute-start | bytes 1376264 | tf_op jit(solution)/shard_map/ppermute | solution.py:27
  88.9 11.4 %collective-permute-start.17 = (bf16[2,64,1792]{2,1,0:T(8,128)(2,1)S(1)}, bf16[2,64,1792]{2,1,0:T(8,128)(2,1)S(1)}, u32[]{:S(2)}, u32[]{:S(2)}) collective-permute-start(bf16[2,64,1792]{2,1,0:T(8,128)(2,1)S(1)} %get-tuple-element.82.refs_1_), channel_id=1, source_target_pairs={{0,1},{1,2},{2,3},{3,0},{4,5},{5,6},{6,7},{7,4},{8,9},{9,10},{10,1... | collective-permute-start | bytes 1376264 | tf_op jit(solution)/shard_map/ppermute | solution.py:27
  90.1 11.4 %collective-permute-start.18 = (bf16[2,64,1792]{2,1,0:T(8,128)(2,1)S(1)}, bf16[2,64,1792]{2,1,0:T(8,128)(2,1)S(1)}, u32[]{:S(2)}, u32[]{:S(2)}) collective-permute-start(bf16[2,64,1792]{2,1,0:T(8,128)(2,1)S(1)} %get-tuple-element.81.refs_0_), channel_id=1, source_target_pairs={{0,3},{1,0},{2,1},{3,2},{4,7},{5,4},{6,5},{7,6},{8,11},{9,8},{10,9... | collective-permute-start | bytes 1376264 | tf_op jit(solution)/shard_map/ppermute | solution.py:27
  95.4 10.8 %collective-permute-start.20 = (bf16[2,64,1792]{2,1,0:T(8,128)(2,1)S(1)}, bf16[2,64,1792]{2,1,0:T(8,128)(2,1)S(1)}, u32[]{:S(2)}, u32[]{:S(2)}) collective-permute-start(bf16[2,64,1792]{2,1,0:T(8,128)(2,1)S(1)} %collective-permute-done.16.refs_2_), channel_id=1, source_target_pairs={{0,1},{1,2},{2,3},{3,0},{4,5},{5,6},{6,7},{7,4},{8,9},{9,10},{10,1... | collective-permute-start | bytes 1376264 | tf_op jit(solution)/shard_map/ppermute | solution.py:27
  96.6 9.8 %collective-permute-start.21 = (bf16[2,64,1792]{2,1,0:T(8,128)(2,1)S(1)}, bf16[2,64,1792]{2,1,0:T(8,128)(2,1)S(1)}, u32[]{:S(2)}, u32[]{:S(2)}) collective-permute-start(bf16[2,64,1792]{2,1,0:T(8,128)(2,1)S(1)} %collective-permute-done.19.refs_5_), channel_id=1, source_target_pairs={{0,3},{1,0},{2,1},{3,2},{4,7},{5,4},{6,5},{7,6},{8,11},{9,8},{10,9... | collective-permute-start | bytes 1376264 | tf_op jit(solution)/shard_map/ppermute | solution.py:27
  101.5 14.6 %collective-permute-start.23 = (bf16[128,1792]{1,0:T(8,128)(2,1)S(1)}, bf16[128,1792]{1,0:T(8,128)(2,1)S(1)}, u32[]{:S(2)}, u32[]{:S(2)}) collective-permute-start(bf16[128,1792]{1,0:T(8,128)(2,1)S(1)} %get-tuple-element.110.refs_0_), channel_id=1, source_target_pairs={{0,2},{1,3},{2,0},{3,1},{4,6},{5,7},{6,4},{7,5},{8,10},{9,11},{10,... | collective-permute-start | bytes 1376264 | tf_op jit(solution)/shard_map/ppermute | solution.py:27
  104.1 12.6 %collective-permute-start.24 = (bf16[128,1792]{1,0:T(8,128)(2,1)S(1)}, bf16[128,1792]{1,0:T(8,128)(2,1)S(1)}, u32[]{:S(2)}, u32[]{:S(2)}) collective-permute-start(bf16[128,1792]{1,0:T(8,128)(2,1)S(1)} %get-tuple-element.110.refs_0_), channel_id=1, source_target_pairs={{0,1},{1,2},{2,3},{3,0},{4,5},{5,6},{6,7},{7,4},{8,9},{9,10},{10,1... | collective-permute-start | bytes 1376264 | tf_op jit(solution)/shard_map/ppermute | solution.py:27
  104.1 13.3 %collective-permute-start.25 = (bf16[128,1792]{1,0:T(8,128)(2,1)S(1)}, bf16[128,1792]{1,0:T(8,128)(2,1)S(1)}, u32[]{:S(2)}, u32[]{:S(2)}) collective-permute-start(bf16[128,1792]{1,0:T(8,128)(2,1)S(1)} %get-tuple-element.110.refs_0_), channel_id=1, source_target_pairs={{0,3},{1,0},{2,1},{3,2},{4,7},{5,4},{6,5},{7,6},{8,11},{9,8},{10,9... | collective-permute-start | bytes 1376264 | tf_op jit(solution)/shard_map/ppermute | solution.py:27
  108.2 7.8 %collective-permute-start.22 = (bf16[256,512]{1,0:T(8,128)(2,1)S(1)}, bf16[256,512]{1,0:T(8,128)(2,1)S(1)}, u32[]{:S(2)}, u32[]{:S(2)}) collective-permute-start(bf16[256,512]{1,0:T(8,128)(2,1)S(1)} %get-tuple-element.86), channel_id=1, source_target_pairs={{0,16},{16,0},{32,48},{48,32},{64,80},{80,64},{96,112},{112,96},{1... | collective-permute-start | bytes 786440 | tf_op jit(solution)/shard_map/ppermute | solution.py:45
  117.4 8.8 %collective-permute-start.30 = (bf16[512,1792]{1,0:T(8,128)(2,1)S(1)}, bf16[512,1792]{1,0:T(8,128)(2,1)S(1)}, u32[]{:S(2)}, u32[]{:S(2)}) collective-permute-start(bf16[512,1792]{1,0:T(8,128)(2,1)S(1)} %get-tuple-element.103.mine), channel_id=1, source_target_pairs={{0,128},{128,0},{1,129},{129,1},{2,130},{130,2},{3,131},{131,3},{4... | collective-permute-start | bytes 5505032 | tf_op jit(solution)/shard_map/ppermute | solution.py:49
  117.4 11.4 %collective-permute-start.29 = (bf16[512,1792]{1,0:T(8,128)(2,1)S(1)}, bf16[512,1792]{1,0:T(8,128)(2,1)S(1)}, u32[]{:S(2)}, u32[]{:S(2)}) collective-permute-start(bf16[512,1792]{1,0:T(8,128)(2,1)S(1)} %get-tuple-element.102.mine), channel_id=1, source_target_pairs={{0,128},{128,0},{1,129},{129,1},{2,130},{130,2},{3,131},{131,3},{4... | collective-permute-start | bytes 5505032 | tf_op jit(solution)/shard_map/ppermute | solution.py:49
  119.7 14.1 %collective-permute-start.31 = (bf16[1792,512]{1,0:T(8,128)(2,1)S(1)}, bf16[1792,512]{1,0:T(8,128)(2,1)S(1)}, u32[]{:S(2)}, u32[]{:S(2)}) collective-permute-start(bf16[1792,512]{1,0:T(8,128)(2,1)S(1)} %shard_map.100.mine), channel_id=1, source_target_pairs={{0,128},{128,0},{1,129},{129,1},{2,130},{130,2},{3,131},{131,3},{4... | collective-permute-start | bytes 5505032 | tf_op jit(solution)/shard_map/ppermute | solution.py:49
  119.8 10.4 %collective-permute-start.26 = (bf16[64,512]{1,0:T(8,128)(2,1)S(1)}, bf16[64,512]{1,0:T(8,128)(2,1)S(1)}, u32[]{:S(2)}, u32[]{:S(2)}) collective-permute-start(bf16[64,512]{1,0:T(8,128)(2,1)S(1)} %get-tuple-element.99), channel_id=1, source_target_pairs={{0,64},{16,80},{32,96},{48,112},{64,0},{80,16},{96,32},{112,48},{1... | collective-permute-start | bytes 196616 | tf_op jit(solution)/shard_map/ppermute | solution.py:36
  123.3 7.8 %collective-permute-start.27 = (bf16[64,512]{1,0:T(8,128)(2,1)S(1)}, bf16[64,512]{1,0:T(8,128)(2,1)S(1)}, u32[]{:S(2)}, u32[]{:S(2)}) collective-permute-start(bf16[64,512]{1,0:T(8,128)(2,1)S(1)} %get-tuple-element.100), channel_id=1, source_target_pairs={{0,32},{16,48},{32,64},{48,80},{64,96},{80,112},{96,0},{112,16},{1... | collective-permute-start | bytes 196616 | tf_op jit(solution)/shard_map/ppermute | solution.py:36
  126.1 7.0 %collective-permute-start.28 = (bf16[64,512]{1,0:T(8,128)(2,1)S(1)}, bf16[64,512]{1,0:T(8,128)(2,1)S(1)}, u32[]{:S(2)}, u32[]{:S(2)}) collective-permute-start(bf16[64,512]{1,0:T(8,128)(2,1)S(1)} %get-tuple-element.101), channel_id=1, source_target_pairs={{0,96},{16,112},{32,0},{48,16},{64,32},{80,48},{96,64},{112,80},{1... | collective-permute-start | bytes 196616 | tf_op jit(solution)/shard_map/ppermute | solution.py:36
